TPU v7x, 32 devices: a whole 2x2x4 slice. The times are simulated.
32 devices in a mesh: grp: 16 (over z, x, core), tp: 2 (over y).
Axes of the slice: x: 2, y: 2, z: 4, core: 2. Of those that a mesh axis runs over, the one named last changes fastest.
Arguments:
- prefill_states: bfloat16 [16384, 8192], P('grp', 'tp'), may hold values from -6 to 6
- key_weight: bfloat16 [8192, 1024], P('tp'), may hold values from -0.0625 to 0.0625
- value_weight: bfloat16 [8192, 1024], P('tp'), may hold values from -0.0625 to 0.0625
- offsets: int32 [16], P('grp'), may hold values from 0 to 7168, as said below
- matching: int32 [16], P('grp'), may hold values from 0 to 1, as said below
- queries: bfloat16 [512, 64, 128], P('grp', 'tp'), may hold values from -60 to 60
- cache_keys: bfloat16 [512, 8, 256, 128], P('grp', 'tp'), may hold values from -6 to 6
- cache_values: bfloat16 [512, 8, 256, 128], P('grp', 'tp'), may hold values from -6 to 6
- cache_lengths: int32 [512], P('grp'), may hold values from 1 to 256, as said below
Outputs:
- context: bfloat16 [512, 64, 128], P('grp', 'tp')
Inputs may be any that keep to these rules, and one draw needn't show every extreme that they name: For each prompt p, the offsets of groups p * 8 to (p + 1) * 8 - 1 are 0, 1024, 2048, ... in some order, each once. `matching`: every prompt is continued by exactly 8 decode groups. `cache_lengths`: the first row of every group has 256 live entries.
All inputs are finite; a program needn't handle non-finite values.
Results may differ from a plain program's by a relative error of at most 0.012.
The roundings to bfloat16 on the way count: a program that leaves them out, or rounds other values in their place, can miss the bound.
Values may be sent and summed in bfloat16 or wider, within the bound.
No kernel may reach another device: no remote copies, remote signals or barrier semaphores. Data moves between devices by JAX's collectives and lax.ppermute only.
A program may use at most 320 MiB of HBM per device.

v0:
```python
import jax
import jax.numpy as jnp
from jax import lax
from jax.sharding import PartitionSpec as P

HD = 128
PROMPTS = 2


def rotate(raw_heads, positions):
    half_width = HD // 2
    inverse_freq = 500000.0 ** (-(jnp.arange(half_width, dtype=jnp.float32) * 2.0 / HD))
    angles = positions.astype(jnp.float32)[:, None] * inverse_freq[None, :]
    cosine = jnp.cos(angles)[None, :, :]
    sine_part = jnp.sin(angles)[None, :, :]
    first_half = raw_heads[..., :half_width]
    second_half = raw_heads[..., half_width:]
    return jnp.concatenate(
        [
            first_half * cosine - second_half * sine_part,
            second_half * cosine + first_half * sine_part,
        ],
        -1,
    )


def on_device(
    prefill_states,
    key_weight,
    value_weight,
    offsets,
    matching,
    queries,
    cache_keys,
    cache_values,
    cache_lengths,
):
    block_len = prefill_states.shape[0]
    kv_total = key_weight.shape[1] // HD
    kv_local = kv_total // lax.axis_size("tp")
    key_part = jnp.dot(prefill_states, key_weight, preferred_element_type=jnp.float32)
    value_part = jnp.dot(prefill_states, value_weight, preferred_element_type=jnp.float32)
    stacked = jnp.concatenate(
        [
            key_part.reshape(block_len, lax.axis_size("tp") * kv_local, HD),
            value_part.reshape(block_len, lax.axis_size("tp") * kv_local, HD),
        ],
        2,
    )
    shares = lax.psum_scatter(stacked.transpose(1, 0, 2), "tp", scatter_dimension=0, tiled=True)
    own_keys = shares[..., :HD]
    own_values = shares[..., HD:]
    positions = offsets[0] + jnp.arange(block_len, dtype=jnp.int32)
    page_keys = rotate(own_keys, positions).astype(jnp.bfloat16)
    page_values = own_values.astype(jnp.bfloat16)
    row_count = queries.shape[0]
    group_size = queries.shape[1] // kv_local
    grouped = queries.reshape(row_count, kv_local, group_size, HD)
    score_scale = HD ** (-0.5)
    per_prompt = lax.axis_size("grp") // PROMPTS
    wanted = matching[0]
    top_score = jnp.full((row_count, kv_local, group_size), -1e30, jnp.float32)
    piece_keys = lax.all_gather(page_keys, "grp", axis=1, tiled=True)
    piece_values = lax.all_gather(page_values, "grp", axis=1, tiled=True)
    piece_len = piece_keys.shape[1]
    source_prompt = jnp.arange(piece_len, dtype=jnp.int32) // (block_len * per_prompt)
    valid = source_prompt == wanted
    scores = (
        jnp.einsum("rkgd,knd->rkgn", grouped, piece_keys, preferred_element_type=jnp.float32)
        * score_scale
    )
    scores = jnp.where(valid, scores, -1e30)
    new_top = jnp.maximum(top_score, scores.max(-1))
    weights = jnp.where(valid, jnp.exp(scores - new_top[..., None]), 0.0)
    denominator = weights.sum(-1)
    summed = jnp.einsum(
        "rkgn,knd->rkgd",
        weights.astype(jnp.bfloat16),
        piece_values,
        preferred_element_type=jnp.float32,
    )
    top_score, denominator, summed = (new_top, denominator, summed)
    cache_len = cache_keys.shape[2]
    cache_scores = (
        jnp.einsum("rkgd,rktd->rkgt", grouped, cache_keys, preferred_element_type=jnp.float32)
        * score_scale
    )
    alive_mask = (jnp.arange(cache_len, dtype=jnp.int32)[None, :] < cache_lengths[:, None])[
        :, None, None, :
    ]
    cache_scores = jnp.where(alive_mask, cache_scores, -1e30)
    final_top = jnp.maximum(top_score, cache_scores.max(-1))
    cache_weights = jnp.where(alive_mask, jnp.exp(cache_scores - final_top[..., None]), 0.0)
    factor = jnp.exp(top_score - final_top)
    denominator = denominator * factor + cache_weights.sum(-1)
    summed = summed * factor[..., None] + jnp.einsum(
        "rkgt,rktd->rkgd",
        cache_weights.astype(jnp.bfloat16),
        cache_values,
        preferred_element_type=jnp.float32,
    )
    return (
        (summed / denominator[..., None])
        .reshape(row_count, kv_local * group_size, HD)
        .astype(jnp.bfloat16)
    )


def solution(mesh):
    placed = (
        P("grp", "tp"),
        P("tp", None),
        P("tp", None),
        P("grp"),
        P("grp"),
        P("grp", "tp", None),
        P("grp", "tp", None, None),
        P("grp", "tp", None, None),
        P("grp"),
    )
    return jax.shard_map(
        on_device, mesh=mesh, in_specs=placed, out_specs=P("grp", "tp", None), check_vma=False
    )
```

profile of v0, /device:TPU:0, one launch (start us, length us, event | category | flops | bytes accessed | tf_op | source)
XLA Modules:
  0.0 451.8 jit_solution(15465037222339224160)
XLA Ops:
  6.5 0.0 copy-start
  6.5 0.0 reduce-scatter.2.cloned.1.call-start
  6.5 15.1 %fusion.56 = f32[1024,1024]{0,1:T(8,128)} fusion(bf16[1024,4096]{1,0:T(8,128)(2,1)} %param.9, bf16[4096,1024]{1,0:T(8,128)(2,1)} %param.10), kind=kOutput, calls=%fused_computation.56 | convolution fusion | flops 8589934592 | bytes 20971520 | tf_op jit(solution)/shard_map/dot_general | solution.py:41
  21.6 5.3 %copy.24 = f32[1024,8,128]{2,0,1:T(8,128)} copy(f32[1024,8,128]{0,2,1:T(8,128)} %bitcast.75) | data formatting | bytes 8388608 | tf_op jit(solution)/shard_map/reshape | solution.py:45
  26.9 15.0 %fusion.57 = f32[1024,1024]{0,1:T(8,128)} fusion(bf16[1024,4096]{1,0:T(8,128)(2,1)} %param.9, bf16[4096,1024]{1,0:T(8,128)(2,1)} %param.11), kind=kOutput, calls=%fused_computation.57 | convolution fusion | flops 8589934592 | bytes 20971520 | tf_op jit(solution)/shard_map/dot_general | solution.py:42
  42.0 5.3 %copy.25 = f32[1024,8,128]{2,0,1:T(8,128)} copy(f32[1024,8,128]{0,2,1:T(8,128)} %bitcast.76) | data formatting | bytes 8388608 | tf_op jit(solution)/shard_map/reshape | solution.py:46
  47.3 7.3 %maximum_bitcast_fusion = f32[8,1024,256]{2,1,0:T(8,128)} fusion(f32[1024,8,128]{2,0,1:T(8,128)} %copy.25, f32[1024,8,128]{2,0,1:T(8,128)} %copy.24), kind=kLoop, calls=%fused_computation.13 | loop fusion | flops 2097152 | bytes 16777216 | tf_op jit(solution)/shard_map/transpose | solution.py:50
  54.5 0.0 reduce-scatter.2.cloned.1.call-update
  54.6 0.0 copy-start.2
  54.6 0.2 all-gather.5.cloned.1.call-start
  55.5 1.9 multiply_cosine_fusion
  57.4 99.3 %reduce-scatter.2.cloned.1.call-done = f32[4,1024,256]{2,1,0:T(8,128)} async-done(((f32[8,1024,256]{2,1,0:T(8,128)}), f32[4,1024,256]{2,1,0:T(8,128)}) %reduce-scatter.2.cloned.1.call-update) | async-done | bytes 4194320 | tf_op jit(solution)/shard_map/reduce_scatter | solution.py:50
  156.7 3.0 subtract_convert_fusion
  159.7 1.5 pad_maximum_fusion
  161.2 0.0 all-gather.5.cloned.1.call-update
  161.2 0.0 all-gather.3.cloned.1.call-start
  161.3 2.7 slice.24
  164.0 0.0 all-gather.3.cloned.1.call-update
  164.6 0.0 copy-done.2
  164.7 0.1 iota_compare_fusion
  164.7 5.8 %fusion.55 = (f32[32,4,8]{2,1,0:T(4,128)S(1)}, f32[32,4,8,256]{3,2,1,0:T(8,128)S(1)}) fusion(bf16[32,4,256,128]{3,2,1,0:T(8,128)(2,1)} %param.15, bf16[32,32,128]{2,1,0:T(8,128)(2,1)S(1)} %copy-done, pred[32,256]{1,0:T(8,128)(4,1)S(1)} %iota_compare_fusion), kind=kOutput, calls=%fused_computation.55 | convolution fusion | flops 67894272 | bytes 9711616 | tf_op jit(solution)/shard_map/rkgd,rktd->rkgt/dot_general | solution.py:85
  170.5 0.1 copy.27
  170.6 117.7 %all-gather.5.cloned.1.call-done = bf16[4,16384,128]{2,1,0:T(8,128)(2,1)} async-done(((bf16[4,1024,128]{2,1,0:T(8,128)(2,1)}), bf16[4,16384,128]{2,1,0:T(8,128)(2,1)}) %all-gather.5.cloned.1.call-update) | async-done | bytes 16777232 | tf_op jit(solution)/shard_map/all_gather | solution.py:63
  288.3 29.9 %bitcast_reduce_fusion = (f32[32,4,8]{0,2,1:T(8,128)S(1)}, f32[4,16384,32,8]{1,2,3,0:T(8,128)}) fusion(pred[16384]{0:T(1024)(128)(4,1)S(1)} %fusion.45, bf16[32,4,8,128]{3,2,1,0:T(8,128)(2,1)S(1)} %bitcast.74, bf16[4,16384,128]{2,1,0:T(8,128)(2,1)} %all-gather.5.cloned.1.call-done), kind=kOutput, calls=%fused_computation.1 | convolution fusion | flops 4345297920 | bytes 84168704 | tf_op jit(solution)/shard_map/rkgd,knd->rkgn/dot_general | solution.py:69
  318.2 0.1 copy.28
  318.2 0.5 fusion.37
  318.7 0.1 copy.30
  318.8 22.7 %fusion.2 = f32[32,4,8]{0,2,1:T(8,128)S(1)} fusion(f32[4,16384,32,8]{1,2,3,0:T(8,128)} %get-tuple-element.16, f32[32,4,8]{0,2,1:T(8,128)S(1)} %get-tuple-element.10, pred[16384]{0:T(1024)(128)(4,1)S(1)} %fusion.45), kind=kLoop, calls=%fused_computation.5 | loop fusion | flops 83885056 | bytes 67133440 | tf_op jit(solution)/shard_map/reduce_sum | solution.py:75
  341.5 4.8 %fusion.39 = f32[32,4,8,128]{3,2,1,0:T(8,128)S(1)} fusion(bf16[32,4,256,128]{3,2,1,0:T(8,128)(2,1)} %param.16, f32[32,4,8,256]{3,2,1,0:T(8,128)S(1)} %get-tuple-element.14, f32[32,4,8]{2,1,0:T(4,128)S(1)} %copy.28, pred[32,256]{1,0:T(8,128)(4,1)S(1)} %iota_compare_fusion), kind=kOutput, calls=%fused_computation.30 | convolution fusion | flops 67895296 | bytes 9973760 | tf_op jit(solution)/shard_map/rkgt,rktd->rkgd/dot_general | solution.py:96
  346.3 69.6 %all-gather.3.cloned.1.call-done = bf16[4,16384,128]{2,1,0:T(8,128)(2,1)} async-done(((bf16[4,1024,128]{2,1,0:T(8,128)(2,1)}), bf16[4,16384,128]{2,1,0:T(8,128)(2,1)}) %all-gather.3.cloned.1.call-update) | async-done | bytes 16777232 | tf_op jit(solution)/shard_map/all_gather | solution.py:64
  415.9 28.6 %fusion.32 = bf16[32,4,8,128]{3,0,2,1:T(8,128)(2,1)S(1)} fusion(f32[4,16384,32,8]{1,2,3,0:T(8,128)} %get-tuple-element.16, f32[32,4,8]{0,2,1:T(8,128)S(1)} %get-tuple-element.10, pred[16384]{0:T(1024)(128)(4,1)S(1)} %fusion.45, bf16[4,16384,128]{2,1,0:T(8,128)(2,1)} %all-gather.3.cloned.1.call-done, f32[32,4,8,128]{3,2,1,0:T(8,128)S(1)} %fusion.39, ...), kind=kOutput, calls=%fused_computation.23 | convolution fusion | flops 4379377664 | bytes 84701184 | tf_op jit(solution)/shard_map/rkgn,knd->rkgd/dot_general | solution.py:76
  444.5 0.8 copy.31
  (8 shorter events, 0.1 us)
Async XLA Ops:
  6.5 158.2 %copy-start = (bf16[32,32,128]{2,1,0:T(8,128)(2,1)S(1)}, bf16[32,32,128]{2,1,0:T(8,128)(2,1)}, u32[]{:S(2)}) copy-start(bf16[32,32,128]{2,1,0:T(8,128)(2,1)} %param.14) | copy-start | bytes 786436
  6.5 150.1 %reduce-scatter.2.cloned.1.call-start = ((), (), s32[]{:S(2)}) async-start(), calls=%async_computation.1 | async-start | bytes 12582912 | tf_op jit(solution)/shard_map/reduce_scatter | solution.py:50
  54.6 110.1 %copy-start.2 = (s32[32]{0:T(128)S(1)}, s32[32]{0:T(128)}, u32[]{:S(2)}) copy-start(s32[32]{0:T(128)} %param.17) | copy-start | bytes 388
  54.6 233.7 %all-gather.5.cloned.1.call-start = ((), (), s32[]{:S(2)}) async-start(), calls=%async_computation.3 | async-start | bytes 17825792 | tf_op jit(solution)/shard_map/all_gather | solution.py:63
  161.2 254.7 %all-gather.3.cloned.1.call-start = ((), (), s32[]{:S(2)}) async-start(), calls=%async_computation.2 | async-start | bytes 17825792 | tf_op jit(solution)/shard_map/all_gather | solution.py:64
  415.9 29.4 %copy-start.1 = (bf16[32,32,128]{2,1,0:T(8,128)(2,1)S(1)}, bf16[32,32,128]{2,1,0:T(8,128)(2,1)}, u32[]{:S(2)}) copy-start(bf16[32,32,128]{2,1,0:T(8,128)(2,1)} %param.14) | copy-start | bytes 786436
Sparse Core Ops, SparseCore 0:
  54.7 101.9 reduce-scatter.1
  161.4 126.8 all-gather.4
  290.7 125.1 all-gather.2
where the time goes:
time: 452 us
  waiting for transfers between devices  287 us (63%)
  matrix products  99.1 us (22%)
  other arithmetic  36.9 us (8%)
  between operations  14.5 us (3%)
  local copies, waits for them, and re-layouts  14.4 us (3%)
    all_gather x1, waiting for transfers between devices, on_device(): piece_keys = lax.all_gather(page_keys, 'grp', axis=1, tiled=True)  118 us
    reduce_scatter x1, waiting for transfers between devices, on_device(): lax.psum_scatter(stacked.transpose(1, 0, 2), 'tp', scatter_dimension=0, t...  99.3 us
    all_gather x1, waiting for transfers between devices, on_device(): piece_values = lax.all_gather(page_values, 'grp', axis=1, tiled=True)  69.6 us
    dot_general x1, matrix products, on_device(): jnp.einsum('rkgd,knd->rkgn', grouped, piece_keys, preferred_element_type=...  29.9 us
    dot_general x1, matrix products, on_device(): jnp.einsum('rkgn,knd->rkgd', weights.astype(jnp.bfloat16), piece_values,...  28.6 us
    reduce_sum x1, other arithmetic, on_device(): denominator = weights.sum(-1)  22.7 us
    dot_general x1, matrix products, on_device(): jnp.dot(prefill_states, key_weight, preferred_element_type=jnp.float32)  15.1 us
    dot_general x1, matrix products, on_device(): jnp.dot(prefill_states, value_weight, preferred_element_type=jnp.float32)  15 us
  transfers between devices with their start and end apart: 3, of which 3 were waited for; matrix products, arithmetic and copies ran while one was open for 15% of the time, Pallas kernels for 0%

commit v1 on v0

v1 whole, which is shorter than its diff:
```python
import functools

import jax
import jax.numpy as jnp
import numpy as np
from jax import lax
from jax.experimental import pallas as pl
from jax.experimental.pallas import tpu as pltpu
from jax.sharding import PartitionSpec as P

HD = 128
PROMPTS = 2
CODE_BLOCKS = 16
CODE_TOP = 32000.0
STAT_ROWS = 16
EMPTY = -1e30
LOG2E = 1.4426950408889634
BIG = 60 * 1024 * 1024


def encode(values):
    rows = values.shape[0]
    blocks = values.reshape(CODE_BLOCKS, rows // CODE_BLOCKS, HD)
    largest = jnp.maximum(jnp.max(jnp.abs(blocks), axis=1), 1e-30)
    exponent = jnp.floor(jnp.log(largest) * LOG2E) + 1.0
    factor = jnp.exp2(-exponent) * CODE_TOP
    codes = jnp.round(blocks * factor[:, None, :]).astype(jnp.int32).astype(jnp.int16)
    return codes.reshape(rows, HD), exponent.astype(jnp.int32).astype(jnp.int16)


def decode(codes, exponent):
    rows = codes.shape[0]
    factor = jnp.exp2(exponent.astype(jnp.int32).astype(jnp.float32)) * (1.0 / CODE_TOP)
    blocks = codes.astype(jnp.int32).astype(jnp.float32).reshape(CODE_BLOCKS, rows // CODE_BLOCKS, HD)
    return (blocks * factor[:, None, :]).reshape(rows, HD)


def send_kernel(steps, heads, target_ref, x_ref, wk_ref, wv_ref, out_ref, key_acc, value_acc):
    step = pl.program_id(0)

    @pl.when(step == 0)
    def _():
        key_acc[...] = jnp.zeros_like(key_acc)
        value_acc[...] = jnp.zeros_like(value_acc)

    key_acc[...] += jnp.dot(x_ref[...], wk_ref[...], preferred_element_type=jnp.float32)
    value_acc[...] += jnp.dot(x_ref[...], wv_ref[...], preferred_element_type=jnp.float32)

    @pl.when(step == steps - 1)
    def _():
        rows = x_ref.shape[0]
        for head in range(heads):
            lanes = slice(head * HD, (head + 1) * HD)
            for half, acc in ((0, key_acc), (1, value_acc)):
                codes, exponent = encode(acc[:, lanes])
                out_ref[head, :rows, half * HD : (half + 1) * HD] = codes
                out_ref[head, rows:, half * HD : (half + 1) * HD] = exponent


def project_send(x, wk, wv, target, chunk, heads, kv_local):
    rows, depth = x.shape
    tile = min(512, depth)
    steps = depth // tile
    width = heads * HD
    per_target = kv_local // heads
    weight_spec = pl.BlockSpec((tile, width), lambda k, t: (k, t[0] * per_target + chunk))
    return pl.pallas_call(
        functools.partial(send_kernel, steps, heads),
        out_shape=jax.ShapeDtypeStruct((heads, rows + CODE_BLOCKS, 2 * HD), jnp.int16),
        grid_spec=pltpu.PrefetchScalarGridSpec(
            num_scalar_prefetch=1,
            grid=(steps,),
            in_specs=[pl.BlockSpec((rows, tile), lambda k, t: (0, k)), weight_spec, weight_spec],
            out_specs=pl.BlockSpec((heads, rows + CODE_BLOCKS, 2 * HD), lambda k, t: (0, 0, 0)),
            scratch_shapes=[pltpu.VMEM((rows, width), jnp.float32), pltpu.VMEM((rows, width), jnp.float32)],
        ),
        compiler_params=pltpu.CompilerParams(vmem_limit_bytes=BIG),
        cost_estimate=pl.CostEstimate(
            flops=4 * rows * depth * width,
            bytes_accessed=2 * rows * depth + 4 * depth * width + 4 * rows * width,
            transcendentals=0,
        ),
        name="project_send",
    )(target, x, wk, wv)


def own_kernel(target_ref, x_ref, wk_ref, wv_ref, key_ref, value_ref):
    @pl.when(pl.program_id(0) == 0)
    def _():
        key_ref[...] = jnp.zeros_like(key_ref)
        value_ref[...] = jnp.zeros_like(value_ref)

    key_ref[...] += jnp.dot(x_ref[...], wk_ref[...], preferred_element_type=jnp.float32)
    value_ref[...] += jnp.dot(x_ref[...], wv_ref[...], preferred_element_type=jnp.float32)


def project_own(x, wk, wv, target, kv_local):
    rows, depth = x.shape
    tile = min(512, depth)
    steps = depth // tile
    width = kv_local * HD
    weight_spec = pl.BlockSpec((tile, width), lambda k, t: (k, t[0]))
    out_spec = pl.BlockSpec((rows, width), lambda k, t: (0, 0))
    out_shape = jax.ShapeDtypeStruct((rows, width), jnp.float32)
    return pl.pallas_call(
        own_kernel,
        out_shape=(out_shape, out_shape),
        grid_spec=pltpu.PrefetchScalarGridSpec(
            num_scalar_prefetch=1,
            grid=(steps,),
            in_specs=[pl.BlockSpec((rows, tile), lambda k, t: (0, k)), weight_spec, weight_spec],
            out_specs=(out_spec, out_spec),
        ),
        compiler_params=pltpu.CompilerParams(vmem_limit_bytes=BIG),
        cost_estimate=pl.CostEstimate(
            flops=4 * rows * depth * width,
            bytes_accessed=2 * rows * depth + 4 * depth * width + 8 * rows * width,
            transcendentals=0,
        ),
        name="project_own",
    )(target, x, wk, wv)


def pack(context, logsum):
    high = logsum.astype(jnp.bfloat16).astype(jnp.float32)
    middle = (logsum - high).astype(jnp.bfloat16).astype(jnp.float32)
    low = logsum - high - middle
    line = lax.broadcasted_iota(jnp.int32, (STAT_ROWS, context.shape[1]), 0)
    stats = jnp.where(line == 0, high, jnp.where(line == 1, middle, jnp.where(line == 2, low, 0.0)))
    return context.astype(jnp.bfloat16), stats.astype(jnp.bfloat16)


def attend_kernel(
    parts, per, slots, order_ref, place_ref, key_ref, value_ref, cos_ref, sin_ref, q_ref, *rest
):
    received = rest[:parts]
    keep_ref, keep_log_ref, send_ref = rest[parts : parts + 3]
    key_scr, value_scr, context_scr, log_scr = rest[parts + 3 :]
    rows = key_ref.shape[0]
    keys = key_ref[...]
    values = value_ref[...]
    for part in received:
        keys = keys + decode(part[0, :rows, :HD], part[0, rows:, :HD])
        values = values + decode(part[0, :rows, HD:], part[0, rows:, HD:])
    keys = keys * cos_ref[...] + pltpu.roll(keys, HD // 2, 1) * sin_ref[...]
    key_scr[...] = keys.astype(jnp.bfloat16)
    value_scr[...] = jnp.transpose(values).astype(jnp.bfloat16)
    to_log2 = HD ** (-0.5) * LOG2E

    def one(index):
        scores = jnp.dot(key_scr[...], q_ref[order_ref[index]], preferred_element_type=jnp.float32)
        top = jnp.max(scores, axis=0, keepdims=True) * to_log2
        weights = jnp.exp2(scores * to_log2 - top)
        total = jnp.sum(weights, axis=0, keepdims=True)
        summed = jnp.dot(value_scr[...], weights.astype(jnp.bfloat16), preferred_element_type=jnp.float32)
        context_scr[place_ref[index]] = summed * (1.0 / total)
        log_scr[place_ref[index]] = jnp.broadcast_to(top + jnp.log(total) * LOG2E, log_scr.shape[1:])

    def empty(index):
        context_scr[place_ref[index]] = jnp.zeros(context_scr.shape[1:], jnp.float32)
        log_scr[place_ref[index]] = jnp.full(log_scr.shape[1:], EMPTY, jnp.float32)

    @pl.loop(0, per // 2)
    def _(index):
        one(2 * index)
        one(2 * index + 1)

    @pl.loop(per, slots)
    def _(index):
        empty(index)

    half = slots // 2
    for slot in range(half):
        keep_ref[0, slot] = context_scr[slot]
        keep_log_ref[0, slot] = log_scr[slot]
        context, stats = pack(context_scr[half + slot], log_scr[half + slot][:1])
        send_ref[0, slot, :HD] = context
        send_ref[0, slot, HD:] = stats


def attend(order, place, keys, values, cosine, sine, q_all, received, chunk, heads, per):
    rows = keys.shape[0]
    slots, _, wide = q_all.shape
    half = slots // 2
    head_spec = pl.BlockSpec((rows, HD), lambda h, a, b: (0, chunk * heads + h))
    table_spec = pl.BlockSpec((rows, HD), lambda h, a, b: (0, 0))
    part_spec = pl.BlockSpec((1, rows + CODE_BLOCKS, 2 * HD), lambda h, a, b: (h, 0, 0))

    def slot_spec(depth):
        return pl.BlockSpec((1, half, depth, wide), lambda h, a, b: (h, 0, 0, 0))

    return pl.pallas_call(
        functools.partial(attend_kernel, len(received), per, slots),
        out_shape=(
            jax.ShapeDtypeStruct((heads, half, HD, wide), jnp.float32),
            jax.ShapeDtypeStruct((heads, half, 8, wide), jnp.float32),
            jax.ShapeDtypeStruct((heads, half, HD + STAT_ROWS, wide), jnp.bfloat16),
        ),
        grid_spec=pltpu.PrefetchScalarGridSpec(
            num_scalar_prefetch=2,
            grid=(heads,),
            in_specs=[
                head_spec,
                head_spec,
                table_spec,
                table_spec,
                pl.BlockSpec((slots, HD, wide), lambda h, a, b: (0, chunk * heads + h, 0)),
            ]
            + [part_spec] * len(received),
            out_specs=(slot_spec(HD), slot_spec(8), slot_spec(HD + STAT_ROWS)),
            scratch_shapes=[
                pltpu.VMEM((rows, HD), jnp.bfloat16),
                pltpu.VMEM((HD, rows), jnp.bfloat16),
                pltpu.VMEM((slots, HD, wide), jnp.float32),
                pltpu.VMEM((slots, 8, wide), jnp.float32),
            ],
        ),
        compiler_params=pltpu.CompilerParams(vmem_limit_bytes=BIG),
        cost_estimate=pl.CostEstimate(
            flops=8 * heads * per * rows * wide * HD,
            bytes_accessed=heads * (rows * HD * 16 + slots * HD * wide * 6),
            transcendentals=heads * per * rows * wide,
        ),
        name="attend",
    )(order, place, keys, values, cosine, sine, q_all, *received)


def merge_kernel(last, keep_ref, keep_log_ref, part_ref, *outs):
    heads, count = keep_ref.shape[:2]
    half = count // 2
    for head in range(heads):
        for slot in range(count):
            stats = part_ref[head, slot, HD:].astype(jnp.float32)
            other_log = stats[0:1] + stats[1:2] + stats[2:3]
            own_log = keep_log_ref[head, slot][:1]
            top = jnp.maximum(own_log, other_log)
            own_share = jnp.exp2(own_log - top)
            other_share = jnp.exp2(other_log - top)
            total = own_share + other_share
            inverse = 1.0 / total
            context = keep_ref[head, slot] * (own_share * inverse) + part_ref[
                head, slot, :HD
            ].astype(jnp.float32) * (other_share * inverse)
            logsum = top + jnp.log(total) * LOG2E
            if last:
                outs[0][head] = jnp.transpose(context)
                outs[1][head] = jnp.broadcast_to(logsum, (8, logsum.shape[1]))
            elif slot < half:
                outs[0][head, slot] = context
                outs[1][head, slot] = jnp.broadcast_to(logsum, (8, logsum.shape[1]))
            else:
                packed, stats = pack(context, logsum)
                outs[2][head, slot - half, :HD] = packed
                outs[2][head, slot - half, HD:] = stats


def merge(keep, keep_log, part):
    heads, count, _, wide = keep.shape
    half = count // 2
    last = count == 1
    if last:
        out_shape = (
            jax.ShapeDtypeStruct((heads, wide, HD), jnp.float32),
            jax.ShapeDtypeStruct((heads, 8, wide), jnp.float32),
        )
    else:
        out_shape = (
            jax.ShapeDtypeStruct((heads, half, HD, wide), jnp.float32),
            jax.ShapeDtypeStruct((heads, half, 8, wide), jnp.float32),
            jax.ShapeDtypeStruct((heads, half, HD + STAT_ROWS, wide), jnp.bfloat16),
        )
    return pl.pallas_call(
        functools.partial(merge_kernel, last),
        out_shape=out_shape,
        compiler_params=pltpu.CompilerParams(vmem_limit_bytes=BIG),
        cost_estimate=pl.CostEstimate(
            flops=4 * heads * count * HD * wide,
            bytes_accessed=heads * count * HD * wide * 9,
            transcendentals=0,
        ),
        name="merge",
    )(keep, keep_log, part)


def tables(offset, rows):
    half_width = HD // 2
    inverse_freq = 500000.0 ** (-(jnp.arange(half_width, dtype=jnp.float32) * 2.0 / HD))
    positions = offset + jnp.arange(rows, dtype=jnp.int32)
    angles = positions.astype(jnp.float32)[:, None] * inverse_freq[None, :]
    cosine = jnp.cos(angles)
    sine = jnp.sin(angles)
    return jnp.concatenate([cosine, cosine], 1), jnp.concatenate([-sine, sine], 1)


def bit_reversed(values, bits):
    flipped = jnp.zeros_like(values)
    for bit in range(bits):
        flipped = flipped + (((values >> bit) & 1) << (bits - 1 - bit))
    return flipped


def on_device(
    prefill_states,
    key_weight,
    value_weight,
    offsets,
    matching,
    queries,
    cache_keys,
    cache_values,
    cache_lengths,
):
    tp = lax.axis_size("tp")
    groups = lax.axis_size("grp")
    per = groups // PROMPTS
    bits = groups.bit_length() - 1
    me = lax.axis_index("grp")
    rank = lax.axis_index("tp")
    block_len = prefill_states.shape[0]
    kv_local = key_weight.shape[1] // HD // tp
    row_count = queries.shape[0]
    group_size = queries.shape[1] // kv_local
    wide = row_count * group_size
    heads = 2 if kv_local % 2 == 0 else 1
    chunks = kv_local // heads

    grouped = queries.reshape(row_count, kv_local, group_size, HD)
    turned = grouped.transpose(1, 3, 0, 2).reshape(kv_local * HD, wide)
    tag = jnp.broadcast_to(matching[0].astype(jnp.bfloat16), (STAT_ROWS, wide))
    q_all = lax.all_gather(jnp.concatenate([turned, tag], 0), "grp")
    wanted = q_all[:, kv_local * HD, 0].astype(jnp.int32)

    received = []
    for chunk in range(chunks):
        parts = []
        for shift in range(1, tp):
            target = ((rank + shift) % tp).astype(jnp.int32).reshape(1)
            coded = project_send(
                prefill_states, key_weight, value_weight, target, chunk, heads, kv_local
            )
            parts.append(
                lax.ppermute(coded, "tp", [(i, (i + shift) % tp) for i in range(tp)])
            )
        received.append(parts)
    own_keys, own_values = project_own(
        prefill_states, key_weight, value_weight, rank.astype(jnp.int32).reshape(1), kv_local
    )
    cosine, sine = tables(offsets[0], block_len)

    mine = (wanted == me // per).astype(jnp.int32)
    rank_in = jnp.cumsum(mine) - 1
    rank_out = per + jnp.cumsum(1 - mine) - 1
    spot = jnp.where(mine == 1, rank_in, rank_out)
    names = jnp.arange(groups, dtype=jnp.int32)
    order = jnp.sum(jnp.where(spot[None, :] == names[:, None], names[None, :], 0), 1).astype(jnp.int32)
    place = bit_reversed(order ^ me.astype(jnp.int32), bits)

    score_scale = HD ** (-0.5)
    cache_len = cache_keys.shape[2]
    cache_scores = (
        jnp.einsum("rkgd,rktd->rkgt", grouped, cache_keys, preferred_element_type=jnp.float32)
        * score_scale
    )
    alive = (jnp.arange(cache_len, dtype=jnp.int32)[None, :] < cache_lengths[:, None])[:, None, None, :]
    cache_scores = jnp.where(alive, cache_scores, EMPTY)
    cache_top = cache_scores.max(-1)
    cache_weights = jnp.where(alive, jnp.exp(cache_scores - cache_top[..., None]), 0.0)
    cache_total = cache_weights.sum(-1)
    cache_sum = jnp.einsum(
        "rkgt,rktd->rkgd",
        cache_weights.astype(jnp.bfloat16),
        cache_values,
        preferred_element_type=jnp.float32,
    )

    contexts = []
    logs = []
    for chunk in range(chunks):
        keep, keep_log, send = attend(
            order, place, own_keys, own_values, cosine, sine, q_all, received[chunk], chunk, heads, per
        )
        for bit in range(bits):
            arrived = lax.ppermute(send, "grp", [(i, i ^ (1 << bit)) for i in range(groups)])
            if bit < bits - 1:
                keep, keep_log, send = merge(keep, keep_log, arrived)
            else:
                context, log = merge(keep, keep_log, arrived)
        contexts.append(context)
        logs.append(log[:, 0])
    prompt_context = jnp.concatenate(contexts, 0).reshape(kv_local, row_count, group_size, HD)
    prompt_context = prompt_context.transpose(1, 0, 2, 3)
    prompt_log = jnp.concatenate(logs, 0).reshape(kv_local, row_count, group_size).transpose(1, 0, 2)
    cache_log = cache_top * LOG2E
    top = jnp.maximum(prompt_log, cache_log)
    prompt_share = jnp.exp2(prompt_log - top)
    cache_share = jnp.exp2(cache_log - top)
    total = prompt_share + cache_share * cache_total
    context = (prompt_context * prompt_share[..., None] + cache_sum * cache_share[..., None]) / total[..., None]
    return context.reshape(row_count, kv_local * group_size, HD).astype(jnp.bfloat16)


def solution(mesh):
    placed = (
        P("grp", "tp"),
        P("tp", None),
        P("tp", None),
        P("grp"),
        P("grp"),
        P("grp", "tp", None),
        P("grp", "tp", None, None),
        P("grp", "tp", None, None),
        P("grp"),
    )
    return jax.shard_map(
        on_device, mesh=mesh, in_specs=placed, out_specs=P("grp", "tp", None), check_vma=False
    )
```

time: 452 us -> 181 us (0.40)
  waiting for transfers between devices: 287 us -> 34.5 us
  Pallas kernels: 0 us -> 90.3 us
  matrix products: 99.1 us -> 11.3 us
  other arithmetic: 36.9 us -> 6.17 us
  starting transfers between devices: 0.27 us -> 11.5 us
    all_gather x2 -> x1, waiting for transfers between devices: 187 us -> 11.3 us  [on_device(): q_all = lax.all_gather(jnp.concatenate([turned, tag], 0), 'grp')]
    reduce_scatter x1 -> x0, waiting for transfers between devices: 99.3 us -> none  [on_device(): lax.psum_scatter(stacked.transpose(1, 0, 2), 'tp', scatter_dimension=0, t...]
    pallas_call x0 -> x13, Pallas kernels: none -> 90.3 us  [the longest x2 34.4 us: attend(): pl.pallas_call(functools.partial(attend_kernel, len(received), per, slots...]
    dot_general x4 -> x0, matrix products: 88.5 us -> none  [the longest x1 29.9 us: on_device(): jnp.einsum('rkgd,knd->rkgn', grouped, piece_keys, preferred_element_type=...]
    ppermute x0 -> x10, waiting for transfers between devices: none -> 23.2 us  [the longest x8 23.2 us: on_device(): lax.ppermute(send, 'grp', [(i, i ^ 1 << bit) for i in range(groups)])]
    reduce_sum x2, other arithmetic: 23.2 us -> 0.59 us  [the longest x1 0.47 us: on_device(): cache_total = cache_weights.sum(-1)]
    ppermute x0 -> x10, starting transfers between devices: none -> 11.5 us  [the longest x8 8.53 us: on_device(): lax.ppermute(send, 'grp', [(i, i ^ 1 << bit) for i in range(groups)])]
    reshape x2 -> x1, local copies, waits for them, and re-layouts: 10.6 us -> 1.05 us  [on_device(): grouped = queries.reshape(row_count, kv_local, group_size, HD)]
  transfers between devices with their start and end apart: 3 -> 11, of which waited for: 3 -> 4; matrix products, arithmetic and copies ran while one was open for 15% -> 7% of each run, Pallas kernels for 0% -> 49%
where the time goes in v1:
time: 181 us; the launch traced here: 180 us
  Pallas kernels  90.3 us (50%)
  waiting for transfers between devices  34.5 us (19%)
  between operations  14.9 us (8%)
  local copies, waits for them, and re-layouts  11.7 us (6%)
  starting transfers between devices  11.5 us (6%)
  matrix products  11.3 us (6%)
  other arithmetic  6.17 us (3%)
    pallas_call x2, Pallas kernels, attend(): pl.pallas_call(functools.partial(attend_kernel, len(received), per, slots...  34.4 us
    ppermute x8, waiting for transfers between devices, on_device(): lax.ppermute(send, 'grp', [(i, i ^ 1 << bit) for i in range(groups)])  23.2 us
    pallas_call x2, Pallas kernels, project_send(): pl.pallas_call(functools.partial(send_kernel, steps, heads), out_shape=ja...  22 us
    pallas_call x8, Pallas kernels, merge(): pl.pallas_call(functools.partial(merge_kernel, last), out_shape=out_shape...  19.6 us
    pallas_call x1, Pallas kernels, project_own(): pl.pallas_call(own_kernel, out_shape=(out_shape, out_shape), grid_spec=pl...  14.3 us
    all_gather x1, waiting for transfers between devices, on_device(): q_all = lax.all_gather(jnp.concatenate([turned, tag], 0), 'grp')  11.3 us
    ppermute x8, starting transfers between devices, on_device(): lax.ppermute(send, 'grp', [(i, i ^ 1 << bit) for i in range(groups)])  8.53 us
    unnamed x26, local copies, waits for them, and re-layouts  7.68 us
  transfers between devices with their start and end apart: 11, of which 4 were waited for; matrix products, arithmetic and copies ran while one was open for 7% of the time, Pallas kernels for 49%

profile of v1, /device:TPU:0, one launch (start us, length us, event | category | flops | bytes accessed | tf_op | source)
XLA Modules:
  0.0 180.4 jit_solution(7876299864705276841)
XLA Ops:
  6.5 1.1 copy.59
  9.2 10.9 %project_send.2 = s16[2,1040,256]{2,1,0:T(8,128)(2,1)} custom-call(s32[1]{0:T(128)} %bitcast.7.target_ref, bf16[1024,4096]{1,0:T(8,128)(2,1)} %x_ref.5, bf16[4096,1024]{1,0:T(8,128)(2,1)} %wk_ref.5, bf16[4096,1024]{1,0:T(8,128)(2,1)} %wv_ref.5), custom_call_target="tpu_custom_call" | custom-call | flops 4294967296 | bytes 13631488 | tf_op jit(solution)/shard_map/project_send/pallas_call | solution.py:67
  20.1 3.0 %collective-permute-start = (s16[2,1040,256]{2,1,0:T(8,128)(2,1)}, s16[2,1040,256]{2,1,0:T(8,128)(2,1)S(1)}, u32[]{:S(2)}, u32[]{:S(2)}) collective-permute-start(s16[2,1040,256]{2,1,0:T(8,128)(2,1)} %project_send.2), channel_id=1, source_target_pairs={{0,1},{1,0},{2,3},{3,2},{4,5},{5,4},{6,7},{7,6},{8,9},{9,8},{10,11... | collective-permute-start | bytes 3194888 | tf_op jit(solution)/shard_map/ppermute | solution.py:342
  23.1 11.0 %project_send.3 = s16[2,1040,256]{2,1,0:T(8,128)(2,1)} custom-call(s32[1]{0:T(128)} %bitcast.7.target_ref, bf16[1024,4096]{1,0:T(8,128)(2,1)} %x_ref.5, bf16[4096,1024]{1,0:T(8,128)(2,1)} %wk_ref.5, bf16[4096,1024]{1,0:T(8,128)(2,1)} %wv_ref.5), custom_call_target="tpu_custom_call" | custom-call | flops 4294967296 | bytes 13631488 | tf_op jit(solution)/shard_map/project_send/pallas_call | solution.py:67
  34.8 1.9 %fusion.11 = (f32[1024,64]{1,0:T(8,128)S(1)}, f32[1024,64]{1,0:T(8,128)S(1)}, f32[1024,64]{1,0:T(8,128)S(1)}) fusion(f32[64]{0:T(128)S(1)} %negate_power_fusion, f32[1024]{0:T(1024)S(1)} %add_convert_fusion), kind=kLoop, calls=%fused_computation.21 | loop fusion | flops 131072 | bytes 790784 | tf_op jit(solution)/shard_map/neg | solution.py:292
  36.7 14.3 %project_own.1 = (f32[1024,512]{1,0:T(8,128)}, f32[1024,512]{1,0:T(8,128)}) custom-call(s32[1]{0:T(128)} %bitcast.5.target_ref, bf16[1024,4096]{1,0:T(8,128)(2,1)} %x_ref.5, bf16[4096,1024]{1,0:T(8,128)(2,1)} %wk_ref.5, bf16[4096,1024]{1,0:T(8,128)(2,1)} %wv_ref.5), custom_call_target="tpu_custom_call" | custom-call | flops 8589934592 | bytes 20971520 | tf_op jit(solution)/shard_map/project_own/pallas_call | solution.py:105
  51.0 1.3 pad_maximum_fusion
  52.4 11.3 %all-gather.3.cloned.1.call-done = bf16[8448,256]{1,0:T(8,128)(2,1)} async-done(((bf16[528,256]{1,0:T(8,128)(2,1)}), bf16[8448,256]{1,0:T(8,128)(2,1)}) %all-gather.3.cloned.1.call-update) | async-done | bytes 4325392 | tf_op jit(solution)/shard_map/all_gather | solution.py:330
  63.6 1.1 fusion.20
  66.1 1.0 copy-done.10
  67.1 17.2 %attend.2 = (f32[2,8,128,256]{3,2,1,0:T(8,128)}, f32[2,8,8,256]{3,2,1,0:T(8,128)}, bf16[2,8,144,256]{3,2,1,0:T(8,128)(2,1)}) custom-call(s32[16]{0:T(128)} %copy-done.11, s32[16]{0:T(128)} %shift-left_add_fusion.place_ref, f32[1024,512]{1,0:T(8,128)} %get-tuple-element.35.key_ref, f32[1024,512]{1,0:T(8,128)} %get-tuple-element.36.value_ref, ...), custom_call_target="tpu_custom_call" | custom-call | flops 4294967296 | bytes 10485760 | tf_op jit(solution)/shard_map/attend/pallas_call | solution.py:192
  84.5 17.2 %attend.3 = (f32[2,8,128,256]{3,2,1,0:T(8,128)}, f32[2,8,8,256]{3,2,1,0:T(8,128)}, bf16[2,8,144,256]{3,2,1,0:T(8,128)(2,1)}) custom-call(s32[16]{0:T(128)} %copy-done.11, s32[16]{0:T(128)} %shift-left_add_fusion.place_ref, f32[1024,512]{1,0:T(8,128)} %get-tuple-element.35.key_ref, f32[1024,512]{1,0:T(8,128)} %get-tuple-element.36.value_ref, ...), custom_call_target="tpu_custom_call" | custom-call | flops 4294967296 | bytes 10485760 | tf_op jit(solution)/shard_map/attend/pallas_call | solution.py:192
  102.1 1.1 copy-done
  103.2 3.5 %merge.8 = (f32[2,4,128,256]{3,2,1,0:T(8,128)}, f32[2,4,8,256]{3,2,1,0:T(8,128)}, bf16[2,4,144,256]{3,2,1,0:T(8,128)(2,1)}) custom-call(f32[2,8,128,256]{3,2,1,0:T(8,128)} %get-tuple-element.37.keep_ref, f32[2,8,8,256]{3,2,1,0:T(8,128)} %get-tuple-element.38.keep_log_ref, bf16[2,8,144,256]{3,2,1,0:T(8,128)(2,1)} %copy-done), custom_call_target="tpu_custom_call" | custom-call | flops 2097152 | bytes 4718592 | tf_op jit(solution)/shard_map/merge/pallas_call | solution.py:272
  107.3 1.0 copy-done.1
  108.3 3.5 %merge.12 = (f32[2,4,128,256]{3,2,1,0:T(8,128)}, f32[2,4,8,256]{3,2,1,0:T(8,128)}, bf16[2,4,144,256]{3,2,1,0:T(8,128)(2,1)}) custom-call(f32[2,8,128,256]{3,2,1,0:T(8,128)} %get-tuple-element.50.keep_ref, f32[2,8,8,256]{3,2,1,0:T(8,128)} %get-tuple-element.51.keep_log_ref, bf16[2,8,144,256]{3,2,1,0:T(8,128)(2,1)} %copy-done.1), custom_call_target="tpu_custom_call" | custom-call | flops 2097152 | bytes 4718592 | tf_op jit(solution)/shard_map/merge/pallas_call | solution.py:272
  111.8 1.5 collective-permute-start.7
  113.3 9.7 %collective-permute-done.2.part_ref = bf16[2,4,144,256]{3,2,1,0:T(8,128)(2,1)S(1)} collective-permute-done((bf16[2,4,144,256]{3,2,1,0:T(8,128)(2,1)}, bf16[2,4,144,256]{3,2,1,0:T(8,128)(2,1)S(1)}, u32[]{:S(2)}, u32[]{:S(2)}) %collective-permute-start.2) | collective-permute-done | bytes 589856 | tf_op jit(solution)/shard_map/ppermute | solution.py:383
  123.9 2.5 %merge.9 = (f32[2,2,128,256]{3,2,1,0:T(8,128)}, f32[2,2,8,256]{3,2,1,0:T(8,128)}, bf16[2,2,144,256]{3,2,1,0:T(8,128)(2,1)}) custom-call(f32[2,4,128,256]{3,2,1,0:T(8,128)} %get-tuple-element.40.keep_ref, f32[2,4,8,256]{3,2,1,0:T(8,128)} %get-tuple-element.41.keep_log_ref, bf16[2,4,144,256]{3,2,1,0:T(8,128)(2,1)} %copy-done.3), custom_call_target="tpu_custom_call" | custom-call | flops 1048576 | bytes 2359296 | tf_op jit(solution)/shard_map/merge/pallas_call | solution.py:272
  126.4 1.5 collective-permute-start.3
  127.9 7.2 %collective-permute-done.7.part_ref = bf16[2,4,144,256]{3,2,1,0:T(8,128)(2,1)S(1)} collective-permute-done((bf16[2,4,144,256]{3,2,1,0:T(8,128)(2,1)}, bf16[2,4,144,256]{3,2,1,0:T(8,128)(2,1)S(1)}, u32[]{:S(2)}, u32[]{:S(2)}) %collective-permute-start.7) | collective-permute-done | bytes 589856 | tf_op jit(solution)/shard_map/ppermute | solution.py:383
  135.9 2.5 %merge.13 = (f32[2,2,128,256]{3,2,1,0:T(8,128)}, f32[2,2,8,256]{3,2,1,0:T(8,128)}, bf16[2,2,144,256]{3,2,1,0:T(8,128)(2,1)}) custom-call(f32[2,4,128,256]{3,2,1,0:T(8,128)} %get-tuple-element.53.keep_ref, f32[2,4,8,256]{3,2,1,0:T(8,128)} %get-tuple-element.54.keep_log_ref, bf16[2,4,144,256]{3,2,1,0:T(8,128)(2,1)} %copy-done.4), custom_call_target="tpu_custom_call" | custom-call | flops 1048576 | bytes 2359296 | tf_op jit(solution)/shard_map/merge/pallas_call | solution.py:272
  138.3 1.5 collective-permute-start.8
  139.9 5.8 %fusion.21 = (f32[32,4,8]{2,1,0:T(4,128)S(1)}, f32[32,4,8,256]{3,2,1,0:T(8,128)S(1)}) fusion(bf16[32,4,256,128]{3,2,1,0:T(8,128)(2,1)} %param.15, bf16[32,32,128]{2,1,0:T(8,128)(2,1)S(1)} %copy-done.2, pred[32,256]{1,0:T(8,128)(4,1)S(1)} %iota_compare_fusion), kind=kOutput, calls=%fused_computation.47 | convolution fusion | flops 67894272 | bytes 9711616 | tf_op jit(solution)/shard_map/rkgd,rktd->rkgt/dot_general | solution.py:361
  146.3 2.0 %merge.10 = (f32[2,1,128,256]{3,2,1,0:T(8,128)}, f32[2,1,8,256]{3,2,1,0:T(8,128)}, bf16[2,1,144,256]{3,2,1,0:T(8,128)(2,1)}) custom-call(f32[2,2,128,256]{3,2,1,0:T(8,128)} %get-tuple-element.43.keep_ref, f32[2,2,8,256]{3,2,1,0:T(8,128)} %get-tuple-element.44.keep_log_ref, bf16[2,2,144,256]{3,2,1,0:T(8,128)(2,1)} %copy-done.5), custom_call_target="tpu_custom_call" | custom-call | flops 524288 | bytes 1179648 | tf_op jit(solution)/shard_map/merge/pallas_call | solution.py:272
  148.3 0.9 collective-permute-start.4
  150.0 2.0 %merge.14 = (f32[2,1,128,256]{3,2,1,0:T(8,128)}, f32[2,1,8,256]{3,2,1,0:T(8,128)}, bf16[2,1,144,256]{3,2,1,0:T(8,128)(2,1)}) custom-call(f32[2,2,128,256]{3,2,1,0:T(8,128)} %get-tuple-element.56.keep_ref, f32[2,2,8,256]{3,2,1,0:T(8,128)} %get-tuple-element.57.keep_log_ref, bf16[2,2,144,256]{3,2,1,0:T(8,128)(2,1)} %copy-done.6), custom_call_target="tpu_custom_call" | custom-call | flops 524288 | bytes 1179648 | tf_op jit(solution)/shard_map/merge/pallas_call | solution.py:272
  151.9 2.0 %collective-permute-start.9 = (bf16[2,1,144,256]{3,2,1,0:T(8,128)(2,1)}, bf16[2,1,144,256]{3,2,1,0:T(8,128)(2,1)S(1)}, u32[]{:S(2)}, u32[]{:S(2)}) collective-permute-start(bf16[2,1,144,256]{3,2,1,0:T(8,128)(2,1)} %get-tuple-element.61), channel_id=1, source_target_pairs={{0,16},{2,18},{4,20},{6,22},{8,24},{10,26},{12,28},{14,30},{16,0},... | collective-permute-start | bytes 442376 | tf_op jit(solution)/shard_map/ppermute | solution.py:383
  154.6 6.3 %collective-permute-done.4.part_ref = bf16[2,1,144,256]{3,2,1,0:T(8,128)(2,1)S(1)} collective-permute-done((bf16[2,1,144,256]{3,2,1,0:T(8,128)(2,1)}, bf16[2,1,144,256]{3,2,1,0:T(8,128)(2,1)S(1)}, u32[]{:S(2)}, u32[]{:S(2)}) %collective-permute-start.4) | collective-permute-done | bytes 147488 | tf_op jit(solution)/shard_map/ppermute | solution.py:383
  161.5 1.9 %merge.11 = (f32[2,256,128]{2,1,0:T(8,128)}, f32[2,8,256]{2,1,0:T(8,128)}) custom-call(f32[2,1,128,256]{3,2,1,0:T(8,128)} %get-tuple-element.46.keep_ref, f32[2,1,8,256]{3,2,1,0:T(8,128)} %get-tuple-element.47.keep_log_ref, bf16[2,1,144,256]{3,2,1,0:T(8,128)(2,1)} %copy-done.8), custom_call_target="tpu_custom_call" | custom-call | flops 262144 | bytes 589824 | tf_op jit(solution)/shard_map/merge/pallas_call | solution.py:272
  164.9 1.9 %merge.15 = (f32[2,256,128]{2,1,0:T(8,128)}, f32[2,8,256]{2,1,0:T(8,128)}) custom-call(f32[2,1,128,256]{3,2,1,0:T(8,128)} %get-tuple-element.59.keep_ref, f32[2,1,8,256]{3,2,1,0:T(8,128)} %get-tuple-element.60.keep_log_ref, bf16[2,1,144,256]{3,2,1,0:T(8,128)(2,1)} %copy-done.7), custom_call_target="tpu_custom_call" | custom-call | flops 262144 | bytes 589824 | tf_op jit(solution)/shard_map/merge/pallas_call | solution.py:272
  168.0 5.5 %fusion.4 = bf16[32,32,128]{2,1,0:T(8,128)(2,1)} fusion(bf16[32,4,256,128]{3,2,1,0:T(8,128)(2,1)} %param.16, f32[32,4,8,256]{3,2,1,0:T(8,128)S(1)} %get-tuple-element.74, f32[32,4,8]{2,1,0:T(4,128)S(1)} %get-tuple-element.73, pred[32,256]{1,0:T(8,128)(4,1)S(1)} %iota_compare_fusion, f32[32,4,8]{2,1,0:T(4,128)S(1)} %copy.52, f32[32,4,8]{2,1,0:T(4,128)S(1)} %copy.50, ...), kind=kOutput, calls=%fused_computation.6 | convolution fusion | flops 68681728 | bytes 10248192 | tf_op jit(solution)/shard_map/rkgt,rktd->rkgd/dot_general | solution.py:369
  (62 shorter events, 10.6 us)
Async XLA Ops:
  6.5 57.1 %all-gather.3.cloned.1.call-start = ((), (), s32[]{:S(2)}) async-start(), calls=%async_computation | async-start | bytes 4595712 | tf_op jit(solution)/shard_map/all_gather | solution.py:330
  20.1 46.0 %collective-permute-start = (s16[2,1040,256]{2,1,0:T(8,128)(2,1)}, s16[2,1040,256]{2,1,0:T(8,128)(2,1)S(1)}, u32[]{:S(2)}, u32[]{:S(2)}) collective-permute-start(s16[2,1040,256]{2,1,0:T(8,128)(2,1)} %project_send.2), channel_id=1, source_target_pairs={{0,1},{1,0},{2,3},{3,2},{4,5},{5,4},{6,7},{7,6},{8,9},{9,8},{10,11... | collective-permute-start | bytes 3194888 | tf_op jit(solution)/shard_map/ppermute | solution.py:342
  34.1 50.4 %collective-permute-start.5 = (s16[2,1040,256]{2,1,0:T(8,128)(2,1)}, s16[2,1040,256]{2,1,0:T(8,128)(2,1)}, u32[]{:S(2)}, u32[]{:S(2)}) collective-permute-start(s16[2,1040,256]{2,1,0:T(8,128)(2,1)} %project_send.3), channel_id=1, source_target_pairs={{0,1},{1,0},{2,3},{3,2},{4,5},{5,4},{6,7},{7,6},{8,9},{9,8},{10,11... | collective-permute-start | bytes 3194888 | tf_op jit(solution)/shard_map/ppermute | solution.py:342
  65.5 0.6 copy-start.11
  66.1 1.0 copy-start.10
  84.3 17.8 %collective-permute-start.1 = (bf16[2,8,144,256]{3,2,1,0:T(8,128)(2,1)}, bf16[2,8,144,256]{3,2,1,0:T(8,128)(2,1)S(1)}, u32[]{:S(2)}, u32[]{:S(2)}) collective-permute-start(bf16[2,8,144,256]{3,2,1,0:T(8,128)(2,1)} %get-tuple-element.39), channel_id=1, source_target_pairs={{0,2},{2,0},{4,6},{6,4},{8,10},{10,8},{12,14},{14,12},{16,18},{18,... | collective-permute-start | bytes 3538952 | tf_op jit(solution)/shard_map/ppermute | solution.py:383
  101.8 11.5 %copy-start.9 = (s32[32]{0:T(128)S(1)}, s32[32]{0:T(128)}, u32[]{:S(2)}) copy-start(s32[32]{0:T(128)} %param.17) | copy-start | bytes 388
  101.8 5.5 %collective-permute-start.6 = (bf16[2,8,144,256]{3,2,1,0:T(8,128)(2,1)}, bf16[2,8,144,256]{3,2,1,0:T(8,128)(2,1)S(1)}, u32[]{:S(2)}, u32[]{:S(2)}) collective-permute-start(bf16[2,8,144,256]{3,2,1,0:T(8,128)(2,1)} %get-tuple-element.52), channel_id=1, source_target_pairs={{0,2},{2,0},{4,6},{6,4},{8,10},{10,8},{12,14},{14,12},{16,18},{18,... | collective-permute-start | bytes 3538952 | tf_op jit(solution)/shard_map/ppermute | solution.py:383
  102.1 1.1 copy-start
  103.2 36.6 %copy-start.2 = (bf16[32,32,128]{2,1,0:T(8,128)(2,1)S(1)}, bf16[32,32,128]{2,1,0:T(8,128)(2,1)}, u32[]{:S(2)}) copy-start(bf16[32,32,128]{2,1,0:T(8,128)(2,1)} %param.14) | copy-start | bytes 786436
  106.7 16.4 %collective-permute-start.2 = (bf16[2,4,144,256]{3,2,1,0:T(8,128)(2,1)}, bf16[2,4,144,256]{3,2,1,0:T(8,128)(2,1)S(1)}, u32[]{:S(2)}, u32[]{:S(2)}) collective-permute-start(bf16[2,4,144,256]{3,2,1,0:T(8,128)(2,1)} %get-tuple-element.42), channel_id=1, source_target_pairs={{0,4},{2,6},{4,0},{6,2},{8,12},{10,14},{12,8},{14,10},{16,20},{18,... | collective-permute-start | bytes 1769480 | tf_op jit(solution)/shard_map/ppermute | solution.py:383
  107.3 1.0 copy-start.1
  111.8 23.3 %collective-permute-start.7 = (bf16[2,4,144,256]{3,2,1,0:T(8,128)(2,1)}, bf16[2,4,144,256]{3,2,1,0:T(8,128)(2,1)S(1)}, u32[]{:S(2)}, u32[]{:S(2)}) collective-permute-start(bf16[2,4,144,256]{3,2,1,0:T(8,128)(2,1)} %get-tuple-element.55), channel_id=1, source_target_pairs={{0,4},{2,6},{4,0},{6,2},{8,12},{10,14},{12,8},{14,10},{16,20},{18,... | collective-permute-start | bytes 1769480 | tf_op jit(solution)/shard_map/ppermute | solution.py:383
  123.1 0.8 copy-start.3
  126.4 19.3 %collective-permute-start.3 = (bf16[2,2,144,256]{3,2,1,0:T(8,128)(2,1)}, bf16[2,2,144,256]{3,2,1,0:T(8,128)(2,1)S(1)}, u32[]{:S(2)}, u32[]{:S(2)}) collective-permute-start(bf16[2,2,144,256]{3,2,1,0:T(8,128)(2,1)} %get-tuple-element.45), channel_id=1, source_target_pairs={{0,8},{2,10},{4,12},{6,14},{8,0},{10,2},{12,4},{14,6},{16,24},{18,... | collective-permute-start | bytes 884744 | tf_op jit(solution)/shard_map/ppermute | solution.py:383
  135.0 0.8 copy-start.4
  138.3 10.9 %collective-permute-start.8 = (bf16[2,2,144,256]{3,2,1,0:T(8,128)(2,1)}, bf16[2,2,144,256]{3,2,1,0:T(8,128)(2,1)S(1)}, u32[]{:S(2)}, u32[]{:S(2)}) collective-permute-start(bf16[2,2,144,256]{3,2,1,0:T(8,128)(2,1)} %get-tuple-element.58), channel_id=1, source_target_pairs={{0,8},{2,10},{4,12},{6,14},{8,0},{10,2},{12,4},{14,6},{16,24},{18,... | collective-permute-start | bytes 884744 | tf_op jit(solution)/shard_map/ppermute | solution.py:383
  145.6 0.7 copy-start.5
  148.3 12.5 %collective-permute-start.4 = (bf16[2,1,144,256]{3,2,1,0:T(8,128)(2,1)}, bf16[2,1,144,256]{3,2,1,0:T(8,128)(2,1)S(1)}, u32[]{:S(2)}, u32[]{:S(2)}) collective-permute-start(bf16[2,1,144,256]{3,2,1,0:T(8,128)(2,1)} %get-tuple-element.48), channel_id=1, source_target_pairs={{0,16},{2,18},{4,20},{6,22},{8,24},{10,26},{12,28},{14,30},{16,0},... | collective-permute-start | bytes 442376 | tf_op jit(solution)/shard_map/ppermute | solution.py:383
  149.2 0.7 copy-start.6
  151.9 12.4 %collective-permute-start.9 = (bf16[2,1,144,256]{3,2,1,0:T(8,128)(2,1)}, bf16[2,1,144,256]{3,2,1,0:T(8,128)(2,1)S(1)}, u32[]{:S(2)}, u32[]{:S(2)}) collective-permute-start(bf16[2,1,144,256]{3,2,1,0:T(8,128)(2,1)} %get-tuple-element.61), channel_id=1, source_target_pairs={{0,16},{2,18},{4,20},{6,22},{8,24},{10,26},{12,28},{14,30},{16,0},... | collective-permute-start | bytes 442376 | tf_op jit(solution)/shard_map/ppermute | solution.py:383
  160.9 0.7 copy-start.8
  164.3 0.7 copy-start.7
Sparse Core Ops, SparseCore 0:
  9.6 53.9 all-gather.2

commit v2 on v0

v2 whole, which is shorter than its diff:
```python
import functools

import jax
import jax.numpy as jnp
from jax import lax
from jax.experimental import pallas as pl
from jax.experimental.pallas import tpu as pltpu
from jax.sharding import PartitionSpec as P

HD = 128
PROMPTS = 2
CODE_BLOCKS = 16
CODE_TOP = 32000.0
STAT_ROWS = 16
EMPTY = -1e30
LOG2E = 1.4426950408889634
TO_LOG2 = HD ** (-0.5) * LOG2E
BIG = 60 * 1024 * 1024
ANY = pl.BlockSpec(memory_space=pl.ANY)


def encode(values):
    rows = values.shape[0]
    blocks = values.reshape(CODE_BLOCKS, rows // CODE_BLOCKS, HD)
    largest = jnp.maximum(jnp.max(jnp.abs(blocks), axis=1), 1e-30)
    exponent = jnp.floor(jnp.log(largest) * LOG2E) + 1.0
    factor = jnp.exp2(-exponent) * CODE_TOP
    codes = jnp.round(blocks * factor[:, None, :]).astype(jnp.int32).astype(jnp.int16)
    return codes.reshape(rows, HD), exponent.astype(jnp.int32).astype(jnp.int16)


def decode(codes, exponent):
    rows = codes.shape[0]
    factor = jnp.exp2(exponent.astype(jnp.int32).astype(jnp.float32)) * (1.0 / CODE_TOP)
    blocks = codes.astype(jnp.int32).astype(jnp.float32).reshape(CODE_BLOCKS, rows // CODE_BLOCKS, HD)
    return (blocks * factor[:, None, :]).reshape(rows, HD)


def project_kernel(plan, split, pieces, place_ref, x_hbm, wk_ref, wv_ref, *rest):
    count = sum(split - (kind == "own") for kind in plan) + 2 * plan.count("own")
    outs = rest[:count]
    x_ref, acc, sems = rest[count:]
    step = pl.program_id(0)
    rows = x_ref.shape[0]
    width = wk_ref.shape[1]
    part = rows // pieces

    def fetch(piece):
        window = pl.ds(piece * part, part)
        return pltpu.make_async_copy(x_hbm.at[window], x_ref.at[window], sems.at[piece])

    @pl.when(step == 0)
    def _():
        for piece in range(pieces):
            fetch(piece).start()

    for piece in range(pieces):

        @pl.when(step == 0)
        def _():
            fetch(piece).wait()

        window = pl.ds(piece * part, part)
        acc[window, :width] = jnp.dot(x_ref[window], wk_ref[...], preferred_element_type=jnp.float32)
        acc[window, width:] = jnp.dot(x_ref[window], wv_ref[...], preferred_element_type=jnp.float32)

    core = place_ref[0]
    index = 0
    for number, kind in enumerate(plan):
        here = list(outs[index : index + split + (kind == "own")])
        index += split + (kind == "own")

        @pl.when(step == number)
        def _():
            refs = list(here)
            for apart in range(split):
                lanes = pl.multiple_of((core ^ apart) * HD, HD)
                if kind == "own" and apart == 0:
                    refs.pop(0)[...] = acc[:, pl.ds(lanes, HD)]
                    refs.pop(0)[...] = acc[:, pl.ds(width + lanes, HD)]
                    continue
                ref = refs.pop(0)
                for half in range(2):
                    codes, exponent = encode(acc[:, pl.ds(half * width + lanes, HD)])
                    ref[:rows, half * HD : (half + 1) * HD] = codes
                    ref[rows:, half * HD : (half + 1) * HD] = exponent


def project(x, wk, wv, core, columns, plan, split):
    rows, depth = x.shape
    width = split * HD
    steps = len(plan)
    pieces = 2
    coded = jax.ShapeDtypeStruct((rows + CODE_BLOCKS, 2 * HD), jnp.int16)
    plain = jax.ShapeDtypeStruct((rows, HD), jnp.float32)
    shapes = []
    for kind in plan:
        shapes += ([plain, plain] if kind == "own" else [coded]) + [coded] * (split - 1)
    weight_spec = pl.BlockSpec((depth, width), lambda s, p: (0, p[1 + s]))
    place = jnp.stack([core] + columns).astype(jnp.int32)
    outs = pl.pallas_call(
        functools.partial(project_kernel, plan, split, pieces),
        out_shape=tuple(shapes),
        grid_spec=pltpu.PrefetchScalarGridSpec(
            num_scalar_prefetch=1,
            grid=(steps,),
            in_specs=[ANY, weight_spec, weight_spec],
            out_specs=tuple(pl.BlockSpec(shape.shape, lambda s, p: (0, 0)) for shape in shapes),
            scratch_shapes=[
                pltpu.VMEM((rows, depth), x.dtype),
                pltpu.VMEM((rows, 2 * width), jnp.float32),
                pltpu.SemaphoreType.DMA((pieces,)),
            ],
        ),
        compiler_params=pltpu.CompilerParams(vmem_limit_bytes=BIG),
        cost_estimate=pl.CostEstimate(
            flops=4 * rows * depth * width * steps,
            bytes_accessed=2 * rows * depth + steps * (4 * depth * width + 4 * rows * width),
            transcendentals=0,
        ),
        name="project",
    )(place, x, wk, wv)
    results = []
    index = 0
    for kind in plan:
        size = split + (kind == "own")
        results.append(list(outs[index : index + size]))
        index += size
    return results


def pack(context, logsum):
    high = logsum.astype(jnp.bfloat16).astype(jnp.float32)
    middle = (logsum - high).astype(jnp.bfloat16).astype(jnp.float32)
    low = logsum - high - middle
    line = lax.broadcasted_iota(jnp.int32, (STAT_ROWS, context.shape[1]), 0)
    stats = jnp.where(line == 0, high, jnp.where(line == 1, middle, jnp.where(line == 2, low, 0.0)))
    return context.astype(jnp.bfloat16), stats.astype(jnp.bfloat16)


def unpack(block):
    stats = block[HD:].astype(jnp.float32)
    return block[:HD].astype(jnp.float32), stats[0:1] + stats[1:2] + stats[2:3]


def blend(pieces):
    top = functools.reduce(jnp.maximum, [logsum for _, logsum in pieces])
    shares = [jnp.exp2(logsum - top) for _, logsum in pieces]
    total = functools.reduce(jnp.add, shares)
    inverse = 1.0 / total
    context = functools.reduce(
        jnp.add, [context * (share * inverse) for (context, _), share in zip(pieces, shares)]
    )
    return context, top + jnp.log(total) * LOG2E


def attend_kernel(layout, per, slots, keep, sends, order_ref, place_ref, own_key, own_value, cos_ref, sin_ref, q_ref, *rest):
    parts = sum(layout)
    received = list(rest[:parts])
    keep_ref, keep_log_ref = rest[parts : parts + 2]
    send_refs = rest[parts + 2 : parts + 2 + sends]
    key_scr, value_scr, score_scr, top_scr, context_scr, log_scr = rest[parts + 2 + sends :]
    rows = own_key.shape[0]
    blocks = len(layout)
    for block in range(blocks):
        here = [received.pop(0) for _ in range(layout[block])]
        for is_value in range(2):
            lanes = slice(is_value * HD, (is_value + 1) * HD)
            terms = [decode(part[:rows, lanes], part[rows:, lanes]) for part in here]
            if block == 0:
                terms = [(own_value if is_value else own_key)[...]] + terms
            whole = functools.reduce(jnp.add, terms)
            window = slice(block * rows, (block + 1) * rows)
            if is_value:
                value_scr[:HD, window] = jnp.transpose(whole).astype(jnp.bfloat16)
            else:
                whole = whole * cos_ref[window] + pltpu.roll(whole, HD // 2, 1) * sin_ref[window]
                key_scr[window] = whole.astype(jnp.bfloat16)
    value_scr[HD:] = jnp.ones((STAT_ROWS, blocks * rows), jnp.bfloat16)
    total_keys = blocks * rows
    tile = min(512, total_keys)

    def score(index, buffer):
        query = q_ref[order_ref[index]]
        tops = []
        for start in range(0, total_keys, tile):
            scores = jnp.dot(key_scr[start : start + tile], query, preferred_element_type=jnp.float32)
            score_scr[buffer, start : start + tile] = scores
            tops.append(jnp.max(scores, axis=0, keepdims=True))
        top = functools.reduce(jnp.maximum, tops) * TO_LOG2
        top_scr[buffer] = jnp.broadcast_to(top, top_scr.shape[1:])

    def weigh(index, buffer):
        top = top_scr[buffer][:1]
        summed = None
        for start in range(0, total_keys, tile):
            weights = jnp.exp2(score_scr[buffer, start : start + tile] * TO_LOG2 - top).astype(jnp.bfloat16)
            term = jnp.dot(value_scr[:, start : start + tile], weights, preferred_element_type=jnp.float32)
            summed = term if summed is None else summed + term
        total = summed[HD : HD + 1]
        context_scr[place_ref[index]] = summed[:HD] * (1.0 / total)
        log_scr[place_ref[index]] = jnp.broadcast_to(top + jnp.log(total) * LOG2E, log_scr.shape[1:])

    score(0, 0)

    @pl.loop(0, per // 2)
    def _(pair):
        score(2 * pair + 1, 1)
        weigh(2 * pair, 0)
        score(jnp.minimum(2 * pair + 2, per - 1), 0)
        weigh(2 * pair + 1, 1)

    @pl.loop(per, slots)
    def _(index):
        context_scr[place_ref[index]] = jnp.zeros(context_scr.shape[1:], jnp.float32)
        log_scr[place_ref[index]] = jnp.full(log_scr.shape[1:], EMPTY, jnp.float32)

    for slot in range(keep):
        keep_ref[slot] = context_scr[slot]
        keep_log_ref[slot] = log_scr[slot]
    for number, send_ref in enumerate(send_refs):
        for slot in range(keep):
            where = (number + 1) * keep + slot
            context, stats = pack(context_scr[where], log_scr[where][:1])
            send_ref[slot, :HD] = context
            send_ref[slot, HD:] = stats


def attend(order, place, own, cosine, sine, q_all, received, head, per, keep):
    rows = own[0].shape[0]
    slots, _, wide = q_all.shape
    blocks = len(received)
    layout = [len(parts) for parts in received]
    flat = [part for parts in received for part in parts]
    sends = slots // keep - 1

    def whole(shape):
        return pl.BlockSpec(shape, lambda i, a, b: (0,) * len(shape))

    shapes = [
        jax.ShapeDtypeStruct((keep, HD, wide), jnp.float32),
        jax.ShapeDtypeStruct((keep, 8, wide), jnp.float32),
    ] + [jax.ShapeDtypeStruct((keep, HD + STAT_ROWS, wide), jnp.bfloat16)] * sends
    return pl.pallas_call(
        functools.partial(attend_kernel, layout, per, slots, keep, sends),
        out_shape=tuple(shapes),
        grid_spec=pltpu.PrefetchScalarGridSpec(
            num_scalar_prefetch=2,
            grid=(1,),
            in_specs=[
                whole((rows, HD)),
                whole((rows, HD)),
                whole((blocks * rows, HD)),
                whole((blocks * rows, HD)),
                pl.BlockSpec((slots, HD, wide), lambda i, a, b: (0, head, 0)),
            ]
            + [whole(part.shape) for part in flat],
            out_specs=tuple(whole(shape.shape) for shape in shapes),
            scratch_shapes=[
                pltpu.VMEM((blocks * rows, HD), jnp.bfloat16),
                pltpu.VMEM((HD + STAT_ROWS, blocks * rows), jnp.bfloat16),
                pltpu.VMEM((2, blocks * rows, wide), jnp.float32),
                pltpu.VMEM((2, 8, wide), jnp.float32),
                pltpu.VMEM((slots, HD, wide), jnp.float32),
                pltpu.VMEM((slots, 8, wide), jnp.float32),
            ],
        ),
        compiler_params=pltpu.CompilerParams(vmem_limit_bytes=BIG),
        cost_estimate=pl.CostEstimate(
            flops=8 * per * blocks * rows * wide * HD,
            bytes_accessed=blocks * rows * HD * 16 + slots * HD * wide * 4,
            transcendentals=per * blocks * rows * wide,
        ),
        name="attend",
    )(order, place, *own, cosine, sine, q_all, *flat)


def gather_kernel(parts, keep_ref, keep_log_ref, *rest):
    received = rest[:parts]
    context_ref, log_ref = rest[parts : parts + 2]
    sends = rest[parts + 2 :]
    for slot in range(keep_ref.shape[0]):
        pieces = [(keep_ref[slot], keep_log_ref[slot][:1])] + [unpack(part[slot]) for part in received]
        context, logsum = blend(pieces)
        if slot == 0:
            context_ref[...] = context
            log_ref[...] = jnp.broadcast_to(logsum, log_ref.shape)
        else:
            packed, stats = pack(context, logsum)
            sends[slot - 1][:HD] = packed
            sends[slot - 1][HD:] = stats


def gather(keep, keep_log, received):
    count, _, wide = keep.shape
    shapes = [
        jax.ShapeDtypeStruct((HD, wide), jnp.float32),
        jax.ShapeDtypeStruct((8, wide), jnp.float32),
    ] + [jax.ShapeDtypeStruct((HD + STAT_ROWS, wide), jnp.bfloat16)] * (count - 1)
    outs = pl.pallas_call(
        functools.partial(gather_kernel, len(received)),
        out_shape=tuple(shapes),
        compiler_params=pltpu.CompilerParams(vmem_limit_bytes=BIG),
        cost_estimate=pl.CostEstimate(
            flops=4 * (len(received) + 1) * count * HD * wide,
            bytes_accessed=count * HD * wide * (6 + 2 * len(received)),
            transcendentals=0,
        ),
        name="gather",
    )(keep, keep_log, *received)
    return outs[0], outs[1], list(outs[2:])


def finish_kernel(split, context_ref, log_ref, *rest):
    received = rest[: 2 * split - 1]
    context_out, log_out = rest[2 * split - 1 :]
    for apart in range(split):
        pieces = []
        if apart == 0:
            pieces.append((context_ref[...], log_ref[:1]))
        else:
            pieces.append(unpack(received[apart - 1][...]))
        pieces.append(unpack(received[split - 1 + apart][...]))
        context, logsum = blend(pieces)
        context_out[apart] = jnp.transpose(context)
        log_out[apart] = jnp.broadcast_to(logsum, log_out.shape[1:])


def finish(context, log, received, split):
    wide = context.shape[1]
    return pl.pallas_call(
        functools.partial(finish_kernel, split),
        out_shape=(
            jax.ShapeDtypeStruct((split, wide, HD), jnp.float32),
            jax.ShapeDtypeStruct((split, 8, wide), jnp.float32),
        ),
        compiler_params=pltpu.CompilerParams(vmem_limit_bytes=BIG),
        cost_estimate=pl.CostEstimate(
            flops=8 * split * HD * wide, bytes_accessed=16 * split * HD * wide, transcendentals=0
        ),
        name="finish",
    )(context, log, *received)


def tables(starts, rows):
    half_width = HD // 2
    inverse_freq = 500000.0 ** (-(jnp.arange(half_width, dtype=jnp.float32) * 2.0 / HD))
    positions = (starts[:, None] + jnp.arange(rows, dtype=jnp.int32)[None, :]).reshape(-1)
    angles = positions.astype(jnp.float32)[:, None] * inverse_freq[None, :]
    cosine = jnp.cos(angles)
    sine = jnp.sin(angles)
    return jnp.concatenate([cosine, cosine], 1), jnp.concatenate([-sine, sine], 1)


def on_device(
    prefill_states,
    key_weight,
    value_weight,
    offsets,
    matching,
    queries,
    cache_keys,
    cache_values,
    cache_lengths,
):
    tp = lax.axis_size("tp")
    groups = lax.axis_size("grp")
    me = lax.axis_index("grp").astype(jnp.int32)
    rank = lax.axis_index("tp").astype(jnp.int32)
    block_len = prefill_states.shape[0]
    kv_local = key_weight.shape[1] // HD // tp
    row_count = queries.shape[0]
    group_size = queries.shape[1] // kv_local
    wide = row_count * group_size
    split = 2 if kv_local % 2 == 0 else 1
    chunks = kv_local // split
    per = groups // PROMPTS
    homes = per // split
    keep = PROMPTS * split
    core = me % split
    spot = (me // split) % homes
    side = me // per

    grouped = queries.reshape(row_count, kv_local, group_size, HD)
    turned = grouped.reshape(row_count, chunks, split, group_size, HD).transpose(2, 1, 4, 0, 3)
    turned = turned.reshape(split, chunks * HD, wide)
    line = jnp.arange(STAT_ROWS, dtype=jnp.int32)[None, :, None]
    tag = jnp.where(line == 0, matching[0], offsets[0]).astype(jnp.bfloat16)
    turned = jnp.concatenate([turned, jnp.broadcast_to(tag, (split, STAT_ROWS, wide))], 1)
    sorted_queries = [lax.dynamic_index_in_dim(turned, core ^ apart, 0, False) for apart in range(split)]
    own_queries = [sorted_queries[0]] + [
        lax.ppermute(sorted_queries[apart], "grp", [(i, i ^ apart) for i in range(groups)])
        for apart in range(1, split)
    ]
    def exchange(array, shift, apart):
        pairs = [
            (g * tp + t, (g ^ apart) * tp + (t + shift) % tp) for g in range(groups) for t in range(tp)
        ]
        return lax.ppermute(array, ("grp", "tp"), pairs)

    received = [[[] for _ in range(split)] for _ in range(chunks)]
    own = [None] * chunks

    def column(shift, chunk):
        return ((rank + shift) % tp) * chunks + chunk

    def run(jobs, core):
        results = project(
            prefill_states,
            key_weight,
            value_weight,
            core,
            [column(shift, chunk) for shift, chunk in jobs],
            ["own" if shift == 0 else "send" for shift, _ in jobs],
            split,
        )
        for (shift, chunk), outs in zip(jobs, results):
            if shift == 0:
                own[chunk] = outs[:2]
                outs = [None] + outs[2:]
            for apart in range(split):
                if outs[apart] is not None:
                    received[chunk][apart].append(exchange(outs[apart], shift, apart))

    jobs = [(shift, chunk) for chunk in range(chunks) for shift in range(1, tp)]
    run(jobs[:1], core)
    own_queries, later_core = lax.optimization_barrier((own_queries, core))
    members = [[chip * split + c for chip in range(groups // split)] for c in range(split)]
    q_all = lax.all_gather(jnp.stack(own_queries), "grp", axis_index_groups=members)
    q_all = q_all.reshape(groups, chunks * HD + STAT_ROWS, wide)
    wanted = q_all[:, chunks * HD, 0].astype(jnp.int32)
    starts = jnp.stack([own[chunks * HD + 1, 0] for own in own_queries]).astype(jnp.int32)
    run(jobs[1:] + [(0, chunk) for chunk in range(chunks)], later_core)

    cosine, sine = tables(starts, block_len)
    mine = (wanted == side).astype(jnp.int32)
    before = jnp.cumsum(mine)
    names = jnp.arange(groups, dtype=jnp.int32)
    target = jnp.where(mine == 1, before - 1, per + names - before)
    order = jnp.sum(jnp.where(target[None, :] == names[:, None], names[None, :], 0), 1).astype(jnp.int32)
    away = ((order // split) % homes) ^ spot
    place = (away * PROMPTS + ((order // per) ^ side)) * split + order % split

    grouped, own[-1] = lax.optimization_barrier((grouped, own[-1]))
    score_scale = HD ** (-0.5)
    cache_len = cache_keys.shape[2]
    cache_scores = (
        jnp.einsum("rkgd,rktd->rkgt", grouped, cache_keys, preferred_element_type=jnp.float32)
        * score_scale
    )
    alive = (jnp.arange(cache_len, dtype=jnp.int32)[None, :] < cache_lengths[:, None])[:, None, None, :]
    cache_scores = jnp.where(alive, cache_scores, EMPTY)
    cache_top = cache_scores.max(-1)
    cache_weights = jnp.where(alive, jnp.exp(cache_scores - cache_top[..., None]), 0.0)
    cache_total = cache_weights.sum(-1)
    cache_sum = jnp.einsum(
        "rkgt,rktd->rkgd",
        cache_weights.astype(jnp.bfloat16),
        cache_values,
        preferred_element_type=jnp.float32,
    )
    cache_sum, cache_total, cache_top, order, place = lax.optimization_barrier(
        (cache_sum, cache_total, cache_top, order, place)
    )

    def partner(i, side_apart, apart):
        return (i + side_apart * per) % groups ^ apart

    contexts = []
    logs = []
    for chunk in range(chunks):
        outs = attend(order, place, own[chunk], cosine, sine, q_all, received[chunk], chunk, per, keep)
        arrived = [
            lax.ppermute(outs[2 + far - 1], "grp", [(i, i ^ (far * split)) for i in range(groups)])
            for far in range(1, homes)
        ]
        context, log, sends = gather(outs[0], outs[1], arrived)
        final = [
            lax.ppermute(
                sends[number - 1],
                "grp",
                [(i, partner(i, number // split, number % split)) for i in range(groups)],
            )
            for number in range(1, keep)
        ]
        context, log = finish(context, log, final, split)
        contexts.append(context)
        logs.append(log[:, 0])
    contexts = jnp.stack(contexts)
    logs = jnp.stack(logs)
    if split == 2:
        contexts = jnp.where(core == 0, contexts, contexts[:, ::-1])
        logs = jnp.where(core == 0, logs, logs[:, ::-1])
    prompt_context = contexts.reshape(kv_local, row_count, group_size, HD).transpose(1, 0, 2, 3)
    prompt_log = logs.reshape(kv_local, row_count, group_size).transpose(1, 0, 2)
    cache_log = cache_top * LOG2E
    top = jnp.maximum(prompt_log, cache_log)
    prompt_share = jnp.exp2(prompt_log - top)
    cache_share = jnp.exp2(cache_log - top)
    total = prompt_share + cache_share * cache_total
    context = (prompt_context * prompt_share[..., None] + cache_sum * cache_share[..., None]) / total[..., None]
    return context.reshape(row_count, kv_local * group_size, HD).astype(jnp.bfloat16)


def solution(mesh):
    placed = (
        P("grp", "tp"),
        P("tp", None),
        P("tp", None),
        P("grp"),
        P("grp"),
        P("grp", "tp", None),
        P("grp", "tp", None, None),
        P("grp", "tp", None, None),
        P("grp"),
    )
    return jax.shard_map(
        on_device, mesh=mesh, in_specs=placed, out_specs=P("grp", "tp", None), check_vma=False
    )
```

time: 452 us -> 150 us (0.33)
  waiting for transfers between devices: 287 us -> 24.5 us
  matrix products: 99.1 us -> 7.26 us
  Pallas kernels: 0 us -> 63.8 us
  other arithmetic: 36.9 us -> 14.1 us
  starting transfers between devices: 0.27 us -> 17.2 us
  local copies, waits for them, and re-layouts: 14.4 us -> 8.08 us
    all_gather x2 -> x1, waiting for transfers between devices: 187 us -> 9.86 us  [on_device(): lax.all_gather(jnp.stack(own_queries), 'grp', axis_index_groups=members)]
    reduce_scatter x1 -> x0, waiting for transfers between devices: 99.3 us -> none  [on_device(): lax.psum_scatter(stacked.transpose(1, 0, 2), 'tp', scatter_dimension=0, t...]
    dot_general x4 -> x0, matrix products: 88.5 us -> none  [the longest x1 29.9 us: on_device(): jnp.einsum('rkgd,knd->rkgn', grouped, piece_keys, preferred_element_type=...]
    pallas_call x0 -> x8, Pallas kernels: none -> 63.8 us  [the longest x2 34.8 us: project(): pl.pallas_call(functools.partial(project_kernel, plan, split, pieces), ou...]
    reduce_sum x2, other arithmetic: 23.2 us -> 0.6 us  [the longest x1 0.48 us: on_device(): cache_total = cache_weights.sum(-1)]
    ppermute x0 -> x19, starting transfers between devices: none -> 17.2 us  [the longest x6 6.98 us: on_device(): lax.ppermute(outs[2 + far - 1], 'grp', [(i, i ^ far * split) for i in ran...]
    ppermute x0 -> x19, waiting for transfers between devices: none -> 14.6 us  [the longest x6 10.8 us: on_device(): lax.ppermute(outs[2 + far - 1], 'grp', [(i, i ^ far * split) for i in ran...]
    reshape x2, local copies, waits for them, and re-layouts: 10.6 us -> 0.26 us  [the longest x1 0.17 us: on_device(): turned = turned.reshape(split, chunks * HD, wide)]
  transfers between devices with their start and end apart: 3 -> 20, of which waited for: 3 -> 6; matrix products, arithmetic and copies ran while one was open for 15% -> 14% of each run, Pallas kernels for 0% -> 41%
where the time goes in v2:
time: 150 us
  Pallas kernels  63.8 us (43%)
  waiting for transfers between devices  24.5 us (16%)
  starting transfers between devices  17.2 us (11%)
  between operations  15 us (10%)
  other arithmetic  14.1 us (9%)
  local copies, waits for them, and re-layouts  8.08 us (5%)
  matrix products  7.26 us (5%)
    pallas_call x2, Pallas kernels, project(): pl.pallas_call(functools.partial(project_kernel, plan, split, pieces), ou...  34.8 us
    pallas_call x2, Pallas kernels, attend(): pl.pallas_call(functools.partial(attend_kernel, layout, per, slots, keep,...  20.8 us
    ppermute x6, waiting for transfers between devices, on_device(): lax.ppermute(outs[2 + far - 1], 'grp', [(i, i ^ far * split) for i in ran...  10.8 us
    all_gather x1, waiting for transfers between devices, on_device(): lax.all_gather(jnp.stack(own_queries), 'grp', axis_index_groups=members)  9.86 us
    ppermute x6, starting transfers between devices, on_device(): lax.ppermute(outs[2 + far - 1], 'grp', [(i, i ^ far * split) for i in ran...  6.98 us
    dot_general x1, matrix products, on_device(): jnp.einsum('rkgd,rktd->rkgt', grouped, cache_keys, preferred_element_type...  6 us
    ppermute x6, starting transfers between devices, exchange(): return lax.ppermute(array, ('grp', 'tp'), pairs)  5.05 us
    ppermute x6, starting transfers between devices, on_device(): lax.ppermute(sends[number - 1], 'grp', [(i, partner(i, number // split, n...  4.67 us
  transfers between devices with their start and end apart: 20, of which 6 were waited for; matrix products, arithmetic and copies ran while one was open for 14% of the time, Pallas kernels for 41%

profile of v2, /device:TPU:0, one launch (start us, length us, event | category | flops | bytes accessed | tf_op | source)
XLA Modules:
  0.0 150.0 jit_solution(17844204740887102687)
XLA Ops:
  7.8 1.2 copy.52
  10.6 11.3 %project.3 = (s16[1040,256]{1,0:T(8,128)(2,1)}, s16[1040,256]{1,0:T(8,128)(2,1)}) custom-call(s32[2]{0:T(128)} %pad_add_fusion.1.place_ref, bf16[1024,4096]{1,0:T(8,128)(2,1)} %x_hbm.3, bf16[4096,1024]{1,0:T(8,128)(2,1)} %wk_ref.3, bf16[4096,1024]{1,0:T(8,128)(2,1)} %wv_ref.3), custom_call_target="tpu_custom_call" | custom-call | flops 4294967296 | bytes 13631488 | tf_op jit(solution)/shard_map/project/pallas_call | solution.py:101
  22.0 2.6 %collective-permute-start.1 = (s16[1040,256]{1,0:T(8,128)(2,1)}, s16[1040,256]{1,0:T(8,128)(2,1)S(1)}, u32[]{:S(2)}, u32[]{:S(2)}) collective-permute-start(s16[1040,256]{1,0:T(8,128)(2,1)} %get-tuple-element.60), channel_id=1, source_target_pairs={{0,1},{1,0},{2,3},{3,2},{4,5},{5,4},{6,7},{7,6},{8,9},{9,8},{10,11... | collective-permute-start | bytes 1597448 | tf_op jit(solution)/shard_map/ppermute | solution.py:399
  26.8 1.3 maximum_convert_fusion
  28.9 23.4 %project.2 = (s16[1040,256]{1,0:T(8,128)(2,1)}, s16[1040,256]{1,0:T(8,128)(2,1)}, f32[1024,128]{1,0:T(8,128)}, f32[1024,128]{1,0:T(8,128)}, s16[1040,256]{1,0:T(...) custom-call(s32[4]{0:T(128)} %pad_add_fusion.place_ref, ...), custom_call_target="tpu_custom_call" | custom-call | flops 12884901888 | bytes 24117248 | tf_op jit(solution)/shard_map/project/pallas_call | solution.py:101
  52.3 1.8 %collective-permute-start.10 = (s16[1040,256]{1,0:T(8,128)(2,1)}, s16[1040,256]{1,0:T(8,128)(2,1)S(1)}, u32[]{:S(2)}, u32[]{:S(2)}) collective-permute-start(s16[1040,256]{1,0:T(8,128)(2,1)} %get-tuple-element.76), channel_id=1, source_target_pairs={{0,1},{1,0},{2,3},{3,2},{4,5},{5,4},{6,7},{7,6},{8,9},{9,8},{10,11... | collective-permute-start | bytes 1597448 | tf_op jit(solution)/shard_map/ppermute | solution.py:399
  54.5 6.0 %fusion.26 = (f32[32,4,8]{2,1,0:T(4,128)S(1)}, f32[32,4,8,256]{3,2,1,0:T(8,128)S(1)}) fusion(bf16[32,4,8,128]{3,2,1,0:T(8,128)(2,1)S(1)} %bitcast.60, bf16[32,4,256,128]{3,2,1,0:T(8,128)(2,1)} %param.15, pred[32,256]{1,0:T(8,128)(4,1)S(1)} %iota_compare_fusion), kind=kOutput, calls=%fused_computation.69 | convolution fusion | flops 67894272 | bytes 9711616 | tf_op jit(solution)/shard_map/rkgd,rktd->rkgt/dot_general | solution.py:448
  61.0 3.7 %fusion.11 = (f32[2048,64]{1,0:T(8,128)S(1)}, f32[2048,64]{1,0:T(8,128)S(1)}, f32[2048,64]{1,0:T(8,128)S(1)}) fusion(f32[64]{0:T(128)S(1)} %negate_power_fusion, f32[2048]{0:T(1024)S(1)} %bitcast.67), kind=kLoop, calls=%fused_computation.20 | loop fusion | flops 262144 | bytes 1581312 | tf_op jit(solution)/shard_map/neg | solution.py:352
  64.8 1.9 %pad_maximum_fusion = (f32[2048,128]{1,0:T(8,128)}, f32[2048,128]{1,0:T(8,128)}) fusion(f32[2048,64]{1,0:T(8,128)S(1)} %get-tuple-element.104, f32[2048,64]{1,0:T(8,128)S(1)} %get-tuple-element.103, f32[2048,64]{1,0:T(8,128)S(1)} %get-tuple-element.102), kind=kLoop, calls=%fused_computation.4 | loop fusion | flops 524288 | bytes 3670016 | tf_op jit(solution)/shard_map/concatenate | solution.py:352
  66.7 1.3 fusion.3
  68.0 9.9 %all-gather.3.cloned.1.call-done.q_ref = bf16[16,272,256]{2,1,0:T(8,128)(2,1)} async-done(((bf16[2,272,256]{2,1,0:T(8,128)(2,1)}), bf16[16,272,256]{2,1,0:T(8,128)(2,1)}) %all-gather.3.cloned.1.call-update) | async-done | bytes 2228240 | tf_op jit(solution)/shard_map/all_gather | solution.py:429
  77.8 1.1 compare_reduce_fusion
  80.2 10.3 %attend.3 = (f32[4,128,256]{2,1,0:T(8,128)}, f32[4,8,256]{2,1,0:T(8,128)}, bf16[4,144,256]{2,1,0:T(8,128)(2,1)}, bf16[4,144,256]{2,1,0:T(8,128)(2,1)}, bf16[4,144,256]{2,1,0:T(8,128)(2,1)}) custom-call(s32[16]{0:T(128)} %copy-done.14, s32[16]{0:T(128)} %fusion.17.place_ref, f32[1024,128]{1,0:T(8,128)} %get-tuple-element.74.own_key, ...), custom_call_target="tpu_custom_call" | custom-call | flops 4294967296 | bytes 6291456 | tf_op jit(solution)/shard_map/attend/pallas_call | solution.py:244
  91.0 1.5 collective-permute-start.14
  92.5 1.5 collective-permute-start.15
  94.0 0.8 copy-done.16
  94.8 10.5 %attend.2 = (f32[4,128,256]{2,1,0:T(8,128)}, f32[4,8,256]{2,1,0:T(8,128)}, bf16[4,144,256]{2,1,0:T(8,128)(2,1)}, bf16[4,144,256]{2,1,0:T(8,128)(2,1)}, bf16[4,144,256]{2,1,0:T(8,128)(2,1)}) custom-call(s32[16]{0:T(128)} %copy-done.14, s32[16]{0:T(128)} %fusion.17.place_ref, f32[1024,128]{1,0:T(8,128)} %get-tuple-element.58.own_key, ...), custom_call_target="tpu_custom_call" | custom-call | flops 4294967296 | bytes 6291456 | tf_op jit(solution)/shard_map/attend/pallas_call | solution.py:244
  105.8 1.5 collective-permute-start.5
  107.3 1.5 collective-permute-start.6
  109.6 2.2 %gather.3 = (f32[128,256]{1,0:T(8,128)}, f32[8,256]{1,0:T(8,128)}, bf16[144,256]{1,0:T(8,128)(2,1)}, bf16[144,256]{1,0:T(8,128)(2,1)}, bf16[144,256]{1,0:T(8,128)(2,1)}) custom-call(f32[4,128,256]{2,1,0:T(8,128)} %get-tuple-element.79.keep_ref, f32[4,8,256]{2,1,0:T(8,128)} %get-tuple-element.80.keep_log_ref, bf16[4,144,256]{2,1,0:T(8,128)(2,1)} %copy-done.1, ...), custom_call_target="tpu_custom_call" | custom-call | flops 2097152 | bytes 1572864 | tf_op jit(solution)/shard_map/gather/pallas_call | solution.py:300
  111.8 1.8 %collective-permute-start.17 = (bf16[144,256]{1,0:T(8,128)(2,1)}, bf16[144,256]{1,0:T(8,128)(2,1)S(1)}, u32[]{:S(2)}, u32[]{:S(2)}) collective-permute-start(bf16[144,256]{1,0:T(8,128)(2,1)} %get-tuple-element.87), channel_id=1, source_target_pairs={{0,16},{2,18},{4,20},{6,22},{8,24},{10,26},{12,28},{14,30},{16,0},... | collective-permute-start | bytes 221192 | tf_op jit(solution)/shard_map/ppermute | solution.py:479
  113.7 0.9 collective-permute-done.4.rest_0_
  114.6 1.4 collective-permute-done.5.rest_1_
  115.9 8.5 %collective-permute-done.6.rest_2_ = bf16[4,144,256]{2,1,0:T(8,128)(2,1)S(1)} collective-permute-done((bf16[4,144,256]{2,1,0:T(8,128)(2,1)}, bf16[4,144,256]{2,1,0:T(8,128)(2,1)S(1)}, u32[]{:S(2)}, u32[]{:S(2)}) %collective-permute-start.6) | collective-permute-done | bytes 294944 | tf_op jit(solution)/shard_map/ppermute | solution.py:474
  125.2 2.2 %gather.2 = (f32[128,256]{1,0:T(8,128)}, f32[8,256]{1,0:T(8,128)}, bf16[144,256]{1,0:T(8,128)(2,1)}, bf16[144,256]{1,0:T(8,128)(2,1)}, bf16[144,256]{1,0:T(8,128)(2,1)}) custom-call(f32[4,128,256]{2,1,0:T(8,128)} %get-tuple-element.63.keep_ref, f32[4,8,256]{2,1,0:T(8,128)} %get-tuple-element.64.keep_log_ref, bf16[4,144,256]{2,1,0:T(8,128)(2,1)} %copy-done.2, ...), custom_call_target="tpu_custom_call" | custom-call | flops 2097152 | bytes 1572864 | tf_op jit(solution)/shard_map/gather/pallas_call | solution.py:300
  127.7 2.5 %collective-permute-start.9 = (bf16[144,256]{1,0:T(8,128)(2,1)}, bf16[144,256]{1,0:T(8,128)(2,1)S(1)}, u32[]{:S(2)}, u32[]{:S(2)}) collective-permute-start(bf16[144,256]{1,0:T(8,128)(2,1)} %get-tuple-element.72), channel_id=1, source_target_pairs={{0,18},{2,16},{4,22},{6,20},{8,26},{10,24},{12,30},{14,28},{16,2},... | collective-permute-start | bytes 221192 | tf_op jit(solution)/shard_map/ppermute | solution.py:479
  130.9 1.9 %finish.3 = (f32[2,256,128]{2,1,0:T(8,128)}, f32[2,8,256]{2,1,0:T(8,128)}) custom-call(f32[128,256]{1,0:T(8,128)} %get-tuple-element.84.context_ref, f32[8,256]{1,0:T(8,128)} %get-tuple-element.85.log_ref, bf16[144,256]{1,0:T(8,128)(2,1)} %copy-done.7, bf16[144,256]{1,0:T(8,128)(2,1)} %copy-done.8, bf16[144,256]{1,0:T(8,128)(2,1)} %copy-done.9), custom_call_target="tpu_custom_call" | custom-call | flops 524288 | bytes 1048576 | tf_op jit(solution)/shard_map/finish/pallas_call | solution.py:331
  133.5 2.3 %collective-permute-done.8.rest_1_ = bf16[144,256]{1,0:T(8,128)(2,1)S(1)} collective-permute-done((bf16[144,256]{1,0:T(8,128)(2,1)}, bf16[144,256]{1,0:T(8,128)(2,1)S(1)}, u32[]{:S(2)}, u32[]{:S(2)}) %collective-permute-start.8) | collective-permute-done | bytes 73760 | tf_op jit(solution)/shard_map/ppermute | solution.py:479
  135.8 1.5 collective-permute-done.9.rest_2_
  137.9 1.9 %finish.2 = (f32[2,256,128]{2,1,0:T(8,128)}, f32[2,8,256]{2,1,0:T(8,128)}) custom-call(f32[128,256]{1,0:T(8,128)} %get-tuple-element.68.context_ref, f32[8,256]{1,0:T(8,128)} %get-tuple-element.69.log_ref, bf16[144,256]{1,0:T(8,128)(2,1)} %copy-done.10, bf16[144,256]{1,0:T(8,128)(2,1)} %copy-done.11, bf16[144,256]{1,0:T(8,128)(2,1)} %copy-done.12), custom_call_target="tpu_custom_call" | custom-call | flops 524288 | bytes 1048576 | tf_op jit(solution)/shard_map/finish/pallas_call | solution.py:331
  140.6 1.1 pad_maximum_fusion.2
  141.9 1.2 fusion.12
  (99 shorter events, 12.5 us)
Async XLA Ops:
  6.5 71.3 %all-gather.3.cloned.1.call-start = ((), (), s32[]{:S(2)}) async-start(), calls=%async_computation | async-start | bytes 2506752 | tf_op jit(solution)/shard_map/all_gather | solution.py:429
  9.5 15.4 %collective-permute-start = (bf16[272,256]{1,0:T(8,128)(2,1)S(1)}, bf16[272,256]{1,0:T(8,128)(2,1)S(1)}, u32[]{:S(2)}, u32[]{:S(2)}) collective-permute-start(bf16[272,256]{1,0:T(8,128)(2,1)S(1)} %bitcast.66), channel_id=1, source_target_pairs={{0,2},{2,0},{4,6},{6,4},{8,10},{10,8},{12,14},{14,12},{16,18},{18,... | collective-permute-start | bytes 417800 | tf_op jit(solution)/shard_map/ppermute | solution.py:392
  10.6 15.0 %copy-start.13 = (s32[32]{0:T(128)S(1)}, s32[32]{0:T(128)}, u32[]{:S(2)}) copy-start(s32[32]{0:T(128)} %param.17) | copy-start | bytes 388
  22.0 70.5 %collective-permute-start.1 = (s16[1040,256]{1,0:T(8,128)(2,1)}, s16[1040,256]{1,0:T(8,128)(2,1)S(1)}, u32[]{:S(2)}, u32[]{:S(2)}) collective-permute-start(s16[1040,256]{1,0:T(8,128)(2,1)} %get-tuple-element.60), channel_id=1, source_target_pairs={{0,1},{1,0},{2,3},{3,2},{4,5},{5,4},{6,7},{7,6},{8,9},{9,8},{10,11... | collective-permute-start | bytes 1597448 | tf_op jit(solution)/shard_map/ppermute | solution.py:399
  24.6 69.4 %collective-permute-start.2 = (s16[1040,256]{1,0:T(8,128)(2,1)}, s16[1040,256]{1,0:T(8,128)(2,1)S(1)}, u32[]{:S(2)}, u32[]{:S(2)}) collective-permute-start(s16[1040,256]{1,0:T(8,128)(2,1)} %get-tuple-element.61), channel_id=1, source_target_pairs={{0,3},{1,2},{2,1},{3,0},{4,7},{5,6},{6,5},{7,4},{8,11},{9,10},{10,... | collective-permute-start | bytes 1597448 | tf_op jit(solution)/shard_map/ppermute | solution.py:399
  28.9 25.6 %copy-start = (bf16[32,32,128]{2,1,0:T(8,128)(2,1)S(1)}, bf16[32,32,128]{2,1,0:T(8,128)(2,1)}, u32[]{:S(2)}) copy-start(bf16[32,32,128]{2,1,0:T(8,128)(2,1)} %param.14) | copy-start | bytes 786436
  52.3 27.0 %collective-permute-start.10 = (s16[1040,256]{1,0:T(8,128)(2,1)}, s16[1040,256]{1,0:T(8,128)(2,1)S(1)}, u32[]{:S(2)}, u32[]{:S(2)}) collective-permute-start(s16[1040,256]{1,0:T(8,128)(2,1)} %get-tuple-element.76), channel_id=1, source_target_pairs={{0,1},{1,0},{2,3},{3,2},{4,5},{5,4},{6,7},{7,6},{8,9},{9,8},{10,11... | collective-permute-start | bytes 1597448 | tf_op jit(solution)/shard_map/ppermute | solution.py:399
  54.1 25.9 %collective-permute-start.11 = (s16[1040,256]{1,0:T(8,128)(2,1)}, s16[1040,256]{1,0:T(8,128)(2,1)}, u32[]{:S(2)}, u32[]{:S(2)}) collective-permute-start(s16[1040,256]{1,0:T(8,128)(2,1)} %get-tuple-element.77), channel_id=1, source_target_pairs={{0,3},{1,2},{2,1},{3,0},{4,7},{5,6},{6,5},{7,4},{8,11},{9,10},{10,... | collective-permute-start | bytes 1597448 | tf_op jit(solution)/shard_map/ppermute | solution.py:399
  54.1 12.6 %slice-start = ((s8[8388608]{0:T(1024)(128)(4,1)}), s8[4194304]{0:T(1024)(128)(4,1)S(1)}, s32[]{:S(2)}) async-start(s8[8388608]{0:T(1024)(128)(4,1)} %bitcast.56), calls=%async_computation.1 | async-start | bytes 8388608
  54.1 12.6 %slice-start.1 = ((s8[8388608]{0:T(1024)(128)(4,1)}), s8[4194304]{0:T(1024)(128)(4,1)S(1)}, s32[]{:S(2)}) async-start(s8[8388608]{0:T(1024)(128)(4,1)} %bitcast.56), calls=%async_computation.2 | async-start | bytes 8388608
  54.1 25.9 %collective-permute-start.12 = (s16[1040,256]{1,0:T(8,128)(2,1)}, s16[1040,256]{1,0:T(8,128)(2,1)}, u32[]{:S(2)}, u32[]{:S(2)}) collective-permute-start(s16[1040,256]{1,0:T(8,128)(2,1)} %get-tuple-element.78), channel_id=1, source_target_pairs={{0,2},{1,3},{2,0},{3,1},{4,6},{5,7},{6,4},{7,5},{8,10},{9,11},{10,... | collective-permute-start | bytes 1597448 | tf_op jit(solution)/shard_map/ppermute | solution.py:399
  64.8 14.5 %copy-start.17 = (s16[1040,256]{1,0:T(8,128)(2,1)S(1)}, s16[1040,256]{1,0:T(8,128)(2,1)}, u32[]{:S(2)}) copy-start(s16[1040,256]{1,0:T(8,128)(2,1)} %get-tuple-element.62) | copy-start | bytes 1597444
  79.3 14.6 %collective-permute-start.3 = (s16[1040,256]{1,0:T(8,128)(2,1)S(1)}, s16[1040,256]{1,0:T(8,128)(2,1)}, u32[]{:S(2)}, u32[]{:S(2)}) collective-permute-start(s16[1040,256]{1,0:T(8,128)(2,1)S(1)} %copy-done.17), channel_id=1, source_target_pairs={{0,2},{1,3},{2,0},{3,1},{4,6},{5,7},{6,4},{7,5},{8,10},{9,11},{10,... | collective-permute-start | bytes 1597448 | tf_op jit(solution)/shard_map/ppermute | solution.py:399
  90.4 16.8 %collective-permute-start.13 = (bf16[4,144,256]{2,1,0:T(8,128)(2,1)}, bf16[4,144,256]{2,1,0:T(8,128)(2,1)S(1)}, u32[]{:S(2)}, u32[]{:S(2)}) collective-permute-start(bf16[4,144,256]{2,1,0:T(8,128)(2,1)} %get-tuple-element.81), channel_id=1, source_target_pairs={{0,4},{2,6},{4,0},{6,2},{8,12},{10,14},{12,8},{14,10},{16,20},{18,... | collective-permute-start | bytes 884744 | tf_op jit(solution)/shard_map/ppermute | solution.py:474
  91.0 17.8 %collective-permute-start.14 = (bf16[4,144,256]{2,1,0:T(8,128)(2,1)}, bf16[4,144,256]{2,1,0:T(8,128)(2,1)S(1)}, u32[]{:S(2)}, u32[]{:S(2)}) collective-permute-start(bf16[4,144,256]{2,1,0:T(8,128)(2,1)} %get-tuple-element.82), channel_id=1, source_target_pairs={{0,8},{2,10},{4,12},{6,14},{8,0},{10,2},{12,4},{14,6},{16,24},{18,... | collective-permute-start | bytes 884744 | tf_op jit(solution)/shard_map/ppermute | solution.py:474
  92.5 1.5 copy-start.15
  92.5 16.3 %collective-permute-start.15 = (bf16[4,144,256]{2,1,0:T(8,128)(2,1)}, bf16[4,144,256]{2,1,0:T(8,128)(2,1)S(1)}, u32[]{:S(2)}, u32[]{:S(2)}) collective-permute-start(bf16[4,144,256]{2,1,0:T(8,128)(2,1)} %get-tuple-element.83), channel_id=1, source_target_pairs={{0,12},{2,14},{4,8},{6,10},{8,4},{10,6},{12,0},{14,2},{16,28},{18,... | collective-permute-start | bytes 884744 | tf_op jit(solution)/shard_map/ppermute | solution.py:474
  105.3 9.2 %collective-permute-start.4 = (bf16[4,144,256]{2,1,0:T(8,128)(2,1)}, bf16[4,144,256]{2,1,0:T(8,128)(2,1)S(1)}, u32[]{:S(2)}, u32[]{:S(2)}) collective-permute-start(bf16[4,144,256]{2,1,0:T(8,128)(2,1)} %get-tuple-element.65), channel_id=1, source_target_pairs={{0,4},{2,6},{4,0},{6,2},{8,12},{10,14},{12,8},{14,10},{16,20},{18,... | collective-permute-start | bytes 884744 | tf_op jit(solution)/shard_map/ppermute | solution.py:474
  105.8 10.2 %collective-permute-start.5 = (bf16[4,144,256]{2,1,0:T(8,128)(2,1)}, bf16[4,144,256]{2,1,0:T(8,128)(2,1)S(1)}, u32[]{:S(2)}, u32[]{:S(2)}) collective-permute-start(bf16[4,144,256]{2,1,0:T(8,128)(2,1)} %get-tuple-element.66), channel_id=1, source_target_pairs={{0,8},{2,10},{4,12},{6,14},{8,0},{10,2},{12,4},{14,6},{16,24},{18,... | collective-permute-start | bytes 884744 | tf_op jit(solution)/shard_map/ppermute | solution.py:474
  107.3 1.5 %copy-start.1 = (bf16[4,144,256]{2,1,0:T(8,128)(2,1)}, bf16[4,144,256]{2,1,0:T(8,128)(2,1)S(1)}, u32[]{:S(2)}) copy-start(bf16[4,144,256]{2,1,0:T(8,128)(2,1)S(1)} %collective-permute-done.13.rest_0_) | copy-start | bytes 884740
  107.3 17.2 %collective-permute-start.6 = (bf16[4,144,256]{2,1,0:T(8,128)(2,1)}, bf16[4,144,256]{2,1,0:T(8,128)(2,1)S(1)}, u32[]{:S(2)}, u32[]{:S(2)}) collective-permute-start(bf16[4,144,256]{2,1,0:T(8,128)(2,1)} %get-tuple-element.67), channel_id=1, source_target_pairs={{0,12},{2,14},{4,8},{6,10},{8,4},{10,6},{12,0},{14,2},{16,28},{18,... | collective-permute-start | bytes 884744 | tf_op jit(solution)/shard_map/ppermute | solution.py:474
  111.8 15.9 %collective-permute-start.16 = (bf16[144,256]{1,0:T(8,128)(2,1)}, bf16[144,256]{1,0:T(8,128)(2,1)S(1)}, u32[]{:S(2)}, u32[]{:S(2)}) collective-permute-start(bf16[144,256]{1,0:T(8,128)(2,1)} %get-tuple-element.86), channel_id=1, source_target_pairs={{0,2},{2,0},{4,6},{6,4},{8,10},{10,8},{12,14},{14,12},{16,18},{18,... | collective-permute-start | bytes 221192 | tf_op jit(solution)/shard_map/ppermute | solution.py:479
  111.8 18.4 %collective-permute-start.17 = (bf16[144,256]{1,0:T(8,128)(2,1)}, bf16[144,256]{1,0:T(8,128)(2,1)S(1)}, u32[]{:S(2)}, u32[]{:S(2)}) collective-permute-start(bf16[144,256]{1,0:T(8,128)(2,1)} %get-tuple-element.87), channel_id=1, source_target_pairs={{0,16},{2,18},{4,20},{6,22},{8,24},{10,26},{12,28},{14,30},{16,0},... | collective-permute-start | bytes 221192 | tf_op jit(solution)/shard_map/ppermute | solution.py:479
  114.5 10.0 %copy-start.2 = (bf16[4,144,256]{2,1,0:T(8,128)(2,1)}, bf16[4,144,256]{2,1,0:T(8,128)(2,1)S(1)}, u32[]{:S(2)}) copy-start(bf16[4,144,256]{2,1,0:T(8,128)(2,1)S(1)} %collective-permute-done.4.rest_0_) | copy-start | bytes 884740
  114.5 15.7 %collective-permute-start.18 = (bf16[144,256]{1,0:T(8,128)(2,1)}, bf16[144,256]{1,0:T(8,128)(2,1)S(1)}, u32[]{:S(2)}, u32[]{:S(2)}) collective-permute-start(bf16[144,256]{1,0:T(8,128)(2,1)} %get-tuple-element.88), channel_id=1, source_target_pairs={{0,18},{2,16},{4,22},{6,20},{8,26},{10,24},{12,30},{14,28},{16,2},... | collective-permute-start | bytes 221192 | tf_op jit(solution)/shard_map/ppermute | solution.py:479
  115.9 8.5 %copy-start.4 = (bf16[4,144,256]{2,1,0:T(8,128)(2,1)}, bf16[4,144,256]{2,1,0:T(8,128)(2,1)S(1)}, u32[]{:S(2)}) copy-start(bf16[4,144,256]{2,1,0:T(8,128)(2,1)S(1)} %collective-permute-done.5.rest_1_) | copy-start | bytes 884740
  127.4 6.1 %collective-permute-start.7 = (bf16[144,256]{1,0:T(8,128)(2,1)}, bf16[144,256]{1,0:T(8,128)(2,1)S(1)}, u32[]{:S(2)}, u32[]{:S(2)}) collective-permute-start(bf16[144,256]{1,0:T(8,128)(2,1)} %get-tuple-element.70), channel_id=1, source_target_pairs={{0,2},{2,0},{4,6},{6,4},{8,10},{10,8},{12,14},{14,12},{16,18},{18,... | collective-permute-start | bytes 221192 | tf_op jit(solution)/shard_map/ppermute | solution.py:479
  127.4 8.4 %collective-permute-start.8 = (bf16[144,256]{1,0:T(8,128)(2,1)}, bf16[144,256]{1,0:T(8,128)(2,1)S(1)}, u32[]{:S(2)}, u32[]{:S(2)}) collective-permute-start(bf16[144,256]{1,0:T(8,128)(2,1)} %get-tuple-element.71), channel_id=1, source_target_pairs={{0,16},{2,18},{4,20},{6,22},{8,24},{10,26},{12,28},{14,30},{16,0},... | collective-permute-start | bytes 221192 | tf_op jit(solution)/shard_map/ppermute | solution.py:479
  127.7 2.5 %copy-start.7 = (bf16[144,256]{1,0:T(8,128)(2,1)}, bf16[144,256]{1,0:T(8,128)(2,1)S(1)}, u32[]{:S(2)}) copy-start(bf16[144,256]{1,0:T(8,128)(2,1)S(1)} %collective-permute-done.16.rest_0_) | copy-start | bytes 221188
  127.7 9.6 %collective-permute-start.9 = (bf16[144,256]{1,0:T(8,128)(2,1)}, bf16[144,256]{1,0:T(8,128)(2,1)S(1)}, u32[]{:S(2)}, u32[]{:S(2)}) collective-permute-start(bf16[144,256]{1,0:T(8,128)(2,1)} %get-tuple-element.72), channel_id=1, source_target_pairs={{0,18},{2,16},{4,22},{6,20},{8,26},{10,24},{12,30},{14,28},{16,2},... | collective-permute-start | bytes 221192 | tf_op jit(solution)/shard_map/ppermute | solution.py:479
  133.5 3.8 %copy-start.10 = (bf16[144,256]{1,0:T(8,128)(2,1)}, bf16[144,256]{1,0:T(8,128)(2,1)S(1)}, u32[]{:S(2)}) copy-start(bf16[144,256]{1,0:T(8,128)(2,1)S(1)} %collective-permute-done.7.rest_0_) | copy-start | bytes 221188
  135.8 1.5 %copy-start.11 = (bf16[144,256]{1,0:T(8,128)(2,1)}, bf16[144,256]{1,0:T(8,128)(2,1)S(1)}, u32[]{:S(2)}) copy-start(bf16[144,256]{1,0:T(8,128)(2,1)S(1)} %collective-permute-done.8.rest_1_) | copy-start | bytes 221188
  (9 other events, 6.6 us)
Sparse Core Ops, SparseCore 0:
  25.7 52.0 all-gather.2

commit v3 on v2

--- a/solution.py
+++ b/solution.py
@@ -16,6 +16,7 @@
 LOG2E = 1.4426950408889634
 TO_LOG2 = HD ** (-0.5) * LOG2E
 BIG = 60 * 1024 * 1024
+SMALL = 16 * 1024 * 1024
 ANY = pl.BlockSpec(memory_space=pl.ANY)
 
 
@@ -25,7 +26,7 @@
     largest = jnp.maximum(jnp.max(jnp.abs(blocks), axis=1), 1e-30)
     exponent = jnp.floor(jnp.log(largest) * LOG2E) + 1.0
     factor = jnp.exp2(-exponent) * CODE_TOP
-    codes = jnp.round(blocks * factor[:, None, :]).astype(jnp.int32).astype(jnp.int16)
+    codes = (blocks * factor[:, None, :]).astype(jnp.int32).astype(jnp.int16)
     return codes.reshape(rows, HD), exponent.astype(jnp.int32).astype(jnp.int16)
 
 
@@ -154,7 +155,7 @@
     return context, top + jnp.log(total) * LOG2E
 
 
-def attend_kernel(layout, per, slots, keep, sends, order_ref, place_ref, own_key, own_value, cos_ref, sin_ref, q_ref, *rest):
+def attend_kernel(layout, per, slots, keep, sends, order_ref, place_ref, own_key, own_value, turn_ref, q_ref, *rest):
     parts = sum(layout)
     received = list(rest[:parts])
     keep_ref, keep_log_ref = rest[parts : parts + 2]
@@ -174,7 +175,12 @@
             if is_value:
                 value_scr[:HD, window] = jnp.transpose(whole).astype(jnp.bfloat16)
             else:
-                whole = whole * cos_ref[window] + pltpu.roll(whole, HD // 2, 1) * sin_ref[window]
+                turn = turn_ref[window]
+                turned = pltpu.roll(turn, HD // 2, 1)
+                low = lax.broadcasted_iota(jnp.int32, turn.shape, 1) < HD // 2
+                cosine = jnp.where(low, turn, turned)
+                sine = jnp.where(low, -turned, turn)
+                whole = whole * cosine + pltpu.roll(whole, HD // 2, 1) * sine
                 key_scr[window] = whole.astype(jnp.bfloat16)
     value_scr[HD:] = jnp.ones((STAT_ROWS, blocks * rows), jnp.bfloat16)
     total_keys = blocks * rows
@@ -226,7 +232,7 @@
             send_ref[slot, HD:] = stats
 
 
-def attend(order, place, own, cosine, sine, q_all, received, head, per, keep):
+def attend(order, place, own, turn, q_all, received, head, per, keep):
     rows = own[0].shape[0]
     slots, _, wide = q_all.shape
     blocks = len(received)
@@ -251,8 +257,7 @@
                 whole((rows, HD)),
                 whole((rows, HD)),
                 whole((blocks * rows, HD)),
-                whole((blocks * rows, HD)),
-                pl.BlockSpec((slots, HD, wide), lambda i, a, b: (0, head, 0)),
+                pl.BlockSpec((slots, HD, wide), lambda i, a, b: (0, head + a[slots], 0)),
             ]
             + [whole(part.shape) for part in flat],
             out_specs=tuple(whole(shape.shape) for shape in shapes),
@@ -265,14 +270,14 @@
                 pltpu.VMEM((slots, 8, wide), jnp.float32),
             ],
         ),
-        compiler_params=pltpu.CompilerParams(vmem_limit_bytes=BIG),
+        compiler_params=pltpu.CompilerParams(vmem_limit_bytes=2 * SMALL),
         cost_estimate=pl.CostEstimate(
             flops=8 * per * blocks * rows * wide * HD,
             bytes_accessed=blocks * rows * HD * 16 + slots * HD * wide * 4,
             transcendentals=per * blocks * rows * wide,
         ),
         name="attend",
-    )(order, place, *own, cosine, sine, q_all, *flat)
+    )(order, place, *own, turn, q_all, *flat)
 
 
 def gather_kernel(parts, keep_ref, keep_log_ref, *rest):
@@ -300,7 +305,7 @@
     outs = pl.pallas_call(
         functools.partial(gather_kernel, len(received)),
         out_shape=tuple(shapes),
-        compiler_params=pltpu.CompilerParams(vmem_limit_bytes=BIG),
+        compiler_params=pltpu.CompilerParams(vmem_limit_bytes=SMALL),
         cost_estimate=pl.CostEstimate(
             flops=4 * (len(received) + 1) * count * HD * wide,
             bytes_accessed=count * HD * wide * (6 + 2 * len(received)),
@@ -311,9 +316,13 @@
     return outs[0], outs[1], list(outs[2:])
 
 
-def finish_kernel(split, context_ref, log_ref, *rest):
+def finish_kernel(split, aliased, core_ref, context_ref, log_ref, *rest):
     received = rest[: 2 * split - 1]
-    context_out, log_out = rest[2 * split - 1 :]
+    cache_ref, cache_log_ref = rest[2 * split - 1 : 2 * split + 1]
+    out_ref = rest[2 * split + 1 + aliased]
+    core = core_ref[0]
+    rows, heads = out_ref.shape[:2]
+    done = []
     for apart in range(split):
         pieces = []
         if apart == 0:
@@ -321,25 +330,52 @@
         else:
             pieces.append(unpack(received[apart - 1][...]))
         pieces.append(unpack(received[split - 1 + apart][...]))
-        context, logsum = blend(pieces)
-        context_out[apart] = jnp.transpose(context)
-        log_out[apart] = jnp.broadcast_to(logsum, log_out.shape[1:])
-
-
-def finish(context, log, received, split):
+        pieces.append((cache_ref[core ^ apart], cache_log_ref[core ^ apart][:1]))
+        context, _ = blend(pieces)
+        done.append(jnp.transpose(context).reshape(rows, heads // split, HD))
+    if split == 2:
+        first = jnp.where(core == 0, done[0], done[1])
+        second = jnp.where(core == 0, done[1], done[0])
+        done = [jnp.concatenate([first, second], 1)]
+    out_ref[...] = done[0].astype(out_ref.dtype)
+
+
+def finish(core, context, log, received, cache, cache_log, split, chunk, shape, before):
     wide = context.shape[1]
+    rows, all_heads, _ = shape
+    part = all_heads * split // cache.shape[0]
+
+    def whole(array):
+        return pl.BlockSpec(array.shape, lambda i, c: (0,) * array.ndim)
+
+    operands = [context, log, *received]
+    specs = [whole(array) for array in operands]
+    operands += [cache, cache_log]
+    specs += [
+        pl.BlockSpec((split, HD, wide), lambda i, c: (chunk, 0, 0)),
+        pl.BlockSpec((split, 8, wide), lambda i, c: (chunk, 0, 0)),
+    ]
+    aliases = {}
+    if before is not None:
+        operands.append(before)
+        specs.append(ANY)
+        aliases = {len(operands): 0}
     return pl.pallas_call(
-        functools.partial(finish_kernel, split),
-        out_shape=(
-            jax.ShapeDtypeStruct((split, wide, HD), jnp.float32),
-            jax.ShapeDtypeStruct((split, 8, wide), jnp.float32),
-        ),
-        compiler_params=pltpu.CompilerParams(vmem_limit_bytes=BIG),
+        functools.partial(finish_kernel, split, before is not None),
+        out_shape=jax.ShapeDtypeStruct(shape, jnp.bfloat16),
+        grid_spec=pltpu.PrefetchScalarGridSpec(
+            num_scalar_prefetch=1,
+            grid=(1,),
+            in_specs=specs,
+            out_specs=pl.BlockSpec((rows, part, HD), lambda i, c: (0, chunk, 0)),
+        ),
+        input_output_aliases=aliases,
+        compiler_params=pltpu.CompilerParams(vmem_limit_bytes=SMALL),
         cost_estimate=pl.CostEstimate(
             flops=8 * split * HD * wide, bytes_accessed=16 * split * HD * wide, transcendentals=0
         ),
         name="finish",
-    )(context, log, *received)
+    )(core.reshape(1), *operands)
 
 
 def tables(starts, rows):
@@ -349,7 +385,7 @@
     angles = positions.astype(jnp.float32)[:, None] * inverse_freq[None, :]
     cosine = jnp.cos(angles)
     sine = jnp.sin(angles)
-    return jnp.concatenate([cosine, cosine], 1), jnp.concatenate([-sine, sine], 1)
+    return jnp.concatenate([cosine, sine], 1)
 
 
 def on_device(
@@ -382,16 +418,14 @@
     side = me // per
 
     grouped = queries.reshape(row_count, kv_local, group_size, HD)
-    turned = grouped.reshape(row_count, chunks, split, group_size, HD).transpose(2, 1, 4, 0, 3)
-    turned = turned.reshape(split, chunks * HD, wide)
-    line = jnp.arange(STAT_ROWS, dtype=jnp.int32)[None, :, None]
-    tag = jnp.where(line == 0, matching[0], offsets[0]).astype(jnp.bfloat16)
-    turned = jnp.concatenate([turned, jnp.broadcast_to(tag, (split, STAT_ROWS, wide))], 1)
-    sorted_queries = [lax.dynamic_index_in_dim(turned, core ^ apart, 0, False) for apart in range(split)]
-    own_queries = [sorted_queries[0]] + [
-        lax.ppermute(sorted_queries[apart], "grp", [(i, i ^ apart) for i in range(groups)])
-        for apart in range(1, split)
+    turned = grouped.transpose(1, 3, 0, 2).reshape(kv_local * HD, wide)
+    tag = jnp.broadcast_to(matching[0].astype(jnp.bfloat16), (STAT_ROWS, wide))
+    q_all = lax.all_gather(jnp.concatenate([turned, tag], 0), "grp")
+    wanted = q_all[:, kv_local * HD, 0].astype(jnp.int32)
+    starts = [offsets] + [
+        lax.ppermute(offsets, "grp", [(i, i ^ apart) for i in range(groups)]) for apart in range(1, split)
     ]
+
     def exchange(array, shift, apart):
         pairs = [
             (g * tp + t, (g ^ apart) * tp + (t + shift) % tp) for g in range(groups) for t in range(tp)
@@ -414,6 +448,7 @@
             ["own" if shift == 0 else "send" for shift, _ in jobs],
             split,
         )
+        results, core = lax.optimization_barrier((results, core))
         for (shift, chunk), outs in zip(jobs, results):
             if shift == 0:
                 own[chunk] = outs[:2]
@@ -421,25 +456,21 @@
             for apart in range(split):
                 if outs[apart] is not None:
                     received[chunk][apart].append(exchange(outs[apart], shift, apart))
+        return core
 
     jobs = [(shift, chunk) for chunk in range(chunks) for shift in range(1, tp)]
-    run(jobs[:1], core)
-    own_queries, later_core = lax.optimization_barrier((own_queries, core))
-    members = [[chip * split + c for chip in range(groups // split)] for c in range(split)]
-    q_all = lax.all_gather(jnp.stack(own_queries), "grp", axis_index_groups=members)
-    q_all = q_all.reshape(groups, chunks * HD + STAT_ROWS, wide)
-    wanted = q_all[:, chunks * HD, 0].astype(jnp.int32)
-    starts = jnp.stack([own[chunks * HD + 1, 0] for own in own_queries]).astype(jnp.int32)
-    run(jobs[1:] + [(0, chunk) for chunk in range(chunks)], later_core)
-
-    cosine, sine = tables(starts, block_len)
+    later = run(jobs[:1], core)
+    run(jobs[1:] + [(0, chunk) for chunk in range(chunks)], later)
+
+    turn = tables(jnp.concatenate(starts), block_len)
     mine = (wanted == side).astype(jnp.int32)
     before = jnp.cumsum(mine)
     names = jnp.arange(groups, dtype=jnp.int32)
     target = jnp.where(mine == 1, before - 1, per + names - before)
     order = jnp.sum(jnp.where(target[None, :] == names[:, None], names[None, :], 0), 1).astype(jnp.int32)
     away = ((order // split) % homes) ^ spot
-    place = (away * PROMPTS + ((order // per) ^ side)) * split + order % split
+    place = (away * PROMPTS + ((order // per) ^ side)) * split + (order % split ^ core)
+    order = jnp.concatenate([order, core.reshape(1)])
 
     grouped, own[-1] = lax.optimization_barrier((grouped, own[-1]))
     score_scale = HD ** (-0.5)
@@ -459,17 +490,20 @@
         cache_values,
         preferred_element_type=jnp.float32,
     )
-    cache_sum, cache_total, cache_top, order, place = lax.optimization_barrier(
-        (cache_sum, cache_total, cache_top, order, place)
-    )
+    cache_context = cache_sum / cache_total[..., None]
+    cache_context = cache_context.transpose(1, 3, 0, 2).reshape(kv_local, HD, wide)
+    cache_log = cache_top * LOG2E + jnp.log2(cache_total)
+    cache_log = cache_log.transpose(1, 0, 2).reshape(kv_local, 1, wide)
+    cache_log = jnp.broadcast_to(cache_log, (kv_local, 8, wide))
+    cache_context, cache_log, order, place = lax.optimization_barrier((cache_context, cache_log, order, place))
 
     def partner(i, side_apart, apart):
         return (i + side_apart * per) % groups ^ apart
 
-    contexts = []
-    logs = []
+    result = None
     for chunk in range(chunks):
-        outs = attend(order, place, own[chunk], cosine, sine, q_all, received[chunk], chunk, per, keep)
+        outs = attend(order, place, own[chunk], turn, q_all, received[chunk], chunk * split, per, keep)
+        outs, order = lax.optimization_barrier((outs, order))
         arrived = [
             lax.ppermute(outs[2 + far - 1], "grp", [(i, i ^ (far * split)) for i in range(groups)])
             for far in range(1, homes)
@@ -483,23 +517,10 @@
             )
             for number in range(1, keep)
         ]
-        context, log = finish(context, log, final, split)
-        contexts.append(context)
-        logs.append(log[:, 0])
-    contexts = jnp.stack(contexts)
-    logs = jnp.stack(logs)
-    if split == 2:
-        contexts = jnp.where(core == 0, contexts, contexts[:, ::-1])
-        logs = jnp.where(core == 0, logs, logs[:, ::-1])
-    prompt_context = contexts.reshape(kv_local, row_count, group_size, HD).transpose(1, 0, 2, 3)
-    prompt_log = logs.reshape(kv_local, row_count, group_size).transpose(1, 0, 2)
-    cache_log = cache_top * LOG2E
-    top = jnp.maximum(prompt_log, cache_log)
-    prompt_share = jnp.exp2(prompt_log - top)
-    cache_share = jnp.exp2(cache_log - top)
-    total = prompt_share + cache_share * cache_total
-    context = (prompt_context * prompt_share[..., None] + cache_sum * cache_share[..., None]) / total[..., None]
-    return context.reshape(row_count, kv_local * group_size, HD).astype(jnp.bfloat16)
+        result = finish(
+            core, context, log, final, cache_context, cache_log, split, chunk, queries.shape, result
+        )
+    return result
 
 
 def solution(mesh):

time: 150 us -> 133 us (0.89)
  Pallas kernels: 63.8 us -> 51.8 us
  waiting for transfers between devices: 24.5 us -> 16.2 us
  other arithmetic: 14.1 us -> 8.2 us
  starting transfers between devices: 17.2 us -> 21.6 us
  matrix products: 7.26 us -> 10.6 us
    all_gather x1, waiting for transfers between devices: 9.86 us -> 0.02 us  [on_device(): q_all = lax.all_gather(jnp.concatenate([turned, tag], 0), 'grp')]
    pallas_call x2, Pallas kernels: 20.8 us -> 15 us  [attend(): pl.pallas_call(functools.partial(attend_kernel, layout, per, slots, keep,...]
    ppermute x6, starting transfers between devices: 4.67 us -> 8.67 us  [on_device(): lax.ppermute(sends[number - 1], 'grp', [(i, partner(i, number // split, n...]
    pallas_call x2, Pallas kernels: 4.46 us -> 0.59 us  [gather(): pl.pallas_call(functools.partial(gather_kernel, len(received)), out_shape...]
    neg x1 -> x0, other arithmetic: 3.72 us -> none  [tables(): -sine]
    cos x0 -> x1, other arithmetic: none -> 3.69 us  [tables(): cosine = jnp.cos(angles)]
    dot_general x1, matrix products: 1.26 us -> 4.82 us  [on_device(): jnp.einsum('rkgt,rktd->rkgd', cache_weights.astype(jnp.bfloat16), cache_v...]
    another operation x3 -> x0, local copies, waits for them, and re-layouts: 2.6 us -> none  [the longest x2 1.44 us: on_device(): logs = jnp.stack(logs)]
  transfers between devices with their start and end apart: 20 -> 20, of which waited for: 6 -> 5; matrix products, arithmetic and copies ran while one was open for 14% -> 16% of each run, Pallas kernels for 41% -> 39%
where the time goes in v3:
time: 133 us; the launch traced here: 132 us
  Pallas kernels  51.8 us (39%)
  starting transfers between devices  21.6 us (16%)
  waiting for transfers between devices  16.2 us (12%)
  between operations  15 us (11%)
  matrix products  10.6 us (8%)
  local copies, waits for them, and re-layouts  8.79 us (7%)
  other arithmetic  8.2 us (6%)
    pallas_call x2, Pallas kernels, project(): pl.pallas_call(functools.partial(project_kernel, plan, split, pieces), ou...  34.6 us
    pallas_call x2, Pallas kernels, attend(): pl.pallas_call(functools.partial(attend_kernel, layout, per, slots, keep,...  15 us
    ppermute x6, waiting for transfers between devices, on_device(): lax.ppermute(outs[2 + far - 1], 'grp', [(i, i ^ far * split) for i in ran...  11.1 us
    ppermute x6, starting transfers between devices, on_device(): lax.ppermute(sends[number - 1], 'grp', [(i, partner(i, number // split, n...  8.67 us
    ppermute x6, starting transfers between devices, on_device(): lax.ppermute(outs[2 + far - 1], 'grp', [(i, i ^ far * split) for i in ran...  7.36 us
    dot_general x1, matrix products, on_device(): jnp.einsum('rkgd,rktd->rkgt', grouped, cache_keys, preferred_element_type...  5.82 us
    ppermute x6, starting transfers between devices, exchange(): return lax.ppermute(array, ('grp', 'tp'), pairs)  5.07 us
    ppermute x6, waiting for transfers between devices, on_device(): lax.ppermute(sends[number - 1], 'grp', [(i, partner(i, number // split, n...  5.02 us
  transfers between devices with their start and end apart: 20, of which 5 were waited for; matrix products, arithmetic and copies ran while one was open for 16% of the time, Pallas kernels for 39%

profile of v3, /device:TPU:0, one launch (start us, length us, event | category | flops | bytes accessed | tf_op | source)
XLA Modules:
  0.0 132.2 jit_solution(12013158684414620587)
XLA Ops:
  7.2 1.1 copy.55
  8.4 0.7 concatenate.12.clone
  10.4 11.2 %project.2 = (s16[1040,256]{1,0:T(8,128)(2,1)}, s16[1040,256]{1,0:T(8,128)(2,1)}) custom-call(s32[2]{0:T(128)} %pad_add_fusion.place_ref, bf16[1024,4096]{1,0:T(8,128)(2,1)} %x_hbm.3, bf16[4096,1024]{1,0:T(8,128)(2,1)} %wk_ref.3, bf16[4096,1024]{1,0:T(8,128)(2,1)} %wv_ref.3), custom_call_target="tpu_custom_call" | custom-call | flops 4294967296 | bytes 13631488 | tf_op jit(solution)/shard_map/project/pallas_call | solution.py:102
  21.6 2.6 %collective-permute-start.1 = (s16[1040,256]{1,0:T(8,128)(2,1)}, s16[1040,256]{1,0:T(8,128)(2,1)S(1)}, u32[]{:S(2)}, u32[]{:S(2)}) collective-permute-start(s16[1040,256]{1,0:T(8,128)(2,1)} %get-tuple-element.82), channel_id=1, source_target_pairs={{0,1},{1,0},{2,3},{3,2},{4,5},{5,4},{6,7},{7,6},{8,9},{9,8},{10,11... | collective-permute-start | bytes 1597448 | tf_op jit(solution)/shard_map/ppermute | solution.py:433
  24.9 23.4 %project.3 = (s16[1040,256]{1,0:T(8,128)(2,1)}, s16[1040,256]{1,0:T(8,128)(2,1)}, f32[1024,128]{1,0:T(8,128)}, f32[1024,128]{1,0:T(8,128)}, s16[1040,256]{1,0:T(...) custom-call(s32[4]{0:T(128)} %pad_add_fusion.1.place_ref, ...), custom_call_target="tpu_custom_call" | custom-call | flops 12884901888 | bytes 24117248 | tf_op jit(solution)/shard_map/project/pallas_call | solution.py:102
  48.5 1.9 %collective-permute-start.4 = (s16[1040,256]{1,0:T(8,128)(2,1)}, s16[1040,256]{1,0:T(8,128)(2,1)S(1)}, u32[]{:S(2)}, u32[]{:S(2)}) collective-permute-start(s16[1040,256]{1,0:T(8,128)(2,1)} %get-tuple-element.93), channel_id=1, source_target_pairs={{0,1},{1,0},{2,3},{3,2},{4,5},{5,4},{6,7},{7,6},{8,9},{9,8},{10,11... | collective-permute-start | bytes 1597448 | tf_op jit(solution)/shard_map/ppermute | solution.py:433
  51.1 5.8 %fusion.15 = (f32[32,4,8]{2,1,0:T(4,128)S(1)}, f32[32,4,8,256]{3,2,1,0:T(8,128)S(1)}) fusion(bf16[32,4,8,128]{3,2,1,0:T(8,128)(2,1)S(1)} %bitcast.44, bf16[32,4,256,128]{3,2,1,0:T(8,128)(2,1)} %param.15, pred[32,256]{1,0:T(8,128)(4,1)S(1)} %iota_compare_fusion), kind=kOutput, calls=%fused_computation.49 | convolution fusion | flops 67894272 | bytes 9711616 | tf_op jit(solution)/shard_map/rkgd,rktd->rkgt/dot_general | solution.py:479
  57.7 4.8 %fusion.1 = f32[4,128,32,8]{1,3,0,2:T(8,128)S(1)} fusion(bf16[32,4,256,128]{3,2,1,0:T(8,128)(2,1)} %param.16, f32[32,4,8,256]{3,2,1,0:T(8,128)S(1)} %get-tuple-element.128, f32[32,4,8]{2,1,0:T(4,128)S(1)} %get-tuple-element.127, pred[32,256]{1,0:T(8,128)(4,1)S(1)} %iota_compare_fusion, f32[4,32,8]{2,0,1:T(4,128)S(1)} %copy.37), kind=kOutput, calls=%fused_computation.5 | convolution fusion | flops 68026368 | bytes 9977856 | tf_op jit(solution)/shard_map/rkgt,rktd->rkgd/dot_general | solution.py:487
  62.5 0.8 copy.53
  63.7 0.7 pad_add_fusion.3
  64.5 3.7 %multiply_cosine_fusion = (f32[2048,64]{1,0:T(8,128)S(1)}, f32[2048,64]{1,0:T(8,128)S(1)}) fusion(f32[64]{0:T(128)S(1)} %negate_power_fusion, f32[2048]{0:T(1024)S(1)} %bitcast.48), kind=kLoop, calls=%fused_computation.1 | loop fusion | flops 131072 | bytes 1057024 | tf_op jit(solution)/shard_map/cos | solution.py:386
  68.6 1.1 compare_reduce_fusion
  70.3 2.2 %copy-done = bf16[8448,256]{1,0:T(8,128)(2,1)S(1)} copy-done((bf16[8448,256]{1,0:T(8,128)(2,1)S(1)}, bf16[8448,256]{1,0:T(8,128)(2,1)}, u32[]{:S(2)}) %copy-start) | copy-done | bytes 4325400
  72.5 1.0 copy-done.4
  73.6 1.0 copy-done.5
  74.6 6.9 %attend.2 = (f32[4,128,256]{2,1,0:T(8,128)S(1)}, f32[4,8,256]{2,1,0:T(8,128)S(1)}, bf16[4,144,256]{2,1,0:T(8,128)(2,1)S(1)}, bf16[4,144,256]{2,1,0:T(8,128)(2,1)S(1)}, bf16[4,144,256]{2,1,0:T(8,128)(2,1)S(1)}) custom-call(s32[17]{0:T(128)S(1)} %pad_add_fusion.2.order_ref, s32[16]{0:T(128)S(1)} %fusion.12.place_ref, f32[1024,128]{1,0:T(8,128)S(1)} %copy-done.4, ...), custom_call_target="tpu_custom_call" | custom-call | flops 4294967296 | bytes 6291456 | tf_op jit(solution)/shard_map/attend/pallas_call | solution.py:250
  81.5 2.1 %collective-permute-start.13 = (bf16[4,144,256]{2,1,0:T(8,128)(2,1)S(1)}, bf16[4,144,256]{2,1,0:T(8,128)(2,1)S(1)}, u32[]{:S(2)}, u32[]{:S(2)}) collective-permute-start(bf16[4,144,256]{2,1,0:T(8,128)(2,1)S(1)} %get-tuple-element.115), channel_id=1, source_target_pairs={{0,4},{2,6},{4,0},{6,2},{8,12},{10,14},{12,8},{14,10},{16,20},{18,... | collective-permute-start | bytes 884744 | tf_op jit(solution)/shard_map/ppermute | solution.py:508
  83.6 1.7 %collective-permute-start.14 = (bf16[4,144,256]{2,1,0:T(8,128)(2,1)S(1)}, bf16[4,144,256]{2,1,0:T(8,128)(2,1)S(1)}, u32[]{:S(2)}, u32[]{:S(2)}) collective-permute-start(bf16[4,144,256]{2,1,0:T(8,128)(2,1)S(1)} %get-tuple-element.116), channel_id=1, source_target_pairs={{0,8},{2,10},{4,12},{6,14},{8,0},{10,2},{12,4},{14,6},{16,24},{18,... | collective-permute-start | bytes 884744 | tf_op jit(solution)/shard_map/ppermute | solution.py:508
  85.4 8.1 %attend.3 = (f32[4,128,256]{2,1,0:T(8,128)S(1)}, f32[4,8,256]{2,1,0:T(8,128)S(1)}, bf16[4,144,256]{2,1,0:T(8,128)(2,1)S(1)}, bf16[4,144,256]{2,1,0:T(8,128)(2,1)S(1)}, bf16[4,144,256]{2,1,0:T(8,128)(2,1)S(1)}) custom-call(s32[17]{0:T(128)S(1)} %pad_add_fusion.2.order_ref, s32[16]{0:T(128)S(1)} %fusion.12.place_ref, f32[1024,128]{1,0:T(8,128)S(1)} %copy-done.2, ...), custom_call_target="tpu_custom_call" | custom-call | flops 4294967296 | bytes 6291456 | tf_op jit(solution)/shard_map/attend/pallas_call | solution.py:250
  93.4 1.9 %collective-permute-start.7 = (bf16[4,144,256]{2,1,0:T(8,128)(2,1)S(1)}, bf16[4,144,256]{2,1,0:T(8,128)(2,1)S(1)}, u32[]{:S(2)}, u32[]{:S(2)}) collective-permute-start(bf16[4,144,256]{2,1,0:T(8,128)(2,1)S(1)} %get-tuple-element.103), channel_id=1, source_target_pairs={{0,4},{2,6},{4,0},{6,2},{8,12},{10,14},{12,8},{14,10},{16,20},{18,... | collective-permute-start | bytes 884744 | tf_op jit(solution)/shard_map/ppermute | solution.py:508
  95.3 1.7 %collective-permute-start.8 = (bf16[4,144,256]{2,1,0:T(8,128)(2,1)S(1)}, bf16[4,144,256]{2,1,0:T(8,128)(2,1)S(1)}, u32[]{:S(2)}, u32[]{:S(2)}) collective-permute-start(bf16[4,144,256]{2,1,0:T(8,128)(2,1)S(1)} %get-tuple-element.104), channel_id=1, source_target_pairs={{0,8},{2,10},{4,12},{6,14},{8,0},{10,2},{12,4},{14,6},{16,24},{18,... | collective-permute-start | bytes 884744 | tf_op jit(solution)/shard_map/ppermute | solution.py:508
  97.0 2.3 %collective-permute-done.15.rest_2_ = bf16[4,144,256]{2,1,0:T(8,128)(2,1)S(1)} collective-permute-done((bf16[4,144,256]{2,1,0:T(8,128)(2,1)S(1)}, bf16[4,144,256]{2,1,0:T(8,128)(2,1)S(1)}, u32[]{:S(2)}, u32[]{:S(2)}) %collective-permute-start.15) | collective-permute-done | bytes 294944 | tf_op jit(solution)/shard_map/ppermute | solution.py:508
  99.7 3.1 %collective-permute-start.17 = (bf16[144,256]{1,0:T(8,128)(2,1)S(1)}, bf16[144,256]{1,0:T(8,128)(2,1)S(1)}, u32[]{:S(2)}, u32[]{:S(2)}) collective-permute-start(bf16[144,256]{1,0:T(8,128)(2,1)S(1)} %get-tuple-element.121), channel_id=1, source_target_pairs={{0,16},{2,18},{4,20},{6,22},{8,24},{10,26},{12,28},{14,30},{16,0},... | collective-permute-start | bytes 221192 | tf_op jit(solution)/shard_map/ppermute | solution.py:513
  102.8 2.6 %collective-permute-done.7.rest_0_ = bf16[4,144,256]{2,1,0:T(8,128)(2,1)S(1)} collective-permute-done((bf16[4,144,256]{2,1,0:T(8,128)(2,1)S(1)}, bf16[4,144,256]{2,1,0:T(8,128)(2,1)S(1)}, u32[]{:S(2)}, u32[]{:S(2)}) %collective-permute-start.7) | collective-permute-done | bytes 294944 | tf_op jit(solution)/shard_map/ppermute | solution.py:508
  105.4 2.7 %collective-permute-start.18 = (bf16[144,256]{1,0:T(8,128)(2,1)S(1)}, bf16[144,256]{1,0:T(8,128)(2,1)S(1)}, u32[]{:S(2)}, u32[]{:S(2)}) collective-permute-start(bf16[144,256]{1,0:T(8,128)(2,1)S(1)} %get-tuple-element.122), channel_id=1, source_target_pairs={{0,18},{2,16},{4,22},{6,20},{8,26},{10,24},{12,30},{14,28},{16,2},... | collective-permute-start | bytes 221192 | tf_op jit(solution)/shard_map/ppermute | solution.py:513
  108.1 6.1 %collective-permute-done.9.rest_2_ = bf16[4,144,256]{2,1,0:T(8,128)(2,1)S(1)} collective-permute-done((bf16[4,144,256]{2,1,0:T(8,128)(2,1)S(1)}, bf16[4,144,256]{2,1,0:T(8,128)(2,1)S(1)}, u32[]{:S(2)}, u32[]{:S(2)}) %collective-permute-start.9) | collective-permute-done | bytes 294944 | tf_op jit(solution)/shard_map/ppermute | solution.py:508
  114.6 2.0 %collective-permute-start.11 = (bf16[144,256]{1,0:T(8,128)(2,1)S(1)}, bf16[144,256]{1,0:T(8,128)(2,1)S(1)}, u32[]{:S(2)}, u32[]{:S(2)}) collective-permute-start(bf16[144,256]{1,0:T(8,128)(2,1)S(1)} %get-tuple-element.109), channel_id=1, source_target_pairs={{0,16},{2,18},{4,20},{6,22},{8,24},{10,26},{12,28},{14,30},{16,0},... | collective-permute-start | bytes 221192 | tf_op jit(solution)/shard_map/ppermute | solution.py:513
  116.6 0.8 collective-permute-start.12
  117.4 1.2 copy.45.rest_3_
  118.7 0.8 finish.2.rest_5_
  119.5 4.3 %collective-permute-done.11.rest_1_ = bf16[144,256]{1,0:T(8,128)(2,1)S(1)} collective-permute-done((bf16[144,256]{1,0:T(8,128)(2,1)S(1)}, bf16[144,256]{1,0:T(8,128)(2,1)S(1)}, u32[]{:S(2)}, u32[]{:S(2)}) %collective-permute-start.11) | collective-permute-done | bytes 73760 | tf_op jit(solution)/shard_map/ppermute | solution.py:513
  124.5 0.8 finish.3
  (65 shorter events, 5.8 us)
Async XLA Ops:
  6.5 62.0 %all-gather.3.cloned.1.call-start = ((), (), s32[]{:S(2)}) async-start(), calls=%async_computation | async-start | bytes 4595712 | tf_op jit(solution)/shard_map/all_gather | solution.py:423
  9.2 54.4 %collective-permute-start = (s32[1]{0:T(128)}, s32[1]{0:T(128)}, u32[]{:S(2)}, u32[]{:S(2)}) collective-permute-start(s32[1]{0:T(128)} %param.12), channel_id=1, source_target_pairs={{0,2},{2,0},{4,6},{6,4},{8,10},{10,8},{12,14},{14,12},{16,18},{18,... | collective-permute-start | bytes 20 | tf_op jit(solution)/shard_map/ppermute | solution.py:426
  21.6 48.5 %collective-permute-start.1 = (s16[1040,256]{1,0:T(8,128)(2,1)}, s16[1040,256]{1,0:T(8,128)(2,1)S(1)}, u32[]{:S(2)}, u32[]{:S(2)}) collective-permute-start(s16[1040,256]{1,0:T(8,128)(2,1)} %get-tuple-element.82), channel_id=1, source_target_pairs={{0,1},{1,0},{2,3},{3,2},{4,5},{5,4},{6,7},{7,6},{8,9},{9,8},{10,11... | collective-permute-start | bytes 1597448 | tf_op jit(solution)/shard_map/ppermute | solution.py:433
  24.2 46.1 %collective-permute-start.2 = (s16[1040,256]{1,0:T(8,128)(2,1)}, s16[1040,256]{1,0:T(8,128)(2,1)S(1)}, u32[]{:S(2)}, u32[]{:S(2)}) collective-permute-start(s16[1040,256]{1,0:T(8,128)(2,1)} %get-tuple-element.83), channel_id=1, source_target_pairs={{0,3},{1,2},{2,1},{3,0},{4,7},{5,6},{6,5},{7,4},{8,11},{9,10},{10,... | collective-permute-start | bytes 1597448 | tf_op jit(solution)/shard_map/ppermute | solution.py:433
  24.9 26.1 %copy-start.7 = (s32[32]{0:T(128)S(1)}, s32[32]{0:T(128)}, u32[]{:S(2)}) copy-start(s32[32]{0:T(128)} %param.17) | copy-start | bytes 388
  24.9 26.2 %copy-start.6 = (bf16[32,32,128]{2,1,0:T(8,128)(2,1)S(1)}, bf16[32,32,128]{2,1,0:T(8,128)(2,1)}, u32[]{:S(2)}) copy-start(bf16[32,32,128]{2,1,0:T(8,128)(2,1)} %param.14) | copy-start | bytes 786436
  48.3 22.0 %collective-permute-start.3 = (s16[1040,256]{1,0:T(8,128)(2,1)}, s16[1040,256]{1,0:T(8,128)(2,1)S(1)}, u32[]{:S(2)}, u32[]{:S(2)}) collective-permute-start(s16[1040,256]{1,0:T(8,128)(2,1)} %get-tuple-element.84), channel_id=1, source_target_pairs={{0,2},{1,3},{2,0},{3,1},{4,6},{5,7},{6,4},{7,5},{8,10},{9,11},{10,... | collective-permute-start | bytes 1597448 | tf_op jit(solution)/shard_map/ppermute | solution.py:433
  48.5 36.8 %collective-permute-start.4 = (s16[1040,256]{1,0:T(8,128)(2,1)}, s16[1040,256]{1,0:T(8,128)(2,1)S(1)}, u32[]{:S(2)}, u32[]{:S(2)}) collective-permute-start(s16[1040,256]{1,0:T(8,128)(2,1)} %get-tuple-element.93), channel_id=1, source_target_pairs={{0,1},{1,0},{2,3},{3,2},{4,5},{5,4},{6,7},{7,6},{8,9},{9,8},{10,11... | collective-permute-start | bytes 1597448 | tf_op jit(solution)/shard_map/ppermute | solution.py:433
  63.6 21.7 %collective-permute-start.5 = (s16[1040,256]{1,0:T(8,128)(2,1)}, s16[1040,256]{1,0:T(8,128)(2,1)}, u32[]{:S(2)}, u32[]{:S(2)}) collective-permute-start(s16[1040,256]{1,0:T(8,128)(2,1)} %get-tuple-element.94), channel_id=1, source_target_pairs={{0,3},{1,2},{2,1},{3,0},{4,7},{5,6},{6,5},{7,4},{8,11},{9,10},{10,... | collective-permute-start | bytes 1597448 | tf_op jit(solution)/shard_map/ppermute | solution.py:433
  70.0 15.3 %collective-permute-start.6 = (s16[1040,256]{1,0:T(8,128)(2,1)}, s16[1040,256]{1,0:T(8,128)(2,1)S(1)}, u32[]{:S(2)}, u32[]{:S(2)}) collective-permute-start(s16[1040,256]{1,0:T(8,128)(2,1)} %get-tuple-element.95), channel_id=1, source_target_pairs={{0,2},{1,3},{2,0},{3,1},{4,6},{5,7},{6,4},{7,5},{8,10},{9,11},{10,... | collective-permute-start | bytes 1597448 | tf_op jit(solution)/shard_map/ppermute | solution.py:433
  70.3 2.2 %copy-start = (bf16[8448,256]{1,0:T(8,128)(2,1)S(1)}, bf16[8448,256]{1,0:T(8,128)(2,1)}, u32[]{:S(2)}) copy-start(bf16[8448,256]{1,0:T(8,128)(2,1)} %all-gather.3.cloned.1.call-done) | copy-start | bytes 12976132
  72.5 1.0 copy-start.4
  73.6 1.0 copy-start.5
  74.6 10.7 %copy-start.1 = (bf16[8448,256]{1,0:T(8,128)(2,1)S(1)}, bf16[8448,256]{1,0:T(8,128)(2,1)}, u32[]{:S(2)}) copy-start(bf16[8448,256]{1,0:T(8,128)(2,1)} %all-gather.3.cloned.1.call-done) | copy-start | bytes 12976132
  74.6 10.7 %copy-start.2 = (f32[1024,128]{1,0:T(8,128)S(1)}, f32[1024,128]{1,0:T(8,128)}, u32[]{:S(2)}) copy-start(f32[1024,128]{1,0:T(8,128)} %get-tuple-element.91.own_key) | copy-start | bytes 1572868
  74.6 10.7 %copy-start.3 = (f32[1024,128]{1,0:T(8,128)S(1)}, f32[1024,128]{1,0:T(8,128)}, u32[]{:S(2)}) copy-start(f32[1024,128]{1,0:T(8,128)} %get-tuple-element.92.own_value) | copy-start | bytes 1572868
  81.5 15.5 %collective-permute-start.13 = (bf16[4,144,256]{2,1,0:T(8,128)(2,1)S(1)}, bf16[4,144,256]{2,1,0:T(8,128)(2,1)S(1)}, u32[]{:S(2)}, u32[]{:S(2)}) collective-permute-start(bf16[4,144,256]{2,1,0:T(8,128)(2,1)S(1)} %get-tuple-element.115), channel_id=1, source_target_pairs={{0,4},{2,6},{4,0},{6,2},{8,12},{10,14},{12,8},{14,10},{16,20},{18,... | collective-permute-start | bytes 884744 | tf_op jit(solution)/shard_map/ppermute | solution.py:508
  83.6 13.4 %collective-permute-start.14 = (bf16[4,144,256]{2,1,0:T(8,128)(2,1)S(1)}, bf16[4,144,256]{2,1,0:T(8,128)(2,1)S(1)}, u32[]{:S(2)}, u32[]{:S(2)}) collective-permute-start(bf16[4,144,256]{2,1,0:T(8,128)(2,1)S(1)} %get-tuple-element.116), channel_id=1, source_target_pairs={{0,8},{2,10},{4,12},{6,14},{8,0},{10,2},{12,4},{14,6},{16,24},{18,... | collective-permute-start | bytes 884744 | tf_op jit(solution)/shard_map/ppermute | solution.py:508
  85.3 14.1 %collective-permute-start.15 = (bf16[4,144,256]{2,1,0:T(8,128)(2,1)S(1)}, bf16[4,144,256]{2,1,0:T(8,128)(2,1)S(1)}, u32[]{:S(2)}, u32[]{:S(2)}) collective-permute-start(bf16[4,144,256]{2,1,0:T(8,128)(2,1)S(1)} %get-tuple-element.117), channel_id=1, source_target_pairs={{0,12},{2,14},{4,8},{6,10},{8,4},{10,6},{12,0},{14,2},{16,28},{18,... | collective-permute-start | bytes 884744 | tf_op jit(solution)/shard_map/ppermute | solution.py:508
  93.4 12.0 %collective-permute-start.7 = (bf16[4,144,256]{2,1,0:T(8,128)(2,1)S(1)}, bf16[4,144,256]{2,1,0:T(8,128)(2,1)S(1)}, u32[]{:S(2)}, u32[]{:S(2)}) collective-permute-start(bf16[4,144,256]{2,1,0:T(8,128)(2,1)S(1)} %get-tuple-element.103), channel_id=1, source_target_pairs={{0,4},{2,6},{4,0},{6,2},{8,12},{10,14},{12,8},{14,10},{16,20},{18,... | collective-permute-start | bytes 884744 | tf_op jit(solution)/shard_map/ppermute | solution.py:508
  95.3 12.8 %collective-permute-start.8 = (bf16[4,144,256]{2,1,0:T(8,128)(2,1)S(1)}, bf16[4,144,256]{2,1,0:T(8,128)(2,1)S(1)}, u32[]{:S(2)}, u32[]{:S(2)}) collective-permute-start(bf16[4,144,256]{2,1,0:T(8,128)(2,1)S(1)} %get-tuple-element.104), channel_id=1, source_target_pairs={{0,8},{2,10},{4,12},{6,14},{8,0},{10,2},{12,4},{14,6},{16,24},{18,... | collective-permute-start | bytes 884744 | tf_op jit(solution)/shard_map/ppermute | solution.py:508
  97.0 17.3 %collective-permute-start.9 = (bf16[4,144,256]{2,1,0:T(8,128)(2,1)S(1)}, bf16[4,144,256]{2,1,0:T(8,128)(2,1)S(1)}, u32[]{:S(2)}, u32[]{:S(2)}) collective-permute-start(bf16[4,144,256]{2,1,0:T(8,128)(2,1)S(1)} %get-tuple-element.105), channel_id=1, source_target_pairs={{0,12},{2,14},{4,8},{6,10},{8,4},{10,6},{12,0},{14,2},{16,28},{18,... | collective-permute-start | bytes 884744 | tf_op jit(solution)/shard_map/ppermute | solution.py:508
  99.7 17.0 %collective-permute-start.16 = (bf16[144,256]{1,0:T(8,128)(2,1)S(1)}, bf16[144,256]{1,0:T(8,128)(2,1)S(1)}, u32[]{:S(2)}, u32[]{:S(2)}) collective-permute-start(bf16[144,256]{1,0:T(8,128)(2,1)S(1)} %get-tuple-element.120), channel_id=1, source_target_pairs={{0,2},{2,0},{4,6},{6,4},{8,10},{10,8},{12,14},{14,12},{16,18},{18,... | collective-permute-start | bytes 221192 | tf_op jit(solution)/shard_map/ppermute | solution.py:513
  99.7 18.9 %collective-permute-start.17 = (bf16[144,256]{1,0:T(8,128)(2,1)S(1)}, bf16[144,256]{1,0:T(8,128)(2,1)S(1)}, u32[]{:S(2)}, u32[]{:S(2)}) collective-permute-start(bf16[144,256]{1,0:T(8,128)(2,1)S(1)} %get-tuple-element.121), channel_id=1, source_target_pairs={{0,16},{2,18},{4,20},{6,22},{8,24},{10,26},{12,28},{14,30},{16,0},... | collective-permute-start | bytes 221192 | tf_op jit(solution)/shard_map/ppermute | solution.py:513
  105.4 13.2 %collective-permute-start.18 = (bf16[144,256]{1,0:T(8,128)(2,1)S(1)}, bf16[144,256]{1,0:T(8,128)(2,1)S(1)}, u32[]{:S(2)}, u32[]{:S(2)}) collective-permute-start(bf16[144,256]{1,0:T(8,128)(2,1)S(1)} %get-tuple-element.122), channel_id=1, source_target_pairs={{0,18},{2,16},{4,22},{6,20},{8,26},{10,24},{12,30},{14,28},{16,2},... | collective-permute-start | bytes 221192 | tf_op jit(solution)/shard_map/ppermute | solution.py:513
  114.6 4.9 %collective-permute-start.10 = (bf16[144,256]{1,0:T(8,128)(2,1)S(1)}, bf16[144,256]{1,0:T(8,128)(2,1)S(1)}, u32[]{:S(2)}, u32[]{:S(2)}) collective-permute-start(bf16[144,256]{1,0:T(8,128)(2,1)S(1)} %get-tuple-element.108), channel_id=1, source_target_pairs={{0,2},{2,0},{4,6},{6,4},{8,10},{10,8},{12,14},{14,12},{16,18},{18,... | collective-permute-start | bytes 221192 | tf_op jit(solution)/shard_map/ppermute | solution.py:513
  114.6 9.2 %collective-permute-start.11 = (bf16[144,256]{1,0:T(8,128)(2,1)S(1)}, bf16[144,256]{1,0:T(8,128)(2,1)S(1)}, u32[]{:S(2)}, u32[]{:S(2)}) collective-permute-start(bf16[144,256]{1,0:T(8,128)(2,1)S(1)} %get-tuple-element.109), channel_id=1, source_target_pairs={{0,16},{2,18},{4,20},{6,22},{8,24},{10,26},{12,28},{14,30},{16,0},... | collective-permute-start | bytes 221192 | tf_op jit(solution)/shard_map/ppermute | solution.py:513
  116.6 7.9 %collective-permute-start.12 = (bf16[144,256]{1,0:T(8,128)(2,1)S(1)}, bf16[144,256]{1,0:T(8,128)(2,1)S(1)}, u32[]{:S(2)}, u32[]{:S(2)}) collective-permute-start(bf16[144,256]{1,0:T(8,128)(2,1)S(1)} %get-tuple-element.110), channel_id=1, source_target_pairs={{0,18},{2,16},{4,22},{6,20},{8,26},{10,24},{12,30},{14,28},{16,2},... | collective-permute-start | bytes 221192 | tf_op jit(solution)/shard_map/ppermute | solution.py:513
Sparse Core Ops, SparseCore 0:
  9.6 53.9 all-gather.2

commit v4 on v3

--- a/solution.py
+++ b/solution.py
@@ -37,80 +37,91 @@
     return (blocks * factor[:, None, :]).reshape(rows, HD)
 
 
-def project_kernel(plan, split, pieces, place_ref, x_hbm, wk_ref, wv_ref, *rest):
+def project_kernel(plan, split, pieces, place_ref, x_hbm, wk_hbm, wv_hbm, *rest):
     count = sum(split - (kind == "own") for kind in plan) + 2 * plan.count("own")
-    outs = rest[:count]
-    x_ref, acc, sems = rest[count:]
-    step = pl.program_id(0)
-    rows = x_ref.shape[0]
-    width = wk_ref.shape[1]
-    part = rows // pieces
-
-    def fetch(piece):
-        window = pl.ds(piece * part, part)
-        return pltpu.make_async_copy(x_hbm.at[window], x_ref.at[window], sems.at[piece])
-
-    @pl.when(step == 0)
-    def _():
+    outs = list(rest[:count])
+    x_ref, wk_ref, wv_ref, acc, x_sems, wk_sems, wv_sems = rest[count:]
+    rows, depth = x_ref.shape
+    width = wk_ref.shape[2]
+    part = depth // pieces
+    core = place_ref[0]
+
+    def x_copy(piece):
+        window = pl.ds(pl.multiple_of(piece * part, part), part)
+        return pltpu.make_async_copy(x_hbm.at[:, window], x_ref.at[:, window], x_sems.at[piece])
+
+    def weight_copies(step, piece):
+        window = pl.ds(pl.multiple_of(piece * part, part), part)
+        lanes = pl.ds(pl.multiple_of(place_ref[1 + step] * width, width), width)
+        return [
+            pltpu.make_async_copy(hbm.at[window, lanes], ref.at[step % 2, window], sems.at[step % 2, piece])
+            for hbm, ref, sems in ((wk_hbm, wk_ref, wk_sems), (wv_hbm, wv_ref, wv_sems))
+        ]
+
+    for piece in range(pieces):
+        x_copy(piece).start()
+        for copy in weight_copies(0, piece):
+            copy.start()
+    for step, kind in enumerate(plan):
+        if step + 1 < len(plan):
+            for piece in range(pieces):
+                for copy in weight_copies(step + 1, piece):
+                    copy.start()
+
         for piece in range(pieces):
-            fetch(piece).start()
-
-    for piece in range(pieces):
-
-        @pl.when(step == 0)
-        def _():
-            fetch(piece).wait()
-
-        window = pl.ds(piece * part, part)
-        acc[window, :width] = jnp.dot(x_ref[window], wk_ref[...], preferred_element_type=jnp.float32)
-        acc[window, width:] = jnp.dot(x_ref[window], wv_ref[...], preferred_element_type=jnp.float32)
-
-    core = place_ref[0]
-    index = 0
-    for number, kind in enumerate(plan):
-        here = list(outs[index : index + split + (kind == "own")])
-        index += split + (kind == "own")
-
-        @pl.when(step == number)
-        def _():
-            refs = list(here)
-            for apart in range(split):
-                lanes = pl.multiple_of((core ^ apart) * HD, HD)
-                if kind == "own" and apart == 0:
-                    refs.pop(0)[...] = acc[:, pl.ds(lanes, HD)]
-                    refs.pop(0)[...] = acc[:, pl.ds(width + lanes, HD)]
-                    continue
-                ref = refs.pop(0)
-                for half in range(2):
-                    codes, exponent = encode(acc[:, pl.ds(half * width + lanes, HD)])
-                    ref[:rows, half * HD : (half + 1) * HD] = codes
-                    ref[rows:, half * HD : (half + 1) * HD] = exponent
+            if step == 0:
+                x_copy(piece).wait()
+            for copy in weight_copies(step, piece):
+                copy.wait()
+            window = slice(piece * part, (piece + 1) * part)
+            left = x_ref[:, window]
+            for half, ref in ((0, wk_ref), (1, wv_ref)):
+                lanes = slice(half * width, (half + 1) * width)
+                term = jnp.dot(left, ref[step % 2, window], preferred_element_type=jnp.float32)
+                if piece == 0:
+                    acc[:, lanes] = term
+                else:
+                    acc[:, lanes] += term
+        for apart in range(split):
+            lanes = pl.multiple_of((core ^ apart) * HD, HD)
+            if kind == "own" and apart == 0:
+                outs.pop(0)[...] = acc[:, pl.ds(lanes, HD)]
+                outs.pop(0)[...] = acc[:, pl.ds(width + lanes, HD)]
+                continue
+            ref = outs.pop(0)
+            for half in range(2):
+                codes, exponent = encode(acc[:, pl.ds(half * width + lanes, HD)])
+                ref[:rows, half * HD : (half + 1) * HD] = codes
+                ref[rows:, half * HD : (half + 1) * HD] = exponent
 
 
 def project(x, wk, wv, core, columns, plan, split):
     rows, depth = x.shape
     width = split * HD
     steps = len(plan)
-    pieces = 2
+    pieces = 4
     coded = jax.ShapeDtypeStruct((rows + CODE_BLOCKS, 2 * HD), jnp.int16)
     plain = jax.ShapeDtypeStruct((rows, HD), jnp.float32)
     shapes = []
     for kind in plan:
         shapes += ([plain, plain] if kind == "own" else [coded]) + [coded] * (split - 1)
-    weight_spec = pl.BlockSpec((depth, width), lambda s, p: (0, p[1 + s]))
     place = jnp.stack([core] + columns).astype(jnp.int32)
     outs = pl.pallas_call(
         functools.partial(project_kernel, plan, split, pieces),
         out_shape=tuple(shapes),
         grid_spec=pltpu.PrefetchScalarGridSpec(
             num_scalar_prefetch=1,
-            grid=(steps,),
-            in_specs=[ANY, weight_spec, weight_spec],
+            grid=(1,),
+            in_specs=[ANY, ANY, ANY],
             out_specs=tuple(pl.BlockSpec(shape.shape, lambda s, p: (0, 0)) for shape in shapes),
             scratch_shapes=[
                 pltpu.VMEM((rows, depth), x.dtype),
+                pltpu.VMEM((2, depth, width), wk.dtype),
+                pltpu.VMEM((2, depth, width), wv.dtype),
                 pltpu.VMEM((rows, 2 * width), jnp.float32),
                 pltpu.SemaphoreType.DMA((pieces,)),
+                pltpu.SemaphoreType.DMA((2, pieces)),
+                pltpu.SemaphoreType.DMA((2, pieces)),
             ],
         ),
         compiler_params=pltpu.CompilerParams(vmem_limit_bytes=BIG),
@@ -155,7 +166,7 @@
     return context, top + jnp.log(total) * LOG2E
 
 
-def attend_kernel(layout, per, slots, keep, sends, order_ref, place_ref, own_key, own_value, turn_ref, q_ref, *rest):
+def attend_kernel(layout, per, slots, keep, sends, order_ref, place_ref, own_key, own_value, cos_ref, sin_ref, q_ref, *rest):
     parts = sum(layout)
     received = list(rest[:parts])
     keep_ref, keep_log_ref = rest[parts : parts + 2]
@@ -175,11 +186,13 @@
             if is_value:
                 value_scr[:HD, window] = jnp.transpose(whole).astype(jnp.bfloat16)
             else:
-                turn = turn_ref[window]
-                turned = pltpu.roll(turn, HD // 2, 1)
-                low = lax.broadcasted_iota(jnp.int32, turn.shape, 1) < HD // 2
-                cosine = jnp.where(low, turn, turned)
-                sine = jnp.where(low, -turned, turn)
+                cosine = cos_ref[...]
+                sine = sin_ref[...]
+                low = lax.broadcasted_iota(jnp.int32, cosine.shape, 1) < HD // 2
+                mine = low if block == 0 else ~low
+                cosine = jnp.where(mine, cosine, pltpu.roll(cosine, HD // 2, 1))
+                sine = jnp.where(mine, sine, pltpu.roll(sine, HD // 2, 1))
+                sine = jnp.where(low, -sine, sine)
                 whole = whole * cosine + pltpu.roll(whole, HD // 2, 1) * sine
                 key_scr[window] = whole.astype(jnp.bfloat16)
     value_scr[HD:] = jnp.ones((STAT_ROWS, blocks * rows), jnp.bfloat16)
@@ -232,7 +245,7 @@
             send_ref[slot, HD:] = stats
 
 
-def attend(order, place, own, turn, q_all, received, head, per, keep):
+def attend(order, place, own, cosine, sine, q_all, received, head, per, keep):
     rows = own[0].shape[0]
     slots, _, wide = q_all.shape
     blocks = len(received)
@@ -256,7 +269,8 @@
             in_specs=[
                 whole((rows, HD)),
                 whole((rows, HD)),
-                whole((blocks * rows, HD)),
+                whole((rows, HD)),
+                whole((rows, HD)),
                 pl.BlockSpec((slots, HD, wide), lambda i, a, b: (0, head + a[slots], 0)),
             ]
             + [whole(part.shape) for part in flat],
@@ -277,7 +291,7 @@
             transcendentals=per * blocks * rows * wide,
         ),
         name="attend",
-    )(order, place, *own, turn, q_all, *flat)
+    )(order, place, *own, cosine, sine, q_all, *flat)
 
 
 def gather_kernel(parts, keep_ref, keep_log_ref, *rest):
@@ -381,11 +395,11 @@
 def tables(starts, rows):
     half_width = HD // 2
     inverse_freq = 500000.0 ** (-(jnp.arange(half_width, dtype=jnp.float32) * 2.0 / HD))
-    positions = (starts[:, None] + jnp.arange(rows, dtype=jnp.int32)[None, :]).reshape(-1)
-    angles = positions.astype(jnp.float32)[:, None] * inverse_freq[None, :]
-    cosine = jnp.cos(angles)
-    sine = jnp.sin(angles)
-    return jnp.concatenate([cosine, sine], 1)
+    lane = jnp.arange(HD, dtype=jnp.int32)[None, :]
+    start = jnp.where(lane < half_width, starts[0], starts[1])
+    positions = start + jnp.arange(rows, dtype=jnp.int32)[:, None]
+    angles = positions.astype(jnp.float32) * jnp.concatenate([inverse_freq, inverse_freq])[None, :]
+    return jnp.cos(angles), jnp.sin(angles)
 
 
 def on_device(
@@ -462,7 +476,7 @@
     later = run(jobs[:1], core)
     run(jobs[1:] + [(0, chunk) for chunk in range(chunks)], later)
 
-    turn = tables(jnp.concatenate(starts), block_len)
+    cosine, sine = tables((starts[0][0], starts[-1][0]), block_len)
     mine = (wanted == side).astype(jnp.int32)
     before = jnp.cumsum(mine)
     names = jnp.arange(groups, dtype=jnp.int32)
@@ -502,7 +516,7 @@
 
     result = None
     for chunk in range(chunks):
-        outs = attend(order, place, own[chunk], turn, q_all, received[chunk], chunk * split, per, keep)
+        outs = attend(order, place, own[chunk], cosine, sine, q_all, received[chunk], chunk * split, per, keep)
         outs, order = lax.optimization_barrier((outs, order))
         arrived = [
             lax.ppermute(outs[2 + far - 1], "grp", [(i, i ^ (far * split)) for i in range(groups)])

time: 133 us -> 128 us (0.962)
  Pallas kernels: 51.8 us -> 47.7 us
  waiting for transfers between devices: 16.2 us -> 19.2 us
  other arithmetic: 8.2 us -> 5.97 us
  starting transfers between devices: 21.6 us -> 19.8 us
    pallas_call x2, Pallas kernels: 34.6 us -> 30 us  [project(): pl.pallas_call(functools.partial(project_kernel, plan, split, pieces), ou...]
    cos x1 -> x0, other arithmetic: 3.69 us -> none  [tables(): cosine = jnp.cos(angles)]
    sin x0 -> x1, other arithmetic: none -> 1.87 us  [tables(): return (jnp.cos(angles), jnp.sin(angles))]
    all_gather x1, waiting for transfers between devices: 0.02 us -> 1.85 us  [on_device(): q_all = lax.all_gather(jnp.concatenate([turned, tag], 0), 'grp')]
    ppermute x6, starting transfers between devices: 8.67 us -> 6.96 us  [on_device(): lax.ppermute(sends[number - 1], 'grp', [(i, partner(i, number // split, n...]
    ppermute x6, waiting for transfers between devices: 11.1 us -> 12.6 us  [on_device(): lax.ppermute(outs[2 + far - 1], 'grp', [(i, i ^ far * split) for i in ran...]
    unnamed x19 -> x18, local copies, waits for them, and re-layouts: 4.5 us -> 4.49 us
  transfers between devices with their start and end apart: 20 -> 20, of which waited for: 5 -> 6; matrix products, arithmetic and copies ran while one was open for 16% -> 15% of each run, Pallas kernels for 39% -> 37%
where the time goes in v4:
time: 128 us; the launch traced here: 127 us
  Pallas kernels  47.7 us (37%)
  starting transfers between devices  19.8 us (15%)
  waiting for transfers between devices  19.2 us (15%)
  between operations  15 us (12%)
  matrix products  10.7 us (8%)
  local copies, waits for them, and re-layouts  8.78 us (7%)
  other arithmetic  5.97 us (5%)
    pallas_call x2, Pallas kernels, project(): pl.pallas_call(functools.partial(project_kernel, plan, split, pieces), ou...  30 us
    pallas_call x2, Pallas kernels, attend(): pl.pallas_call(functools.partial(attend_kernel, layout, per, slots, keep,...  15.4 us
    ppermute x6, waiting for transfers between devices, on_device(): lax.ppermute(outs[2 + far - 1], 'grp', [(i, i ^ far * split) for i in ran...  12.6 us
    ppermute x6, starting transfers between devices, on_device(): lax.ppermute(outs[2 + far - 1], 'grp', [(i, i ^ far * split) for i in ran...  7.11 us
    ppermute x6, starting transfers between devices, on_device(): lax.ppermute(sends[number - 1], 'grp', [(i, partner(i, number // split, n...  6.96 us
    dot_general x1, matrix products, on_device(): jnp.einsum('rkgd,rktd->rkgt', grouped, cache_keys, preferred_element_type...  5.8 us
    ppermute x6, starting transfers between devices, exchange(): return lax.ppermute(array, ('grp', 'tp'), pairs)  5.19 us
    dot_general x1, matrix products, on_device(): jnp.einsum('rkgt,rktd->rkgd', cache_weights.astype(jnp.bfloat16), cache_v...  4.89 us
  transfers between devices with their start and end apart: 20, of which 6 were waited for; matrix products, arithmetic and copies ran while one was open for 15% of the time, Pallas kernels for 37%

profile of v4, /device:TPU:0, one launch (start us, length us, event | category | flops | bytes accessed | tf_op | source)
XLA Modules:
  0.0 127.0 jit_solution(11691800366335198009)
XLA Ops:
  7.2 1.1 copy.53
  8.4 0.7 concatenate.9.clone
  10.4 8.7 %project.2 = (s16[1040,256]{1,0:T(8,128)(2,1)}, s16[1040,256]{1,0:T(8,128)(2,1)}) custom-call(s32[2]{0:T(128)} %pad_add_fusion.place_ref, bf16[1024,4096]{1,0:T(8,128)(2,1)} %x_hbm.3, bf16[4096,1024]{1,0:T(8,128)(2,1)} %wk_hbm.3, bf16[4096,1024]{1,0:T(8,128)(2,1)} %wv_hbm.3), custom_call_target="tpu_custom_call" | custom-call | flops 4294967296 | bytes 13631488 | tf_op jit(solution)/shard_map/project/pallas_call | solution.py:109
  19.1 2.6 %collective-permute-start.1 = (s16[1040,256]{1,0:T(8,128)(2,1)}, s16[1040,256]{1,0:T(8,128)(2,1)S(1)}, u32[]{:S(2)}, u32[]{:S(2)}) collective-permute-start(s16[1040,256]{1,0:T(8,128)(2,1)} %get-tuple-element.82), channel_id=1, source_target_pairs={{0,1},{1,0},{2,3},{3,2},{4,5},{5,4},{6,7},{7,6},{8,9},{9,8},{10,11... | collective-permute-start | bytes 1597448 | tf_op jit(solution)/shard_map/ppermute | solution.py:447
  22.5 21.3 %project.3 = (s16[1040,256]{1,0:T(8,128)(2,1)}, s16[1040,256]{1,0:T(8,128)(2,1)}, f32[1024,128]{1,0:T(8,128)}, f32[1024,128]{1,0:T(8,128)}, s16[1040,256]{1,0:T(...) custom-call(s32[4]{0:T(128)} %pad_add_fusion.1.place_ref, ...), custom_call_target="tpu_custom_call" | custom-call | flops 12884901888 | bytes 24117248 | tf_op jit(solution)/shard_map/project/pallas_call | solution.py:109
  43.9 1.9 %collective-permute-start.4 = (s16[1040,256]{1,0:T(8,128)(2,1)}, s16[1040,256]{1,0:T(8,128)(2,1)S(1)}, u32[]{:S(2)}, u32[]{:S(2)}) collective-permute-start(s16[1040,256]{1,0:T(8,128)(2,1)} %get-tuple-element.93), channel_id=1, source_target_pairs={{0,1},{1,0},{2,3},{3,2},{4,5},{5,4},{6,7},{7,6},{8,9},{9,8},{10,11... | collective-permute-start | bytes 1597448 | tf_op jit(solution)/shard_map/ppermute | solution.py:447
  46.6 5.8 %fusion.17 = (f32[32,4,8]{2,1,0:T(4,128)S(1)}, f32[32,4,8,256]{3,2,1,0:T(8,128)S(1)}) fusion(bf16[32,4,8,128]{3,2,1,0:T(8,128)(2,1)S(1)} %bitcast.42, bf16[32,4,256,128]{3,2,1,0:T(8,128)(2,1)} %param.15, pred[32,256]{1,0:T(8,128)(4,1)S(1)} %iota_compare_fusion), kind=kOutput, calls=%fused_computation.48 | convolution fusion | flops 67894272 | bytes 9711616 | tf_op jit(solution)/shard_map/rkgd,rktd->rkgt/dot_general | solution.py:493
  53.2 4.9 %fusion.1 = f32[4,128,32,8]{1,3,0,2:T(8,128)S(1)} fusion(bf16[32,4,256,128]{3,2,1,0:T(8,128)(2,1)} %param.16, f32[32,4,8,256]{3,2,1,0:T(8,128)S(1)} %get-tuple-element.128, f32[32,4,8]{2,1,0:T(4,128)S(1)} %get-tuple-element.127, pred[32,256]{1,0:T(8,128)(4,1)S(1)} %iota_compare_fusion, f32[4,32,8]{2,0,1:T(4,128)S(1)} %copy.37), kind=kOutput, calls=%fused_computation.3 | convolution fusion | flops 68026368 | bytes 9977856 | tf_op jit(solution)/shard_map/rkgt,rktd->rkgd/dot_general | solution.py:501
  58.1 0.8 copy.51
  59.9 1.9 %fusion.5 = (f32[1024,128]{1,0:T(8,128)S(1)}, f32[1024,128]{1,0:T(8,128)S(1)}) fusion(f32[128]{0:T(128)S(1)} %pad_maximum_fusion, s32[128]{0:T(128)S(1)} %compare_select_fusion.2), kind=kLoop, calls=%fused_computation.9 | loop fusion | flops 393216 | bytes 1049600 | tf_op jit(solution)/shard_map/sin | solution.py:402
  61.8 1.9 %all-gather.3.cloned.1.call-done = bf16[8448,256]{1,0:T(8,128)(2,1)} async-done(((bf16[528,256]{1,0:T(8,128)(2,1)}), bf16[8448,256]{1,0:T(8,128)(2,1)}) %all-gather.3.cloned.1.call-update) | async-done | bytes 4325392 | tf_op jit(solution)/shard_map/all_gather | solution.py:437
  63.6 1.1 compare_reduce_fusion
  65.5 2.2 %copy-done = bf16[8448,256]{1,0:T(8,128)(2,1)S(1)} copy-done((bf16[8448,256]{1,0:T(8,128)(2,1)S(1)}, bf16[8448,256]{1,0:T(8,128)(2,1)}, u32[]{:S(2)}) %copy-start) | copy-done | bytes 4325400
  67.7 1.0 copy-done.4
  68.8 1.0 copy-done.5
  69.8 7.1 %attend.2 = (f32[4,128,256]{2,1,0:T(8,128)S(1)}, f32[4,8,256]{2,1,0:T(8,128)S(1)}, bf16[4,144,256]{2,1,0:T(8,128)(2,1)S(1)}, bf16[4,144,256]{2,1,0:T(8,128)(2,1)S(1)}, bf16[4,144,256]{2,1,0:T(8,128)(2,1)S(1)}) custom-call(s32[17]{0:T(128)S(1)} %pad_add_fusion.2.order_ref, s32[16]{0:T(128)S(1)} %fusion.14.place_ref, f32[1024,128]{1,0:T(8,128)S(1)} %copy-done.4, ...), custom_call_target="tpu_custom_call" | custom-call | flops 4294967296 | bytes 6291456 | tf_op jit(solution)/shard_map/attend/pallas_call | solution.py:263
  77.5 1.5 %collective-permute-start.14 = (bf16[4,144,256]{2,1,0:T(8,128)(2,1)S(1)}, bf16[4,144,256]{2,1,0:T(8,128)(2,1)S(1)}, u32[]{:S(2)}, u32[]{:S(2)}) collective-permute-start(bf16[4,144,256]{2,1,0:T(8,128)(2,1)S(1)} %get-tuple-element.116), channel_id=1, source_target_pairs={{0,8},{2,10},{4,12},{6,14},{8,0},{10,2},{12,4},{14,6},{16,24},{18,... | collective-permute-start | bytes 884744 | tf_op jit(solution)/shard_map/ppermute | solution.py:522
  79.0 1.4 %collective-permute-start.15 = (bf16[4,144,256]{2,1,0:T(8,128)(2,1)S(1)}, bf16[4,144,256]{2,1,0:T(8,128)(2,1)S(1)}, u32[]{:S(2)}, u32[]{:S(2)}) collective-permute-start(bf16[4,144,256]{2,1,0:T(8,128)(2,1)S(1)} %get-tuple-element.117), channel_id=1, source_target_pairs={{0,12},{2,14},{4,8},{6,10},{8,4},{10,6},{12,0},{14,2},{16,28},{18,... | collective-permute-start | bytes 884744 | tf_op jit(solution)/shard_map/ppermute | solution.py:522
  80.5 8.3 %attend.3 = (f32[4,128,256]{2,1,0:T(8,128)S(1)}, f32[4,8,256]{2,1,0:T(8,128)S(1)}, bf16[4,144,256]{2,1,0:T(8,128)(2,1)S(1)}, bf16[4,144,256]{2,1,0:T(8,128)(2,1)S(1)}, bf16[4,144,256]{2,1,0:T(8,128)(2,1)S(1)}) custom-call(s32[17]{0:T(128)S(1)} %pad_add_fusion.2.order_ref, s32[16]{0:T(128)S(1)} %fusion.14.place_ref, f32[1024,128]{1,0:T(8,128)S(1)} %copy-done.2, ...), custom_call_target="tpu_custom_call" | custom-call | flops 4294967296 | bytes 6291456 | tf_op jit(solution)/shard_map/attend/pallas_call | solution.py:263
  89.5 1.5 %collective-permute-start.8 = (bf16[4,144,256]{2,1,0:T(8,128)(2,1)S(1)}, bf16[4,144,256]{2,1,0:T(8,128)(2,1)S(1)}, u32[]{:S(2)}, u32[]{:S(2)}) collective-permute-start(bf16[4,144,256]{2,1,0:T(8,128)(2,1)S(1)} %get-tuple-element.104), channel_id=1, source_target_pairs={{0,8},{2,10},{4,12},{6,14},{8,0},{10,2},{12,4},{14,6},{16,24},{18,... | collective-permute-start | bytes 884744 | tf_op jit(solution)/shard_map/ppermute | solution.py:522
  91.0 1.4 %collective-permute-start.9 = (bf16[4,144,256]{2,1,0:T(8,128)(2,1)S(1)}, bf16[4,144,256]{2,1,0:T(8,128)(2,1)S(1)}, u32[]{:S(2)}, u32[]{:S(2)}) collective-permute-start(bf16[4,144,256]{2,1,0:T(8,128)(2,1)S(1)} %get-tuple-element.105), channel_id=1, source_target_pairs={{0,12},{2,14},{4,8},{6,10},{8,4},{10,6},{12,0},{14,2},{16,28},{18,... | collective-permute-start | bytes 884744 | tf_op jit(solution)/shard_map/ppermute | solution.py:522
  92.4 2.3 %collective-permute-done.15.rest_2_ = bf16[4,144,256]{2,1,0:T(8,128)(2,1)S(1)} collective-permute-done((bf16[4,144,256]{2,1,0:T(8,128)(2,1)S(1)}, bf16[4,144,256]{2,1,0:T(8,128)(2,1)S(1)}, u32[]{:S(2)}, u32[]{:S(2)}) %collective-permute-start.15) | collective-permute-done | bytes 294944 | tf_op jit(solution)/shard_map/ppermute | solution.py:522
  95.1 1.9 %collective-permute-start.17 = (bf16[144,256]{1,0:T(8,128)(2,1)S(1)}, bf16[144,256]{1,0:T(8,128)(2,1)S(1)}, u32[]{:S(2)}, u32[]{:S(2)}) collective-permute-start(bf16[144,256]{1,0:T(8,128)(2,1)S(1)} %get-tuple-element.121), channel_id=1, source_target_pairs={{0,16},{2,18},{4,20},{6,22},{8,24},{10,26},{12,28},{14,30},{16,0},... | collective-permute-start | bytes 221192 | tf_op jit(solution)/shard_map/ppermute | solution.py:527
  96.9 3.1 %collective-permute-done.7.rest_0_ = bf16[4,144,256]{2,1,0:T(8,128)(2,1)S(1)} collective-permute-done((bf16[4,144,256]{2,1,0:T(8,128)(2,1)S(1)}, bf16[4,144,256]{2,1,0:T(8,128)(2,1)S(1)}, u32[]{:S(2)}, u32[]{:S(2)}) %collective-permute-start.7) | collective-permute-done | bytes 294944 | tf_op jit(solution)/shard_map/ppermute | solution.py:522
  100.0 2.2 %collective-permute-start.18 = (bf16[144,256]{1,0:T(8,128)(2,1)S(1)}, bf16[144,256]{1,0:T(8,128)(2,1)S(1)}, u32[]{:S(2)}, u32[]{:S(2)}) collective-permute-start(bf16[144,256]{1,0:T(8,128)(2,1)S(1)} %get-tuple-element.122), channel_id=1, source_target_pairs={{0,18},{2,16},{4,22},{6,20},{8,26},{10,24},{12,30},{14,28},{16,2},... | collective-permute-start | bytes 221192 | tf_op jit(solution)/shard_map/ppermute | solution.py:527
  102.3 7.2 %collective-permute-done.9.rest_2_ = bf16[4,144,256]{2,1,0:T(8,128)(2,1)S(1)} collective-permute-done((bf16[4,144,256]{2,1,0:T(8,128)(2,1)S(1)}, bf16[4,144,256]{2,1,0:T(8,128)(2,1)S(1)}, u32[]{:S(2)}, u32[]{:S(2)}) %collective-permute-start.9) | collective-permute-done | bytes 294944 | tf_op jit(solution)/shard_map/ppermute | solution.py:522
  110.0 2.7 %collective-permute-start.12 = (bf16[144,256]{1,0:T(8,128)(2,1)S(1)}, bf16[144,256]{1,0:T(8,128)(2,1)S(1)}, u32[]{:S(2)}, u32[]{:S(2)}) collective-permute-start(bf16[144,256]{1,0:T(8,128)(2,1)S(1)} %get-tuple-element.110), channel_id=1, source_target_pairs={{0,18},{2,16},{4,22},{6,20},{8,26},{10,24},{12,30},{14,28},{16,2},... | collective-permute-start | bytes 221192 | tf_op jit(solution)/shard_map/ppermute | solution.py:527
  112.7 1.2 copy.45.rest_3_
  113.9 0.8 finish.2.rest_5_
  114.7 3.1 %collective-permute-done.11.rest_1_ = bf16[144,256]{1,0:T(8,128)(2,1)S(1)} collective-permute-done((bf16[144,256]{1,0:T(8,128)(2,1)S(1)}, bf16[144,256]{1,0:T(8,128)(2,1)S(1)}, u32[]{:S(2)}, u32[]{:S(2)}) %collective-permute-start.11) | collective-permute-done | bytes 73760 | tf_op jit(solution)/shard_map/ppermute | solution.py:527
  117.9 1.5 %collective-permute-done.12.rest_2_ = bf16[144,256]{1,0:T(8,128)(2,1)S(1)} collective-permute-done((bf16[144,256]{1,0:T(8,128)(2,1)S(1)}, bf16[144,256]{1,0:T(8,128)(2,1)S(1)}, u32[]{:S(2)}, u32[]{:S(2)}) %collective-permute-start.12) | collective-permute-done | bytes 73760 | tf_op jit(solution)/shard_map/ppermute | solution.py:527
  119.4 0.8 finish.3
  (63 shorter events, 6.8 us)
Async XLA Ops:
  6.5 57.1 %all-gather.3.cloned.1.call-start = ((), (), s32[]{:S(2)}) async-start(), calls=%async_computation | async-start | bytes 4595712 | tf_op jit(solution)/shard_map/all_gather | solution.py:437
  9.2 50.0 %collective-permute-start = (s32[1]{0:T(128)}, s32[1]{0:T(128)}, u32[]{:S(2)}, u32[]{:S(2)}) collective-permute-start(s32[1]{0:T(128)} %param.12), channel_id=1, source_target_pairs={{0,2},{2,0},{4,6},{6,4},{8,10},{10,8},{12,14},{14,12},{16,18},{18,... | collective-permute-start | bytes 20 | tf_op jit(solution)/shard_map/ppermute | solution.py:440
  19.1 45.9 %collective-permute-start.1 = (s16[1040,256]{1,0:T(8,128)(2,1)}, s16[1040,256]{1,0:T(8,128)(2,1)S(1)}, u32[]{:S(2)}, u32[]{:S(2)}) collective-permute-start(s16[1040,256]{1,0:T(8,128)(2,1)} %get-tuple-element.82), channel_id=1, source_target_pairs={{0,1},{1,0},{2,3},{3,2},{4,5},{5,4},{6,7},{7,6},{8,9},{9,8},{10,11... | collective-permute-start | bytes 1597448 | tf_op jit(solution)/shard_map/ppermute | solution.py:447
  21.7 43.8 %collective-permute-start.2 = (s16[1040,256]{1,0:T(8,128)(2,1)}, s16[1040,256]{1,0:T(8,128)(2,1)S(1)}, u32[]{:S(2)}, u32[]{:S(2)}) collective-permute-start(s16[1040,256]{1,0:T(8,128)(2,1)} %get-tuple-element.83), channel_id=1, source_target_pairs={{0,3},{1,2},{2,1},{3,0},{4,7},{5,6},{6,5},{7,4},{8,11},{9,10},{10,... | collective-permute-start | bytes 1597448 | tf_op jit(solution)/shard_map/ppermute | solution.py:447
  22.5 24.0 %copy-start.7 = (s32[32]{0:T(128)S(1)}, s32[32]{0:T(128)}, u32[]{:S(2)}) copy-start(s32[32]{0:T(128)} %param.17) | copy-start | bytes 388
  22.5 24.1 %copy-start.6 = (bf16[32,32,128]{2,1,0:T(8,128)(2,1)S(1)}, bf16[32,32,128]{2,1,0:T(8,128)(2,1)}, u32[]{:S(2)}) copy-start(bf16[32,32,128]{2,1,0:T(8,128)(2,1)} %param.14) | copy-start | bytes 786436
  43.8 21.7 %collective-permute-start.3 = (s16[1040,256]{1,0:T(8,128)(2,1)}, s16[1040,256]{1,0:T(8,128)(2,1)S(1)}, u32[]{:S(2)}, u32[]{:S(2)}) collective-permute-start(s16[1040,256]{1,0:T(8,128)(2,1)} %get-tuple-element.84), channel_id=1, source_target_pairs={{0,2},{1,3},{2,0},{3,1},{4,6},{5,7},{6,4},{7,5},{8,10},{9,11},{10,... | collective-permute-start | bytes 1597448 | tf_op jit(solution)/shard_map/ppermute | solution.py:447
  43.9 35.1 %collective-permute-start.4 = (s16[1040,256]{1,0:T(8,128)(2,1)}, s16[1040,256]{1,0:T(8,128)(2,1)S(1)}, u32[]{:S(2)}, u32[]{:S(2)}) collective-permute-start(s16[1040,256]{1,0:T(8,128)(2,1)} %get-tuple-element.93), channel_id=1, source_target_pairs={{0,1},{1,0},{2,3},{3,2},{4,5},{5,4},{6,7},{7,6},{8,9},{9,8},{10,11... | collective-permute-start | bytes 1597448 | tf_op jit(solution)/shard_map/ppermute | solution.py:447
  59.2 21.3 %collective-permute-start.5 = (s16[1040,256]{1,0:T(8,128)(2,1)}, s16[1040,256]{1,0:T(8,128)(2,1)}, u32[]{:S(2)}, u32[]{:S(2)}) collective-permute-start(s16[1040,256]{1,0:T(8,128)(2,1)} %get-tuple-element.94), channel_id=1, source_target_pairs={{0,3},{1,2},{2,1},{3,0},{4,7},{5,6},{6,5},{7,4},{8,11},{9,10},{10,... | collective-permute-start | bytes 1597448 | tf_op jit(solution)/shard_map/ppermute | solution.py:447
  65.1 15.4 %collective-permute-start.6 = (s16[1040,256]{1,0:T(8,128)(2,1)}, s16[1040,256]{1,0:T(8,128)(2,1)S(1)}, u32[]{:S(2)}, u32[]{:S(2)}) collective-permute-start(s16[1040,256]{1,0:T(8,128)(2,1)} %get-tuple-element.95), channel_id=1, source_target_pairs={{0,2},{1,3},{2,0},{3,1},{4,6},{5,7},{6,4},{7,5},{8,10},{9,11},{10,... | collective-permute-start | bytes 1597448 | tf_op jit(solution)/shard_map/ppermute | solution.py:447
  65.5 2.2 %copy-start = (bf16[8448,256]{1,0:T(8,128)(2,1)S(1)}, bf16[8448,256]{1,0:T(8,128)(2,1)}, u32[]{:S(2)}) copy-start(bf16[8448,256]{1,0:T(8,128)(2,1)} %all-gather.3.cloned.1.call-done) | copy-start | bytes 12976132
  67.7 1.0 copy-start.4
  68.8 1.0 copy-start.5
  69.8 10.7 %copy-start.1 = (bf16[8448,256]{1,0:T(8,128)(2,1)S(1)}, bf16[8448,256]{1,0:T(8,128)(2,1)}, u32[]{:S(2)}) copy-start(bf16[8448,256]{1,0:T(8,128)(2,1)} %all-gather.3.cloned.1.call-done) | copy-start | bytes 12976132
  69.8 10.7 %copy-start.2 = (f32[1024,128]{1,0:T(8,128)S(1)}, f32[1024,128]{1,0:T(8,128)}, u32[]{:S(2)}) copy-start(f32[1024,128]{1,0:T(8,128)} %get-tuple-element.91.own_key) | copy-start | bytes 1572868
  69.8 10.7 %copy-start.3 = (f32[1024,128]{1,0:T(8,128)S(1)}, f32[1024,128]{1,0:T(8,128)}, u32[]{:S(2)}) copy-start(f32[1024,128]{1,0:T(8,128)} %get-tuple-element.92.own_value) | copy-start | bytes 1572868
  76.9 14.0 %collective-permute-start.13 = (bf16[4,144,256]{2,1,0:T(8,128)(2,1)S(1)}, bf16[4,144,256]{2,1,0:T(8,128)(2,1)S(1)}, u32[]{:S(2)}, u32[]{:S(2)}) collective-permute-start(bf16[4,144,256]{2,1,0:T(8,128)(2,1)S(1)} %get-tuple-element.115), channel_id=1, source_target_pairs={{0,4},{2,6},{4,0},{6,2},{8,12},{10,14},{12,8},{14,10},{16,20},{18,... | collective-permute-start | bytes 884744 | tf_op jit(solution)/shard_map/ppermute | solution.py:522
  77.5 14.9 %collective-permute-start.14 = (bf16[4,144,256]{2,1,0:T(8,128)(2,1)S(1)}, bf16[4,144,256]{2,1,0:T(8,128)(2,1)S(1)}, u32[]{:S(2)}, u32[]{:S(2)}) collective-permute-start(bf16[4,144,256]{2,1,0:T(8,128)(2,1)S(1)} %get-tuple-element.116), channel_id=1, source_target_pairs={{0,8},{2,10},{4,12},{6,14},{8,0},{10,2},{12,4},{14,6},{16,24},{18,... | collective-permute-start | bytes 884744 | tf_op jit(solution)/shard_map/ppermute | solution.py:522
  79.0 15.7 %collective-permute-start.15 = (bf16[4,144,256]{2,1,0:T(8,128)(2,1)S(1)}, bf16[4,144,256]{2,1,0:T(8,128)(2,1)S(1)}, u32[]{:S(2)}, u32[]{:S(2)}) collective-permute-start(bf16[4,144,256]{2,1,0:T(8,128)(2,1)S(1)} %get-tuple-element.117), channel_id=1, source_target_pairs={{0,12},{2,14},{4,8},{6,10},{8,4},{10,6},{12,0},{14,2},{16,28},{18,... | collective-permute-start | bytes 884744 | tf_op jit(solution)/shard_map/ppermute | solution.py:522
  88.9 11.2 %collective-permute-start.7 = (bf16[4,144,256]{2,1,0:T(8,128)(2,1)S(1)}, bf16[4,144,256]{2,1,0:T(8,128)(2,1)S(1)}, u32[]{:S(2)}, u32[]{:S(2)}) collective-permute-start(bf16[4,144,256]{2,1,0:T(8,128)(2,1)S(1)} %get-tuple-element.103), channel_id=1, source_target_pairs={{0,4},{2,6},{4,0},{6,2},{8,12},{10,14},{12,8},{14,10},{16,20},{18,... | collective-permute-start | bytes 884744 | tf_op jit(solution)/shard_map/ppermute | solution.py:522
  89.5 12.8 %collective-permute-start.8 = (bf16[4,144,256]{2,1,0:T(8,128)(2,1)S(1)}, bf16[4,144,256]{2,1,0:T(8,128)(2,1)S(1)}, u32[]{:S(2)}, u32[]{:S(2)}) collective-permute-start(bf16[4,144,256]{2,1,0:T(8,128)(2,1)S(1)} %get-tuple-element.104), channel_id=1, source_target_pairs={{0,8},{2,10},{4,12},{6,14},{8,0},{10,2},{12,4},{14,6},{16,24},{18,... | collective-permute-start | bytes 884744 | tf_op jit(solution)/shard_map/ppermute | solution.py:522
  91.0 18.5 %collective-permute-start.9 = (bf16[4,144,256]{2,1,0:T(8,128)(2,1)S(1)}, bf16[4,144,256]{2,1,0:T(8,128)(2,1)S(1)}, u32[]{:S(2)}, u32[]{:S(2)}) collective-permute-start(bf16[4,144,256]{2,1,0:T(8,128)(2,1)S(1)} %get-tuple-element.105), channel_id=1, source_target_pairs={{0,12},{2,14},{4,8},{6,10},{8,4},{10,6},{12,0},{14,2},{16,28},{18,... | collective-permute-start | bytes 884744 | tf_op jit(solution)/shard_map/ppermute | solution.py:522
  95.0 15.0 %collective-permute-start.16 = (bf16[144,256]{1,0:T(8,128)(2,1)S(1)}, bf16[144,256]{1,0:T(8,128)(2,1)S(1)}, u32[]{:S(2)}, u32[]{:S(2)}) collective-permute-start(bf16[144,256]{1,0:T(8,128)(2,1)S(1)} %get-tuple-element.120), channel_id=1, source_target_pairs={{0,2},{2,0},{4,6},{6,4},{8,10},{10,8},{12,14},{14,12},{16,18},{18,... | collective-permute-start | bytes 221192 | tf_op jit(solution)/shard_map/ppermute | solution.py:527
  95.1 18.8 %collective-permute-start.17 = (bf16[144,256]{1,0:T(8,128)(2,1)S(1)}, bf16[144,256]{1,0:T(8,128)(2,1)S(1)}, u32[]{:S(2)}, u32[]{:S(2)}) collective-permute-start(bf16[144,256]{1,0:T(8,128)(2,1)S(1)} %get-tuple-element.121), channel_id=1, source_target_pairs={{0,16},{2,18},{4,20},{6,22},{8,24},{10,26},{12,28},{14,30},{16,0},... | collective-permute-start | bytes 221192 | tf_op jit(solution)/shard_map/ppermute | solution.py:527
  100.0 13.9 %collective-permute-start.18 = (bf16[144,256]{1,0:T(8,128)(2,1)S(1)}, bf16[144,256]{1,0:T(8,128)(2,1)S(1)}, u32[]{:S(2)}, u32[]{:S(2)}) collective-permute-start(bf16[144,256]{1,0:T(8,128)(2,1)S(1)} %get-tuple-element.122), channel_id=1, source_target_pairs={{0,18},{2,16},{4,22},{6,20},{8,26},{10,24},{12,30},{14,28},{16,2},... | collective-permute-start | bytes 221192 | tf_op jit(solution)/shard_map/ppermute | solution.py:527
  109.8 4.9 %collective-permute-start.10 = (bf16[144,256]{1,0:T(8,128)(2,1)S(1)}, bf16[144,256]{1,0:T(8,128)(2,1)S(1)}, u32[]{:S(2)}, u32[]{:S(2)}) collective-permute-start(bf16[144,256]{1,0:T(8,128)(2,1)S(1)} %get-tuple-element.108), channel_id=1, source_target_pairs={{0,2},{2,0},{4,6},{6,4},{8,10},{10,8},{12,14},{14,12},{16,18},{18,... | collective-permute-start | bytes 221192 | tf_op jit(solution)/shard_map/ppermute | solution.py:527
  109.9 8.0 %collective-permute-start.11 = (bf16[144,256]{1,0:T(8,128)(2,1)S(1)}, bf16[144,256]{1,0:T(8,128)(2,1)S(1)}, u32[]{:S(2)}, u32[]{:S(2)}) collective-permute-start(bf16[144,256]{1,0:T(8,128)(2,1)S(1)} %get-tuple-element.109), channel_id=1, source_target_pairs={{0,16},{2,18},{4,20},{6,22},{8,24},{10,26},{12,28},{14,30},{16,0},... | collective-permute-start | bytes 221192 | tf_op jit(solution)/shard_map/ppermute | solution.py:527
  110.0 9.4 %collective-permute-start.12 = (bf16[144,256]{1,0:T(8,128)(2,1)S(1)}, bf16[144,256]{1,0:T(8,128)(2,1)S(1)}, u32[]{:S(2)}, u32[]{:S(2)}) collective-permute-start(bf16[144,256]{1,0:T(8,128)(2,1)S(1)} %get-tuple-element.110), channel_id=1, source_target_pairs={{0,18},{2,16},{4,22},{6,20},{8,26},{10,24},{12,30},{14,28},{16,2},... | collective-permute-start | bytes 221192 | tf_op jit(solution)/shard_map/ppermute | solution.py:527
Sparse Core Ops, SparseCore 0:
  9.6 53.9 all-gather.2

commit v5 on v4

--- a/solution.py
+++ b/solution.py
@@ -126,9 +126,7 @@
         ),
         compiler_params=pltpu.CompilerParams(vmem_limit_bytes=BIG),
         cost_estimate=pl.CostEstimate(
-            flops=4 * rows * depth * width * steps,
-            bytes_accessed=2 * rows * depth + steps * (4 * depth * width + 4 * rows * width),
-            transcendentals=0,
+            flops=rows * depth, bytes_accessed=rows * depth // 4, transcendentals=0
         ),
         name="project",
     )(place, x, wk, wv)
@@ -245,7 +243,7 @@
             send_ref[slot, HD:] = stats
 
 
-def attend(order, place, own, cosine, sine, q_all, received, head, per, keep):
+def attend(order, place, own, cosine, sine, q_all, received, per, keep):
     rows = own[0].shape[0]
     slots, _, wide = q_all.shape
     blocks = len(received)
@@ -271,7 +269,7 @@
                 whole((rows, HD)),
                 whole((rows, HD)),
                 whole((rows, HD)),
-                pl.BlockSpec((slots, HD, wide), lambda i, a, b: (0, head + a[slots], 0)),
+                pl.BlockSpec((slots, HD, wide), lambda i, a, b: (0, 0, 0)),
             ]
             + [whole(part.shape) for part in flat],
             out_specs=tuple(whole(shape.shape) for shape in shapes),
@@ -286,9 +284,7 @@
         ),
         compiler_params=pltpu.CompilerParams(vmem_limit_bytes=2 * SMALL),
         cost_estimate=pl.CostEstimate(
-            flops=8 * per * blocks * rows * wide * HD,
-            bytes_accessed=blocks * rows * HD * 16 + slots * HD * wide * 4,
-            transcendentals=per * blocks * rows * wide,
+            flops=rows * HD, bytes_accessed=rows * HD, transcendentals=0
         ),
         name="attend",
     )(order, place, *own, cosine, sine, q_all, *flat)
@@ -432,13 +428,30 @@
     side = me // per
 
     grouped = queries.reshape(row_count, kv_local, group_size, HD)
-    turned = grouped.transpose(1, 3, 0, 2).reshape(kv_local * HD, wide)
-    tag = jnp.broadcast_to(matching[0].astype(jnp.bfloat16), (STAT_ROWS, wide))
-    q_all = lax.all_gather(jnp.concatenate([turned, tag], 0), "grp")
-    wanted = q_all[:, kv_local * HD, 0].astype(jnp.int32)
-    starts = [offsets] + [
-        lax.ppermute(offsets, "grp", [(i, i ^ apart) for i in range(groups)]) for apart in range(1, split)
+    turned = grouped.reshape(row_count, chunks, split, group_size, HD).transpose(2, 1, 4, 0, 3)
+    turned = turned.reshape(split, chunks * HD, wide)
+    line = jnp.arange(STAT_ROWS, dtype=jnp.int32)[:, None]
+    tag = jnp.where(line == 0, matching[0], offsets[0]).astype(jnp.bfloat16)
+    tag = jnp.broadcast_to(tag, (split, STAT_ROWS, wide))
+    turned = jnp.concatenate([turned[:, :HD], tag, turned[:, HD:]], 1)
+    own_queries = [lax.dynamic_index_in_dim(turned, core, 0, False)] + [
+        lax.ppermute(
+            lax.dynamic_index_in_dim(turned, core ^ apart, 0, False),
+            "grp",
+            [(i, i ^ apart) for i in range(groups)],
+        )
+        for apart in range(1, split)
     ]
+    first = HD + STAT_ROWS
+    cuts = [(0, first)] + [(first + chunk * HD, first + (chunk + 1) * HD) for chunk in range(chunks - 1)]
+    pieces = [jnp.stack([each[low:high] for each in own_queries]) for low, high in cuts]
+    members = [[chip * split + c for chip in range(groups // split)] for c in range(split)]
+    gathered = [
+        lax.all_gather(piece, "grp", axis_index_groups=members).reshape(groups, -1, wide)
+        for piece in pieces
+    ]
+    starts = jnp.stack([each[HD + 1, 0] for each in own_queries]).astype(jnp.int32)
+    own_queries, core = lax.optimization_barrier((own_queries, core))
 
     def exchange(array, shift, apart):
         pairs = [
@@ -462,7 +475,7 @@
             ["own" if shift == 0 else "send" for shift, _ in jobs],
             split,
         )
-        results, core = lax.optimization_barrier((results, core))
+        _, core = lax.optimization_barrier((results, core))
         for (shift, chunk), outs in zip(jobs, results):
             if shift == 0:
                 own[chunk] = outs[:2]
@@ -476,17 +489,32 @@
     later = run(jobs[:1], core)
     run(jobs[1:] + [(0, chunk) for chunk in range(chunks)], later)
 
-    cosine, sine = tables((starts[0][0], starts[-1][0]), block_len)
+    gathered[0], received[0] = lax.optimization_barrier((gathered[0], received[0]))
+    wanted = gathered[0][:, HD, 0].astype(jnp.int32)
+    cosine, sine = tables((starts[0], starts[-1]), block_len)
     mine = (wanted == side).astype(jnp.int32)
     before = jnp.cumsum(mine)
     names = jnp.arange(groups, dtype=jnp.int32)
     target = jnp.where(mine == 1, before - 1, per + names - before)
     order = jnp.sum(jnp.where(target[None, :] == names[:, None], names[None, :], 0), 1).astype(jnp.int32)
     away = ((order // split) % homes) ^ spot
-    place = (away * PROMPTS + ((order // per) ^ side)) * split + (order % split ^ core)
-    order = jnp.concatenate([order, core.reshape(1)])
-
-    grouped, own[-1] = lax.optimization_barrier((grouped, own[-1]))
+    place = (away * PROMPTS + ((order // per) ^ side)) * split + order % split
+
+    def partner(i, side_apart, apart):
+        return (i + side_apart * per) % groups ^ apart
+
+    returned = []
+    for chunk in range(chunks):
+        outs = attend(
+            order, place, own[chunk], cosine, sine, gathered[chunk], received[chunk], per, keep
+        )
+        outs, order, grouped = lax.optimization_barrier((outs, order, grouped))
+        arrived = [
+            lax.ppermute(outs[2 + far - 1], "grp", [(i, i ^ (far * split)) for i in range(groups)])
+            for far in range(1, homes)
+        ]
+        returned.append((outs[0], outs[1], arrived))
+
     score_scale = HD ** (-0.5)
     cache_len = cache_keys.shape[2]
     cache_scores = (
@@ -509,20 +537,9 @@
     cache_log = cache_top * LOG2E + jnp.log2(cache_total)
     cache_log = cache_log.transpose(1, 0, 2).reshape(kv_local, 1, wide)
     cache_log = jnp.broadcast_to(cache_log, (kv_local, 8, wide))
-    cache_context, cache_log, order, place = lax.optimization_barrier((cache_context, cache_log, order, place))
-
-    def partner(i, side_apart, apart):
-        return (i + side_apart * per) % groups ^ apart
-
     result = None
     for chunk in range(chunks):
-        outs = attend(order, place, own[chunk], cosine, sine, q_all, received[chunk], chunk * split, per, keep)
-        outs, order = lax.optimization_barrier((outs, order))
-        arrived = [
-            lax.ppermute(outs[2 + far - 1], "grp", [(i, i ^ (far * split)) for i in range(groups)])
-            for far in range(1, homes)
-        ]
-        context, log, sends = gather(outs[0], outs[1], arrived)
+        context, log, sends = gather(*returned[chunk])
         final = [
             lax.ppermute(
                 sends[number - 1],

time: 128 us -> 160 us (1.25)
  waiting for transfers between devices: 19.2 us -> 37.8 us
  local copies, waits for them, and re-layouts: 8.78 us -> 16.4 us
  other arithmetic: 5.97 us -> 9.82 us
  Pallas kernels: 47.7 us -> 50.2 us
    all_gather x1 -> x2, waiting for transfers between devices: 1.85 us -> 25 us  [on_device(): lax.all_gather(piece, 'grp', axis_index_groups=members)]
    ppermute x6, waiting for transfers between devices: 12.6 us -> 5.92 us  [on_device(): lax.ppermute(outs[2 + far - 1], 'grp', [(i, i ^ far * split) for i in ran...]
    unnamed x18 -> x28, local copies, waits for them, and re-layouts: 4.49 us -> 10.7 us
    another operation x0 -> x5, local copies, waits for them, and re-layouts: none -> 2.82 us  [the longest x4 1.66 us: on_device(): jnp.stack([each[low:high] for each in own_queries])]
    slice x0 -> x6, local copies, waits for them, and re-layouts: none -> 1.97 us  [the longest x2 1.2 us: on_device(): each[HD + 1, 0]]
  transfers between devices with their start and end apart: 20 -> 21, of which waited for: 6 -> 5; matrix products, arithmetic and copies ran while one was open for 15% -> 16% of each run, Pallas kernels for 37% -> 31%
where the time goes in v5:
time: 160 us
  Pallas kernels  50.2 us (31%)
  waiting for transfers between devices  37.8 us (24%)
  starting transfers between devices  18.6 us (12%)
  local copies, waits for them, and re-layouts  16.4 us (10%)
  between operations  15 us (9%)
  matrix products  11.8 us (7%)
  other arithmetic  9.82 us (6%)
    pallas_call x2, Pallas kernels, project(): pl.pallas_call(functools.partial(project_kernel, plan, split, pieces), ou...  29.9 us
    all_gather x2, waiting for transfers between devices, on_device(): lax.all_gather(piece, 'grp', axis_index_groups=members)  25 us
    pallas_call x2, Pallas kernels, attend(): pl.pallas_call(functools.partial(attend_kernel, layout, per, slots, keep,...  16.6 us
    unnamed x28, local copies, waits for them, and re-layouts  10.7 us
    ppermute x6, starting transfers between devices, on_device(): lax.ppermute(outs[2 + far - 1], 'grp', [(i, i ^ far * split) for i in ran...  7.06 us
    dot_general x1, matrix products, on_device(): jnp.einsum('rkgd,rktd->rkgt', grouped, cache_keys, preferred_element_type...  6.81 us
    ppermute x6, waiting for transfers between devices, on_device(): lax.ppermute(outs[2 + far - 1], 'grp', [(i, i ^ far * split) for i in ran...  5.92 us
    ppermute x6, waiting for transfers between devices, on_device(): lax.ppermute(sends[number - 1], 'grp', [(i, partner(i, number // split, n...  5.71 us
  transfers between devices with their start and end apart: 21, of which 5 were waited for; matrix products, arithmetic and copies ran while one was open for 16% of the time, Pallas kernels for 31%

profile of v5, /device:TPU:0, one launch (start us, length us, event | category | flops | bytes accessed | tf_op | source)
XLA Modules:
  0.0 159.6 jit_solution(10136802165509344947)
XLA Ops:
  6.5 1.2 copy.54
  10.0 1.1 collective-permute-done
  15.1 8.7 %project.2 = (s16[1040,256]{1,0:T(8,128)(2,1)}, s16[1040,256]{1,0:T(8,128)(2,1)}) custom-call(s32[2]{0:T(128)} %pad_add_fusion.place_ref, bf16[1024,4096]{1,0:T(8,128)(2,1)} %x_hbm.3, bf16[4096,1024]{1,0:T(8,128)(2,1)} %wk_hbm.3, bf16[4096,1024]{1,0:T(8,128)(2,1)} %wv_hbm.3), custom_call_target="tpu_custom_call" | custom-call | flops 4194304 | bytes 1048576 | tf_op jit(solution)/shard_map/project/pallas_call | solution.py:109
  23.8 2.9 %collective-permute-start.1 = (s16[1040,256]{1,0:T(8,128)(2,1)}, s16[1040,256]{1,0:T(8,128)(2,1)S(1)}, u32[]{:S(2)}, u32[]{:S(2)}) collective-permute-start(s16[1040,256]{1,0:T(8,128)(2,1)} %get-tuple-element.55), channel_id=1, source_target_pairs={{0,1},{1,0},{2,3},{3,2},{4,5},{5,4},{6,7},{7,6},{8,9},{9,8},{10,11... | collective-permute-start | bytes 1597448 | tf_op jit(solution)/shard_map/ppermute | solution.py:460
  27.4 21.2 %project.3 = (s16[1040,256]{1,0:T(8,128)(2,1)}, s16[1040,256]{1,0:T(8,128)(2,1)}, f32[1024,128]{1,0:T(8,128)}, f32[1024,128]{1,0:T(8,128)}, s16[1040,256]{1,0:T(...) custom-call(s32[4]{0:T(128)} %pad_add_fusion.1.place_ref, ...), custom_call_target="tpu_custom_call" | custom-call | flops 4194304 | bytes 1048576 | tf_op jit(solution)/shard_map/project/pallas_call | solution.py:109
  48.8 2.0 %collective-permute-start.4 = (s16[1040,256]{1,0:T(8,128)(2,1)}, s16[1040,256]{1,0:T(8,128)(2,1)S(1)}, u32[]{:S(2)}, u32[]{:S(2)}) collective-permute-start(s16[1040,256]{1,0:T(8,128)(2,1)} %get-tuple-element.73), channel_id=1, source_target_pairs={{0,1},{1,0},{2,3},{3,2},{4,5},{5,4},{6,7},{7,6},{8,9},{9,8},{10,11... | collective-permute-start | bytes 1597448 | tf_op jit(solution)/shard_map/ppermute | solution.py:460
  51.4 1.3 maximum_convert_fusion
  53.3 1.3 compare_select_fusion.2
  54.6 1.9 %fusion.7 = (f32[1024,128]{1,0:T(8,128)S(1)}, f32[1024,128]{1,0:T(8,128)S(1)}) fusion(f32[128]{0:T(128)S(1)} %pad_maximum_fusion.3, s32[128]{0:T(128)S(1)} %compare_select_fusion.2), kind=kLoop, calls=%fused_computation.11 | loop fusion | flops 393216 | bytes 1049600 | tf_op jit(solution)/shard_map/sin | solution.py:398
  57.5 1.1 compare_reduce_fusion
  58.9 1.3 copy-done
  60.2 1.0 copy-done.3
  61.2 1.0 copy-done.8
  62.3 1.0 copy-done.9
  63.3 7.9 %attend.2 = (f32[4,128,256]{2,1,0:T(8,128)S(1)}, f32[4,8,256]{2,1,0:T(8,128)S(1)}, bf16[4,144,256]{2,1,0:T(8,128)(2,1)}, bf16[4,144,256]{2,1,0:T(8,128)(2,1)}, bf16[4,144,256]{2,1,0:T(8,128)(2,1)}) custom-call(s32[16]{0:T(128)S(1)} %select_reduce_fusion.order_ref, s32[16]{0:T(128)S(1)} %fusion.10.place_ref, f32[1024,128]{1,0:T(8,128)S(1)} %copy-done.8, ...), custom_call_target="tpu_custom_call" | custom-call | flops 131072 | bytes 131072 | tf_op jit(solution)/shard_map/attend/pallas_call | solution.py:261
  72.1 1.9 %collective-permute-start.13 = (bf16[4,144,256]{2,1,0:T(8,128)(2,1)}, bf16[4,144,256]{2,1,0:T(8,128)(2,1)S(1)}, u32[]{:S(2)}, u32[]{:S(2)}) collective-permute-start(bf16[4,144,256]{2,1,0:T(8,128)(2,1)} %get-tuple-element.95), channel_id=1, source_target_pairs={{0,4},{2,6},{4,0},{6,2},{8,12},{10,14},{12,8},{14,10},{16,20},{18,... | collective-permute-start | bytes 884744 | tf_op jit(solution)/shard_map/ppermute | solution.py:513
  74.0 1.6 collective-permute-start.14
  75.6 25.0 %all-gather.7.cloned.1.call-done.q_ref = bf16[16,128,256]{2,1,0:T(8,128)(2,1)} async-done(((bf16[2,128,256]{2,1,0:T(8,128)(2,1)}), bf16[16,128,256]{2,1,0:T(8,128)(2,1)}) %all-gather.7.cloned.1.call-update) | async-done | bytes 1048592 | tf_op jit(solution)/shard_map/all_gather | solution.py:450
  100.6 1.2 copy-done.1
  101.8 1.0 copy-done.6
  102.9 1.0 copy-done.7
  103.9 8.7 %attend.3 = (f32[4,128,256]{2,1,0:T(8,128)S(1)}, f32[4,8,256]{2,1,0:T(8,128)S(1)}, bf16[4,144,256]{2,1,0:T(8,128)(2,1)}, bf16[4,144,256]{2,1,0:T(8,128)(2,1)S(1)}, bf16[4,144,256]{2,1,0:T(8,128)(2,1)S(1)}) custom-call(s32[16]{0:T(128)S(1)} %select_reduce_fusion.order_ref, s32[16]{0:T(128)S(1)} %fusion.10.place_ref, f32[1024,128]{1,0:T(8,128)S(1)} %copy-done.6, ...), custom_call_target="tpu_custom_call" | custom-call | flops 131072 | bytes 131072 | tf_op jit(solution)/shard_map/attend/pallas_call | solution.py:261
  114.0 6.8 %fusion.19 = (f32[32,4,8]{2,1,0:T(4,128)S(1)}, f32[32,4,8,256]{3,2,1,0:T(8,128)}) fusion(bf16[32,4,8,128]{3,2,1,0:T(8,128)(2,1)} %bitcast.46, bf16[32,4,256,128]{3,2,1,0:T(8,128)(2,1)} %param.15, pred[32,256]{1,0:T(8,128)(4,1)S(1)} %iota_compare_fusion), kind=kOutput, calls=%fused_computation.58 | convolution fusion | flops 67894272 | bytes 9711616 | tf_op jit(solution)/shard_map/rkgd,rktd->rkgt/dot_general | solution.py:521
  120.8 1.6 %fusion.2 = f32[32,4,8]{2,1,0:T(4,128)S(1)} fusion(f32[32,4,8,256]{3,2,1,0:T(8,128)} %get-tuple-element.114, f32[32,4,8]{2,1,0:T(4,128)S(1)} %get-tuple-element.113, pred[32,256]{1,0:T(8,128)(4,1)S(1)} %iota_compare_fusion), kind=kLoop, calls=%fused_computation.5 | loop fusion | flops 785408 | bytes 1064960 | tf_op jit(solution)/shard_map/reduce_sum | solution.py:528
  123.9 2.4 %collective-permute-start.9 = (bf16[4,144,256]{2,1,0:T(8,128)(2,1)S(1)}, bf16[4,144,256]{2,1,0:T(8,128)(2,1)S(1)}, u32[]{:S(2)}, u32[]{:S(2)}) collective-permute-start(bf16[4,144,256]{2,1,0:T(8,128)(2,1)S(1)} %copy-done.11), channel_id=1, source_target_pairs={{0,12},{2,14},{4,8},{6,10},{8,4},{10,6},{12,0},{14,2},{16,28},{18,... | collective-permute-start | bytes 884744 | tf_op jit(solution)/shard_map/ppermute | solution.py:513
  126.2 1.8 %gather.3 = (f32[128,256]{1,0:T(8,128)S(1)}, f32[8,256]{1,0:T(8,128)S(1)}, bf16[144,256]{1,0:T(8,128)(2,1)}, bf16[144,256]{1,0:T(8,128)(2,1)S(1)}, bf16[144,256]{1,0:T(8,128)(2,1)S(1)}) custom-call(f32[4,128,256]{2,1,0:T(8,128)S(1)} %copy-done.5, f32[4,8,256]{2,1,0:T(8,128)S(1)} %get-tuple-element.94.keep_log_ref, ...), custom_call_target="tpu_custom_call" | custom-call | flops 2097152 | bytes 1572864 | tf_op jit(solution)/shard_map/gather/pallas_call | solution.py:315
  128.0 5.0 %fusion.1 = f32[4,128,32,8]{1,3,0,2:T(8,128)S(1)} fusion(bf16[32,4,256,128]{3,2,1,0:T(8,128)(2,1)} %param.16, f32[32,4,8,256]{3,2,1,0:T(8,128)} %get-tuple-element.114, f32[32,4,8]{2,1,0:T(4,128)S(1)} %get-tuple-element.113, pred[32,256]{1,0:T(8,128)(4,1)S(1)} %iota_compare_fusion, f32[4,32,8]{2,0,1:T(4,128)S(1)} %copy.45), kind=kOutput, calls=%fused_computation.3 | convolution fusion | flops 68026368 | bytes 9977856 | tf_op jit(solution)/shard_map/rkgt,rktd->rkgd/dot_general | solution.py:529
  133.1 1.8 %collective-permute-start.17 = (bf16[144,256]{1,0:T(8,128)(2,1)S(1)}, bf16[144,256]{1,0:T(8,128)(2,1)S(1)}, u32[]{:S(2)}, u32[]{:S(2)}) collective-permute-start(bf16[144,256]{1,0:T(8,128)(2,1)S(1)} %get-tuple-element.101), channel_id=1, source_target_pairs={{0,16},{2,18},{4,20},{6,22},{8,24},{10,26},{12,28},{14,30},{16,0},... | collective-permute-start | bytes 221192 | tf_op jit(solution)/shard_map/ppermute | solution.py:544
  135.9 5.9 %collective-permute-done.9.rest_2_ = bf16[4,144,256]{2,1,0:T(8,128)(2,1)S(1)} collective-permute-done((bf16[4,144,256]{2,1,0:T(8,128)(2,1)S(1)}, bf16[4,144,256]{2,1,0:T(8,128)(2,1)S(1)}, u32[]{:S(2)}, u32[]{:S(2)}) %collective-permute-start.9) | collective-permute-done | bytes 294944 | tf_op jit(solution)/shard_map/ppermute | solution.py:513
  142.5 2.5 %collective-permute-start.12 = (bf16[144,256]{1,0:T(8,128)(2,1)S(1)}, bf16[144,256]{1,0:T(8,128)(2,1)S(1)}, u32[]{:S(2)}, u32[]{:S(2)}) collective-permute-start(bf16[144,256]{1,0:T(8,128)(2,1)S(1)} %get-tuple-element.91), channel_id=1, source_target_pairs={{0,18},{2,16},{4,22},{6,20},{8,26},{10,24},{12,30},{14,28},{16,2},... | collective-permute-start | bytes 221192 | tf_op jit(solution)/shard_map/ppermute | solution.py:544
  146.2 4.2 %collective-permute-done.11.rest_1_ = bf16[144,256]{1,0:T(8,128)(2,1)S(1)} collective-permute-done((bf16[144,256]{1,0:T(8,128)(2,1)S(1)}, bf16[144,256]{1,0:T(8,128)(2,1)S(1)}, u32[]{:S(2)}, u32[]{:S(2)}) %collective-permute-start.11) | collective-permute-done | bytes 73760 | tf_op jit(solution)/shard_map/ppermute | solution.py:544
  150.5 1.5 collective-permute-done.12.rest_2_
  (92 shorter events, 15.7 us)
Async XLA Ops:
  6.5 50.9 %all-gather.5.cloned.1.call-start = ((), (), s32[]{:S(2)}) async-start(), calls=%async_computation | async-start | bytes 1327104 | tf_op jit(solution)/shard_map/all_gather | solution.py:450
  9.5 1.6 collective-permute-start
  12.0 88.6 %all-gather.7.cloned.1.call-start = ((), (), s32[]{:S(2)}) async-start(), calls=%async_computation.1 | async-start | bytes 1179648 | tf_op jit(solution)/shard_map/all_gather | solution.py:450
  23.8 33.7 %collective-permute-start.1 = (s16[1040,256]{1,0:T(8,128)(2,1)}, s16[1040,256]{1,0:T(8,128)(2,1)S(1)}, u32[]{:S(2)}, u32[]{:S(2)}) collective-permute-start(s16[1040,256]{1,0:T(8,128)(2,1)} %get-tuple-element.55), channel_id=1, source_target_pairs={{0,1},{1,0},{2,3},{3,2},{4,5},{5,4},{6,7},{7,6},{8,9},{9,8},{10,11... | collective-permute-start | bytes 1597448 | tf_op jit(solution)/shard_map/ppermute | solution.py:460
  26.7 30.7 %collective-permute-start.2 = (s16[1040,256]{1,0:T(8,128)(2,1)}, s16[1040,256]{1,0:T(8,128)(2,1)S(1)}, u32[]{:S(2)}, u32[]{:S(2)}) collective-permute-start(s16[1040,256]{1,0:T(8,128)(2,1)} %get-tuple-element.56), channel_id=1, source_target_pairs={{0,3},{1,2},{2,1},{3,0},{4,7},{5,6},{6,5},{7,4},{8,11},{9,10},{10,... | collective-permute-start | bytes 1597448 | tf_op jit(solution)/shard_map/ppermute | solution.py:460
  48.5 7.9 %collective-permute-start.3 = (s16[1040,256]{1,0:T(8,128)(2,1)}, s16[1040,256]{1,0:T(8,128)(2,1)S(1)}, u32[]{:S(2)}, u32[]{:S(2)}) collective-permute-start(s16[1040,256]{1,0:T(8,128)(2,1)} %get-tuple-element.58), channel_id=1, source_target_pairs={{0,2},{1,3},{2,0},{3,1},{4,6},{5,7},{6,4},{7,5},{8,10},{9,11},{10,... | collective-permute-start | bytes 1597448 | tf_op jit(solution)/shard_map/ppermute | solution.py:460
  48.8 26.8 %collective-permute-start.4 = (s16[1040,256]{1,0:T(8,128)(2,1)}, s16[1040,256]{1,0:T(8,128)(2,1)S(1)}, u32[]{:S(2)}, u32[]{:S(2)}) collective-permute-start(s16[1040,256]{1,0:T(8,128)(2,1)} %get-tuple-element.73), channel_id=1, source_target_pairs={{0,1},{1,0},{2,3},{3,2},{4,5},{5,4},{6,7},{7,6},{8,9},{9,8},{10,11... | collective-permute-start | bytes 1597448 | tf_op jit(solution)/shard_map/ppermute | solution.py:460
  50.8 24.8 %collective-permute-start.5 = (s16[1040,256]{1,0:T(8,128)(2,1)}, s16[1040,256]{1,0:T(8,128)(2,1)S(1)}, u32[]{:S(2)}, u32[]{:S(2)}) collective-permute-start(s16[1040,256]{1,0:T(8,128)(2,1)} %get-tuple-element.74), channel_id=1, source_target_pairs={{0,3},{1,2},{2,1},{3,0},{4,7},{5,6},{6,5},{7,4},{8,11},{9,10},{10,... | collective-permute-start | bytes 1597448 | tf_op jit(solution)/shard_map/ppermute | solution.py:460
  56.4 0.8 copy-start.2
  57.3 18.3 %collective-permute-start.6 = (s16[1040,256]{1,0:T(8,128)(2,1)}, s16[1040,256]{1,0:T(8,128)(2,1)}, u32[]{:S(2)}, u32[]{:S(2)}) collective-permute-start(s16[1040,256]{1,0:T(8,128)(2,1)} %get-tuple-element.75), channel_id=1, source_target_pairs={{0,2},{1,3},{2,0},{3,1},{4,6},{5,7},{6,4},{7,5},{8,10},{9,11},{10,... | collective-permute-start | bytes 1597448 | tf_op jit(solution)/shard_map/ppermute | solution.py:460
  58.9 1.3 copy-start
  60.2 1.0 copy-start.3
  61.2 1.0 copy-start.8
  62.3 1.0 copy-start.9
  72.1 51.8 %collective-permute-start.13 = (bf16[4,144,256]{2,1,0:T(8,128)(2,1)}, bf16[4,144,256]{2,1,0:T(8,128)(2,1)S(1)}, u32[]{:S(2)}, u32[]{:S(2)}) collective-permute-start(bf16[4,144,256]{2,1,0:T(8,128)(2,1)} %get-tuple-element.95), channel_id=1, source_target_pairs={{0,4},{2,6},{4,0},{6,2},{8,12},{10,14},{12,8},{14,10},{16,20},{18,... | collective-permute-start | bytes 884744 | tf_op jit(solution)/shard_map/ppermute | solution.py:513
  74.0 52.2 %collective-permute-start.14 = (bf16[4,144,256]{2,1,0:T(8,128)(2,1)}, bf16[4,144,256]{2,1,0:T(8,128)(2,1)}, u32[]{:S(2)}, u32[]{:S(2)}) collective-permute-start(bf16[4,144,256]{2,1,0:T(8,128)(2,1)} %get-tuple-element.96), channel_id=1, source_target_pairs={{0,8},{2,10},{4,12},{6,14},{8,0},{10,2},{12,4},{14,6},{16,24},{18,... | collective-permute-start | bytes 884744 | tf_op jit(solution)/shard_map/ppermute | solution.py:513
  75.6 50.7 %collective-permute-start.15 = (bf16[4,144,256]{2,1,0:T(8,128)(2,1)}, bf16[4,144,256]{2,1,0:T(8,128)(2,1)}, u32[]{:S(2)}, u32[]{:S(2)}) collective-permute-start(bf16[4,144,256]{2,1,0:T(8,128)(2,1)} %get-tuple-element.97), channel_id=1, source_target_pairs={{0,12},{2,14},{4,8},{6,10},{8,4},{10,6},{12,0},{14,2},{16,28},{18,... | collective-permute-start | bytes 884744 | tf_op jit(solution)/shard_map/ppermute | solution.py:513
  100.6 1.2 copy-start.1
  101.8 1.0 copy-start.6
  102.9 1.0 copy-start.7
  103.9 22.3 %copy-start.5 = (f32[4,128,256]{2,1,0:T(8,128)S(1)}, f32[4,128,256]{2,1,0:T(8,128)}, u32[]{:S(2)}) copy-start(f32[4,128,256]{2,1,0:T(8,128)} %copy-done.4) | copy-start | bytes 1572868
  114.0 9.3 %copy-start.13 = (bf16[4,144,256]{2,1,0:T(8,128)(2,1)S(1)}, bf16[4,144,256]{2,1,0:T(8,128)(2,1)}, u32[]{:S(2)}) copy-start(bf16[4,144,256]{2,1,0:T(8,128)(2,1)} %copy-done.12) | copy-start | bytes 884740
  114.0 9.8 %copy-start.11 = (bf16[4,144,256]{2,1,0:T(8,128)(2,1)S(1)}, bf16[4,144,256]{2,1,0:T(8,128)(2,1)}, u32[]{:S(2)}) copy-start(bf16[4,144,256]{2,1,0:T(8,128)(2,1)} %copy-done.10) | copy-start | bytes 884740
  122.7 12.2 %collective-permute-start.7 = (bf16[4,144,256]{2,1,0:T(8,128)(2,1)}, bf16[4,144,256]{2,1,0:T(8,128)(2,1)S(1)}, u32[]{:S(2)}, u32[]{:S(2)}) collective-permute-start(bf16[4,144,256]{2,1,0:T(8,128)(2,1)} %get-tuple-element.84), channel_id=1, source_target_pairs={{0,4},{2,6},{4,0},{6,2},{8,12},{10,14},{12,8},{14,10},{16,20},{18,... | collective-permute-start | bytes 884744 | tf_op jit(solution)/shard_map/ppermute | solution.py:513
  123.4 12.5 %collective-permute-start.8 = (bf16[4,144,256]{2,1,0:T(8,128)(2,1)S(1)}, bf16[4,144,256]{2,1,0:T(8,128)(2,1)S(1)}, u32[]{:S(2)}, u32[]{:S(2)}) collective-permute-start(bf16[4,144,256]{2,1,0:T(8,128)(2,1)S(1)} %copy-done.13), channel_id=1, source_target_pairs={{0,8},{2,10},{4,12},{6,14},{8,0},{10,2},{12,4},{14,6},{16,24},{18,... | collective-permute-start | bytes 884744 | tf_op jit(solution)/shard_map/ppermute | solution.py:513
  123.9 17.9 %collective-permute-start.9 = (bf16[4,144,256]{2,1,0:T(8,128)(2,1)S(1)}, bf16[4,144,256]{2,1,0:T(8,128)(2,1)S(1)}, u32[]{:S(2)}, u32[]{:S(2)}) collective-permute-start(bf16[4,144,256]{2,1,0:T(8,128)(2,1)S(1)} %copy-done.11), channel_id=1, source_target_pairs={{0,12},{2,14},{4,8},{6,10},{8,4},{10,6},{12,0},{14,2},{16,28},{18,... | collective-permute-start | bytes 884744 | tf_op jit(solution)/shard_map/ppermute | solution.py:513
  128.0 14.4 %collective-permute-start.16 = (bf16[144,256]{1,0:T(8,128)(2,1)}, bf16[144,256]{1,0:T(8,128)(2,1)S(1)}, u32[]{:S(2)}, u32[]{:S(2)}) collective-permute-start(bf16[144,256]{1,0:T(8,128)(2,1)} %get-tuple-element.100), channel_id=1, source_target_pairs={{0,2},{2,0},{4,6},{6,4},{8,10},{10,8},{12,14},{14,12},{16,18},{18,... | collective-permute-start | bytes 221192 | tf_op jit(solution)/shard_map/ppermute | solution.py:544
  133.1 12.3 %collective-permute-start.17 = (bf16[144,256]{1,0:T(8,128)(2,1)S(1)}, bf16[144,256]{1,0:T(8,128)(2,1)S(1)}, u32[]{:S(2)}, u32[]{:S(2)}) collective-permute-start(bf16[144,256]{1,0:T(8,128)(2,1)S(1)} %get-tuple-element.101), channel_id=1, source_target_pairs={{0,16},{2,18},{4,20},{6,22},{8,24},{10,26},{12,28},{14,30},{16,0},... | collective-permute-start | bytes 221192 | tf_op jit(solution)/shard_map/ppermute | solution.py:544
  134.9 10.5 %collective-permute-start.18 = (bf16[144,256]{1,0:T(8,128)(2,1)S(1)}, bf16[144,256]{1,0:T(8,128)(2,1)S(1)}, u32[]{:S(2)}, u32[]{:S(2)}) collective-permute-start(bf16[144,256]{1,0:T(8,128)(2,1)S(1)} %get-tuple-element.102), channel_id=1, source_target_pairs={{0,18},{2,16},{4,22},{6,20},{8,26},{10,24},{12,30},{14,28},{16,2},... | collective-permute-start | bytes 221192 | tf_op jit(solution)/shard_map/ppermute | solution.py:544
  142.1 4.1 %collective-permute-start.10 = (bf16[144,256]{1,0:T(8,128)(2,1)S(1)}, bf16[144,256]{1,0:T(8,128)(2,1)S(1)}, u32[]{:S(2)}, u32[]{:S(2)}) collective-permute-start(bf16[144,256]{1,0:T(8,128)(2,1)S(1)} %get-tuple-element.89), channel_id=1, source_target_pairs={{0,2},{2,0},{4,6},{6,4},{8,10},{10,8},{12,14},{14,12},{16,18},{18,... | collective-permute-start | bytes 221192 | tf_op jit(solution)/shard_map/ppermute | solution.py:544
  142.2 8.3 %collective-permute-start.11 = (bf16[144,256]{1,0:T(8,128)(2,1)S(1)}, bf16[144,256]{1,0:T(8,128)(2,1)S(1)}, u32[]{:S(2)}, u32[]{:S(2)}) collective-permute-start(bf16[144,256]{1,0:T(8,128)(2,1)S(1)} %get-tuple-element.90), channel_id=1, source_target_pairs={{0,16},{2,18},{4,20},{6,22},{8,24},{10,26},{12,28},{14,30},{16,0},... | collective-permute-start | bytes 221192 | tf_op jit(solution)/shard_map/ppermute | solution.py:544
  142.5 9.5 %collective-permute-start.12 = (bf16[144,256]{1,0:T(8,128)(2,1)S(1)}, bf16[144,256]{1,0:T(8,128)(2,1)S(1)}, u32[]{:S(2)}, u32[]{:S(2)}) collective-permute-start(bf16[144,256]{1,0:T(8,128)(2,1)S(1)} %get-tuple-element.91), channel_id=1, source_target_pairs={{0,18},{2,16},{4,22},{6,20},{8,26},{10,24},{12,30},{14,28},{16,2},... | collective-permute-start | bytes 221192 | tf_op jit(solution)/shard_map/ppermute | solution.py:544
  (3 other events, 2.2 us)
Sparse Core Ops, SparseCore 0:
  12.1 43.8 all-gather.4
  58.1 42.4 all-gather.6

commit v6 on v4

--- a/solution.py
+++ b/solution.py
@@ -18,6 +18,7 @@
 BIG = 60 * 1024 * 1024
 SMALL = 16 * 1024 * 1024
 ANY = pl.BlockSpec(memory_space=pl.ANY)
+HBM = pl.BlockSpec(memory_space=pltpu.HBM)
 
 
 def encode(values):
@@ -166,13 +167,28 @@
     return context, top + jnp.log(total) * LOG2E
 
 
-def attend_kernel(layout, per, slots, keep, sends, order_ref, place_ref, own_key, own_value, cos_ref, sin_ref, q_ref, *rest):
+def attend_kernel(layout, per, slots, keep, sends, chunk_head, order_ref, place_ref, own_key_hbm, own_value_hbm, cos_ref, sin_ref, q_hbm, *rest):
     parts = sum(layout)
     received = list(rest[:parts])
     keep_ref, keep_log_ref = rest[parts : parts + 2]
     send_refs = rest[parts + 2 : parts + 2 + sends]
-    key_scr, value_scr, score_scr, top_scr, context_scr, log_scr = rest[parts + 2 + sends :]
+    key_scr, value_scr, score_scr, top_scr, context_scr, log_scr, own_key, own_value, q_ref, sems = rest[
+        parts + 2 + sends :
+    ]
     rows = own_key.shape[0]
+    lanes = pl.ds(pl.multiple_of((chunk_head + order_ref[slots]) * HD, HD), HD)
+    own_copies = [
+        pltpu.make_async_copy(own_key_hbm, own_key, sems.at[per]),
+        pltpu.make_async_copy(own_value_hbm, own_value, sems.at[per + 1]),
+    ]
+    query_copies = [
+        pltpu.make_async_copy(q_hbm.at[order_ref[index], lanes], q_ref.at[index], sems.at[index])
+        for index in range(per)
+    ]
+    for copy in own_copies + query_copies:
+        copy.start()
+    for copy in own_copies:
+        copy.wait()
     blocks = len(layout)
     for block in range(blocks):
         here = [received.pop(0) for _ in range(layout[block])]
@@ -200,7 +216,7 @@
     tile = min(512, total_keys)
 
     def score(index, buffer):
-        query = q_ref[order_ref[index]]
+        query = q_ref[index]
         tops = []
         for start in range(0, total_keys, tile):
             scores = jnp.dot(key_scr[start : start + tile], query, preferred_element_type=jnp.float32)
@@ -220,6 +236,8 @@
         context_scr[place_ref[index]] = summed[:HD] * (1.0 / total)
         log_scr[place_ref[index]] = jnp.broadcast_to(top + jnp.log(total) * LOG2E, log_scr.shape[1:])
 
+    for copy in query_copies:
+        copy.wait()
     score(0, 0)
 
     @pl.loop(0, per // 2)
@@ -261,17 +279,17 @@
         jax.ShapeDtypeStruct((keep, 8, wide), jnp.float32),
     ] + [jax.ShapeDtypeStruct((keep, HD + STAT_ROWS, wide), jnp.bfloat16)] * sends
     return pl.pallas_call(
-        functools.partial(attend_kernel, layout, per, slots, keep, sends),
+        functools.partial(attend_kernel, layout, per, slots, keep, sends, head),
         out_shape=tuple(shapes),
         grid_spec=pltpu.PrefetchScalarGridSpec(
             num_scalar_prefetch=2,
             grid=(1,),
             in_specs=[
+                HBM,
+                HBM,
                 whole((rows, HD)),
                 whole((rows, HD)),
-                whole((rows, HD)),
-                whole((rows, HD)),
-                pl.BlockSpec((slots, HD, wide), lambda i, a, b: (0, head + a[slots], 0)),
+                HBM,
             ]
             + [whole(part.shape) for part in flat],
             out_specs=tuple(whole(shape.shape) for shape in shapes),
@@ -282,9 +300,13 @@
                 pltpu.VMEM((2, 8, wide), jnp.float32),
                 pltpu.VMEM((slots, HD, wide), jnp.float32),
                 pltpu.VMEM((slots, 8, wide), jnp.float32),
+                pltpu.VMEM((rows, HD), jnp.float32),
+                pltpu.VMEM((rows, HD), jnp.float32),
+                pltpu.VMEM((per, HD, wide), jnp.bfloat16),
+                pltpu.SemaphoreType.DMA((per + 2,)),
             ],
         ),
-        compiler_params=pltpu.CompilerParams(vmem_limit_bytes=2 * SMALL),
+        compiler_params=pltpu.CompilerParams(vmem_limit_bytes=54 * 1024 * 1024),
         cost_estimate=pl.CostEstimate(
             flops=8 * per * blocks * rows * wide * HD,
             bytes_accessed=blocks * rows * HD * 16 + slots * HD * wide * 4,

time: 128 us -> 135 us (1.055)
  Pallas kernels: 47.7 us -> 55.1 us
  starting transfers between devices: 19.8 us -> 17.6 us
  local copies, waits for them, and re-layouts: 8.78 us -> 6.81 us
  other arithmetic: 5.97 us -> 7.91 us
  waiting for transfers between devices: 19.2 us -> 21.1 us
    pallas_call x2, Pallas kernels: 15.4 us -> 22.8 us  [attend(): pl.pallas_call(functools.partial(attend_kernel, layout, per, slots, keep,...]
    ppermute x6, starting transfers between devices: 6.96 us -> 4.79 us  [on_device(): lax.ppermute(sends[number - 1], 'grp', [(i, partner(i, number // split, n...]
    unnamed x18 -> x26, local copies, waits for them, and re-layouts: 4.49 us -> 4.37 us
  transfers between devices with their start and end apart: 20 -> 20, of which waited for: 6 -> 6; matrix products, arithmetic and copies ran while one was open for 15% -> 14% of each run, Pallas kernels for 37% -> 40%
where the time goes in v6:
time: 135 us; the launch traced here: 134 us
  Pallas kernels  55.1 us (41%)
  waiting for transfers between devices  21.1 us (16%)
  starting transfers between devices  17.6 us (13%)
  between operations  15 us (11%)
  matrix products  10.7 us (8%)
  other arithmetic  7.91 us (6%)
  local copies, waits for them, and re-layouts  6.81 us (5%)
    pallas_call x2, Pallas kernels, project(): pl.pallas_call(functools.partial(project_kernel, plan, split, pieces), ou...  30.1 us
    pallas_call x2, Pallas kernels, attend(): pl.pallas_call(functools.partial(attend_kernel, layout, per, slots, keep,...  22.8 us
    ppermute x6, waiting for transfers between devices, on_device(): lax.ppermute(outs[2 + far - 1], 'grp', [(i, i ^ far * split) for i in ran...  13.4 us
    ppermute x6, starting transfers between devices, on_device(): lax.ppermute(outs[2 + far - 1], 'grp', [(i, i ^ far * split) for i in ran...  7.11 us
    ppermute x6, waiting for transfers between devices, on_device(): lax.ppermute(sends[number - 1], 'grp', [(i, partner(i, number // split, n...  5.95 us
    dot_general x1, matrix products, on_device(): jnp.einsum('rkgd,rktd->rkgt', grouped, cache_keys, preferred_element_type...  5.8 us
    ppermute x6, starting transfers between devices, exchange(): return lax.ppermute(array, ('grp', 'tp'), pairs)  5.19 us
    dot_general x1, matrix products, on_device(): jnp.einsum('rkgt,rktd->rkgd', cache_weights.astype(jnp.bfloat16), cache_v...  4.9 us
  transfers between devices with their start and end apart: 20, of which 6 were waited for; matrix products, arithmetic and copies ran while one was open for 14% of the time, Pallas kernels for 40%

profile of v6, /device:TPU:0, one launch (start us, length us, event | category | flops | bytes accessed | tf_op | source)
XLA Modules:
  0.0 134.2 jit_solution(4053451905490546425)
XLA Ops:
  7.2 1.1 copy.53
  8.4 0.7 concatenate.9.clone
  10.4 8.7 %project.2 = (s16[1040,256]{1,0:T(8,128)(2,1)}, s16[1040,256]{1,0:T(8,128)(2,1)}) custom-call(s32[2]{0:T(128)} %pad_add_fusion.place_ref, bf16[1024,4096]{1,0:T(8,128)(2,1)} %x_hbm.3, bf16[4096,1024]{1,0:T(8,128)(2,1)} %wk_hbm.3, bf16[4096,1024]{1,0:T(8,128)(2,1)} %wv_hbm.3), custom_call_target="tpu_custom_call" | custom-call | flops 4294967296 | bytes 13631488 | tf_op jit(solution)/shard_map/project/pallas_call | solution.py:110
  19.1 2.6 %collective-permute-start.1 = (s16[1040,256]{1,0:T(8,128)(2,1)}, s16[1040,256]{1,0:T(8,128)(2,1)S(1)}, u32[]{:S(2)}, u32[]{:S(2)}) collective-permute-start(s16[1040,256]{1,0:T(8,128)(2,1)} %get-tuple-element.82), channel_id=1, source_target_pairs={{0,1},{1,0},{2,3},{3,2},{4,5},{5,4},{6,7},{7,6},{8,9},{9,8},{10,11... | collective-permute-start | bytes 1597448 | tf_op jit(solution)/shard_map/ppermute | solution.py:469
  21.9 0.7 pad_add_fusion.1.place_ref
  22.5 21.4 %project.3 = (s16[1040,256]{1,0:T(8,128)(2,1)}, s16[1040,256]{1,0:T(8,128)(2,1)}, f32[1024,128]{1,0:T(8,128)}, f32[1024,128]{1,0:T(8,128)}, s16[1040,256]{1,0:T(...) custom-call(s32[4]{0:T(128)} %pad_add_fusion.1.place_ref, ...), custom_call_target="tpu_custom_call" | custom-call | flops 12884901888 | bytes 24117248 | tf_op jit(solution)/shard_map/project/pallas_call | solution.py:110
  44.0 1.9 %collective-permute-start.4 = (s16[1040,256]{1,0:T(8,128)(2,1)}, s16[1040,256]{1,0:T(8,128)(2,1)S(1)}, u32[]{:S(2)}, u32[]{:S(2)}) collective-permute-start(s16[1040,256]{1,0:T(8,128)(2,1)} %get-tuple-element.93), channel_id=1, source_target_pairs={{0,1},{1,0},{2,3},{3,2},{4,5},{5,4},{6,7},{7,6},{8,9},{9,8},{10,11... | collective-permute-start | bytes 1597448 | tf_op jit(solution)/shard_map/ppermute | solution.py:469
  46.7 5.8 %fusion.17 = (f32[32,4,8]{2,1,0:T(4,128)S(1)}, f32[32,4,8,256]{3,2,1,0:T(8,128)S(1)}) fusion(bf16[32,4,8,128]{3,2,1,0:T(8,128)(2,1)S(1)} %bitcast.39, bf16[32,4,256,128]{3,2,1,0:T(8,128)(2,1)} %param.15, pred[32,256]{1,0:T(8,128)(4,1)S(1)} %iota_compare_fusion), kind=kOutput, calls=%fused_computation.48 | convolution fusion | flops 67894272 | bytes 9711616 | tf_op jit(solution)/shard_map/rkgd,rktd->rkgt/dot_general | solution.py:515
  53.3 4.9 %fusion.1 = f32[4,128,32,8]{1,3,0,2:T(8,128)S(1)} fusion(bf16[32,4,256,128]{3,2,1,0:T(8,128)(2,1)} %param.16, f32[32,4,8,256]{3,2,1,0:T(8,128)S(1)} %get-tuple-element.128, f32[32,4,8]{2,1,0:T(4,128)S(1)} %get-tuple-element.127, pred[32,256]{1,0:T(8,128)(4,1)S(1)} %iota_compare_fusion, f32[4,32,8]{2,0,1:T(4,128)S(1)} %copy.37), kind=kOutput, calls=%fused_computation.3 | convolution fusion | flops 68026368 | bytes 9977856 | tf_op jit(solution)/shard_map/rkgt,rktd->rkgd/dot_general | solution.py:523
  59.2 2.8 %fusion.5 = (f32[1024,128]{1,0:T(8,128)}, f32[1024,128]{1,0:T(8,128)}) fusion(f32[128]{0:T(128)S(1)} %pad_maximum_fusion, s32[128]{0:T(128)S(1)} %compare_select_fusion.2), kind=kLoop, calls=%fused_computation.9 | loop fusion | flops 393216 | bytes 1049600 | tf_op jit(solution)/shard_map/sin | solution.py:424
  62.0 1.6 %all-gather.3.cloned.1.call-done = bf16[8448,256]{1,0:T(8,128)(2,1)} async-done(((bf16[528,256]{1,0:T(8,128)(2,1)}), bf16[8448,256]{1,0:T(8,128)(2,1)}) %all-gather.3.cloned.1.call-update) | async-done | bytes 4325392 | tf_op jit(solution)/shard_map/all_gather | solution.py:459
  63.6 1.1 compare_reduce_fusion
  66.6 0.8 copy-done.7
  67.3 11.4 %attend.2 = (f32[4,128,256]{2,1,0:T(8,128)}, f32[4,8,256]{2,1,0:T(8,128)}, bf16[4,144,256]{2,1,0:T(8,128)(2,1)}, bf16[4,144,256]{2,1,0:T(8,128)(2,1)}, bf16[4,144,256]{2,1,0:T(8,128)(2,1)}) custom-call(s32[17]{0:T(128)} %pad_add_fusion.2.order_ref, s32[16]{0:T(128)} %fusion.14.place_ref, f32[1024,128]{1,0:T(8,128)} %get-tuple-element.80.own_key_hbm, ...), custom_call_target="tpu_custom_call" | custom-call | flops 4294967296 | bytes 6291456 | tf_op jit(solution)/shard_map/attend/pallas_call | solution.py:281
  79.4 1.5 %collective-permute-start.14 = (bf16[4,144,256]{2,1,0:T(8,128)(2,1)}, bf16[4,144,256]{2,1,0:T(8,128)(2,1)S(1)}, u32[]{:S(2)}, u32[]{:S(2)}) collective-permute-start(bf16[4,144,256]{2,1,0:T(8,128)(2,1)} %get-tuple-element.116), channel_id=1, source_target_pairs={{0,8},{2,10},{4,12},{6,14},{8,0},{10,2},{12,4},{14,6},{16,24},{18,... | collective-permute-start | bytes 884744 | tf_op jit(solution)/shard_map/ppermute | solution.py:544
  80.9 1.4 %collective-permute-start.15 = (bf16[4,144,256]{2,1,0:T(8,128)(2,1)}, bf16[4,144,256]{2,1,0:T(8,128)(2,1)S(1)}, u32[]{:S(2)}, u32[]{:S(2)}) collective-permute-start(bf16[4,144,256]{2,1,0:T(8,128)(2,1)} %get-tuple-element.117), channel_id=1, source_target_pairs={{0,12},{2,14},{4,8},{6,10},{8,4},{10,6},{12,0},{14,2},{16,28},{18,... | collective-permute-start | bytes 884744 | tf_op jit(solution)/shard_map/ppermute | solution.py:544
  82.4 0.8 copy-done.10
  83.2 0.8 copy-done.11
  84.0 11.4 %attend.3 = (f32[4,128,256]{2,1,0:T(8,128)}, f32[4,8,256]{2,1,0:T(8,128)}, bf16[4,144,256]{2,1,0:T(8,128)(2,1)}, bf16[4,144,256]{2,1,0:T(8,128)(2,1)}, bf16[4,144,256]{2,1,0:T(8,128)(2,1)}) custom-call(s32[17]{0:T(128)} %pad_add_fusion.2.order_ref, s32[16]{0:T(128)} %fusion.14.place_ref, f32[1024,128]{1,0:T(8,128)} %get-tuple-element.91.own_key_hbm, ...), custom_call_target="tpu_custom_call" | custom-call | flops 4294967296 | bytes 6291456 | tf_op jit(solution)/shard_map/attend/pallas_call | solution.py:281
  96.0 1.5 %collective-permute-start.8 = (bf16[4,144,256]{2,1,0:T(8,128)(2,1)}, bf16[4,144,256]{2,1,0:T(8,128)(2,1)S(1)}, u32[]{:S(2)}, u32[]{:S(2)}) collective-permute-start(bf16[4,144,256]{2,1,0:T(8,128)(2,1)} %get-tuple-element.104), channel_id=1, source_target_pairs={{0,8},{2,10},{4,12},{6,14},{8,0},{10,2},{12,4},{14,6},{16,24},{18,... | collective-permute-start | bytes 884744 | tf_op jit(solution)/shard_map/ppermute | solution.py:544
  97.5 1.4 %collective-permute-start.9 = (bf16[4,144,256]{2,1,0:T(8,128)(2,1)}, bf16[4,144,256]{2,1,0:T(8,128)(2,1)S(1)}, u32[]{:S(2)}, u32[]{:S(2)}) collective-permute-start(bf16[4,144,256]{2,1,0:T(8,128)(2,1)} %get-tuple-element.105), channel_id=1, source_target_pairs={{0,12},{2,14},{4,8},{6,10},{8,4},{10,6},{12,0},{14,2},{16,28},{18,... | collective-permute-start | bytes 884744 | tf_op jit(solution)/shard_map/ppermute | solution.py:544
  99.3 1.9 %collective-permute-start.17 = (bf16[144,256]{1,0:T(8,128)(2,1)S(1)}, bf16[144,256]{1,0:T(8,128)(2,1)S(1)}, u32[]{:S(2)}, u32[]{:S(2)}) collective-permute-start(bf16[144,256]{1,0:T(8,128)(2,1)S(1)} %get-tuple-element.121), channel_id=1, source_target_pairs={{0,16},{2,18},{4,20},{6,22},{8,24},{10,26},{12,28},{14,30},{16,0},... | collective-permute-start | bytes 221192 | tf_op jit(solution)/shard_map/ppermute | solution.py:549
  101.2 2.9 %collective-permute-done.7.rest_0_ = bf16[4,144,256]{2,1,0:T(8,128)(2,1)S(1)} collective-permute-done((bf16[4,144,256]{2,1,0:T(8,128)(2,1)}, bf16[4,144,256]{2,1,0:T(8,128)(2,1)S(1)}, u32[]{:S(2)}, u32[]{:S(2)}) %collective-permute-start.7) | collective-permute-done | bytes 294944 | tf_op jit(solution)/shard_map/ppermute | solution.py:544
  104.0 3.7 %collective-permute-done.8.rest_1_ = bf16[4,144,256]{2,1,0:T(8,128)(2,1)S(1)} collective-permute-done((bf16[4,144,256]{2,1,0:T(8,128)(2,1)}, bf16[4,144,256]{2,1,0:T(8,128)(2,1)S(1)}, u32[]{:S(2)}, u32[]{:S(2)}) %collective-permute-start.8) | collective-permute-done | bytes 294944 | tf_op jit(solution)/shard_map/ppermute | solution.py:544
  107.7 6.9 %collective-permute-done.9.rest_2_ = bf16[4,144,256]{2,1,0:T(8,128)(2,1)S(1)} collective-permute-done((bf16[4,144,256]{2,1,0:T(8,128)(2,1)}, bf16[4,144,256]{2,1,0:T(8,128)(2,1)S(1)}, u32[]{:S(2)}, u32[]{:S(2)}) %collective-permute-start.9) | collective-permute-done | bytes 294944 | tf_op jit(solution)/shard_map/ppermute | solution.py:544
  114.6 1.0 copy-done.1
  115.7 0.8 copy-done.3
  117.2 2.4 %collective-permute-start.12 = (bf16[144,256]{1,0:T(8,128)(2,1)S(1)}, bf16[144,256]{1,0:T(8,128)(2,1)S(1)}, u32[]{:S(2)}, u32[]{:S(2)}) collective-permute-start(bf16[144,256]{1,0:T(8,128)(2,1)S(1)} %get-tuple-element.110), channel_id=1, source_target_pairs={{0,18},{2,16},{4,22},{6,20},{8,26},{10,24},{12,30},{14,28},{16,2},... | collective-permute-start | bytes 221192 | tf_op jit(solution)/shard_map/ppermute | solution.py:549
  119.8 0.8 finish.2.rest_5_
  120.6 4.5 %collective-permute-done.11.rest_1_ = bf16[144,256]{1,0:T(8,128)(2,1)S(1)} collective-permute-done((bf16[144,256]{1,0:T(8,128)(2,1)S(1)}, bf16[144,256]{1,0:T(8,128)(2,1)S(1)}, u32[]{:S(2)}, u32[]{:S(2)}) %collective-permute-start.11) | collective-permute-done | bytes 73760 | tf_op jit(solution)/shard_map/ppermute | solution.py:549
  125.1 1.5 %collective-permute-done.12.rest_2_ = bf16[144,256]{1,0:T(8,128)(2,1)S(1)} collective-permute-done((bf16[144,256]{1,0:T(8,128)(2,1)S(1)}, bf16[144,256]{1,0:T(8,128)(2,1)S(1)}, u32[]{:S(2)}, u32[]{:S(2)}) %collective-permute-start.12) | collective-permute-done | bytes 73760 | tf_op jit(solution)/shard_map/ppermute | solution.py:549
  126.5 0.8 finish.3
  (71 shorter events, 7.7 us)
Async XLA Ops:
  6.5 57.1 %all-gather.3.cloned.1.call-start = ((), (), s32[]{:S(2)}) async-start(), calls=%async_computation | async-start | bytes 4595712 | tf_op jit(solution)/shard_map/all_gather | solution.py:459
  9.2 49.4 %collective-permute-start = (s32[1]{0:T(128)}, s32[1]{0:T(128)}, u32[]{:S(2)}, u32[]{:S(2)}) collective-permute-start(s32[1]{0:T(128)} %param.12), channel_id=1, source_target_pairs={{0,2},{2,0},{4,6},{6,4},{8,10},{10,8},{12,14},{14,12},{16,18},{18,... | collective-permute-start | bytes 20 | tf_op jit(solution)/shard_map/ppermute | solution.py:462
  19.1 46.0 %collective-permute-start.1 = (s16[1040,256]{1,0:T(8,128)(2,1)}, s16[1040,256]{1,0:T(8,128)(2,1)S(1)}, u32[]{:S(2)}, u32[]{:S(2)}) collective-permute-start(s16[1040,256]{1,0:T(8,128)(2,1)} %get-tuple-element.82), channel_id=1, source_target_pairs={{0,1},{1,0},{2,3},{3,2},{4,5},{5,4},{6,7},{7,6},{8,9},{9,8},{10,11... | collective-permute-start | bytes 1597448 | tf_op jit(solution)/shard_map/ppermute | solution.py:469
  21.7 44.8 %collective-permute-start.2 = (s16[1040,256]{1,0:T(8,128)(2,1)}, s16[1040,256]{1,0:T(8,128)(2,1)S(1)}, u32[]{:S(2)}, u32[]{:S(2)}) collective-permute-start(s16[1040,256]{1,0:T(8,128)(2,1)} %get-tuple-element.83), channel_id=1, source_target_pairs={{0,3},{1,2},{2,1},{3,0},{4,7},{5,6},{6,5},{7,4},{8,11},{9,10},{10,... | collective-permute-start | bytes 1597448 | tf_op jit(solution)/shard_map/ppermute | solution.py:469
  22.5 24.1 %copy-start.5 = (s32[32]{0:T(128)S(1)}, s32[32]{0:T(128)}, u32[]{:S(2)}) copy-start(s32[32]{0:T(128)} %param.17) | copy-start | bytes 388
  22.5 24.2 %copy-start.4 = (bf16[32,32,128]{2,1,0:T(8,128)(2,1)S(1)}, bf16[32,32,128]{2,1,0:T(8,128)(2,1)}, u32[]{:S(2)}) copy-start(bf16[32,32,128]{2,1,0:T(8,128)(2,1)} %param.14) | copy-start | bytes 786436
  43.9 22.7 %collective-permute-start.3 = (s16[1040,256]{1,0:T(8,128)(2,1)}, s16[1040,256]{1,0:T(8,128)(2,1)}, u32[]{:S(2)}, u32[]{:S(2)}) collective-permute-start(s16[1040,256]{1,0:T(8,128)(2,1)} %get-tuple-element.84), channel_id=1, source_target_pairs={{0,2},{1,3},{2,0},{3,1},{4,6},{5,7},{6,4},{7,5},{8,10},{9,11},{10,... | collective-permute-start | bytes 1597448 | tf_op jit(solution)/shard_map/ppermute | solution.py:469
  44.0 36.9 %collective-permute-start.4 = (s16[1040,256]{1,0:T(8,128)(2,1)}, s16[1040,256]{1,0:T(8,128)(2,1)S(1)}, u32[]{:S(2)}, u32[]{:S(2)}) collective-permute-start(s16[1040,256]{1,0:T(8,128)(2,1)} %get-tuple-element.93), channel_id=1, source_target_pairs={{0,1},{1,0},{2,3},{3,2},{4,5},{5,4},{6,7},{7,6},{8,9},{9,8},{10,11... | collective-permute-start | bytes 1597448 | tf_op jit(solution)/shard_map/ppermute | solution.py:469
  52.5 12.5 %copy-start.9 = (s16[1040,256]{1,0:T(8,128)(2,1)S(1)}, s16[1040,256]{1,0:T(8,128)(2,1)}, u32[]{:S(2)}) copy-start(s16[1040,256]{1,0:T(8,128)(2,1)} %get-tuple-element.95) | copy-start | bytes 1597444
  58.6 23.8 %collective-permute-start.5 = (s16[1040,256]{1,0:T(8,128)(2,1)}, s16[1040,256]{1,0:T(8,128)(2,1)S(1)}, u32[]{:S(2)}, u32[]{:S(2)}) collective-permute-start(s16[1040,256]{1,0:T(8,128)(2,1)} %get-tuple-element.94), channel_id=1, source_target_pairs={{0,3},{1,2},{2,1},{3,0},{4,7},{5,6},{6,5},{7,4},{8,11},{9,10},{10,... | collective-permute-start | bytes 1597448 | tf_op jit(solution)/shard_map/ppermute | solution.py:469
  65.1 1.5 %copy-start.6 = (s16[1040,256]{1,0:T(8,128)(2,1)}, s16[1040,256]{1,0:T(8,128)(2,1)S(1)}, u32[]{:S(2)}) copy-start(s16[1040,256]{1,0:T(8,128)(2,1)S(1)} %collective-permute-done.1.rest_0_) | copy-start | bytes 1597444
  65.1 17.3 %collective-permute-start.6 = (s16[1040,256]{1,0:T(8,128)(2,1)S(1)}, s16[1040,256]{1,0:T(8,128)(2,1)S(1)}, u32[]{:S(2)}, u32[]{:S(2)}) collective-permute-start(s16[1040,256]{1,0:T(8,128)(2,1)S(1)} %copy-done.9), channel_id=1, source_target_pairs={{0,2},{1,3},{2,0},{3,1},{4,6},{5,7},{6,4},{7,5},{8,10},{9,11},{10,... | collective-permute-start | bytes 1597448 | tf_op jit(solution)/shard_map/ppermute | solution.py:469
  66.5 0.8 copy-start.7
  78.8 20.1 %copy-start = (f32[4,128,256]{2,1,0:T(8,128)S(1)}, f32[4,128,256]{2,1,0:T(8,128)}, u32[]{:S(2)}) copy-start(f32[4,128,256]{2,1,0:T(8,128)} %get-tuple-element.113.keep_ref) | copy-start | bytes 1572868
  78.8 20.1 %copy-start.2 = (f32[4,8,256]{2,1,0:T(8,128)S(1)}, f32[4,8,256]{2,1,0:T(8,128)}, u32[]{:S(2)}) copy-start(f32[4,8,256]{2,1,0:T(8,128)} %get-tuple-element.114.keep_log_ref) | copy-start | bytes 98308
  78.8 18.7 %collective-permute-start.13 = (bf16[4,144,256]{2,1,0:T(8,128)(2,1)}, bf16[4,144,256]{2,1,0:T(8,128)(2,1)S(1)}, u32[]{:S(2)}, u32[]{:S(2)}) collective-permute-start(bf16[4,144,256]{2,1,0:T(8,128)(2,1)} %get-tuple-element.115), channel_id=1, source_target_pairs={{0,4},{2,6},{4,0},{6,2},{8,12},{10,14},{12,8},{14,10},{16,20},{18,... | collective-permute-start | bytes 884744 | tf_op jit(solution)/shard_map/ppermute | solution.py:544
  79.4 19.5 %collective-permute-start.14 = (bf16[4,144,256]{2,1,0:T(8,128)(2,1)}, bf16[4,144,256]{2,1,0:T(8,128)(2,1)S(1)}, u32[]{:S(2)}, u32[]{:S(2)}) collective-permute-start(bf16[4,144,256]{2,1,0:T(8,128)(2,1)} %get-tuple-element.116), channel_id=1, source_target_pairs={{0,8},{2,10},{4,12},{6,14},{8,0},{10,2},{12,4},{14,6},{16,24},{18,... | collective-permute-start | bytes 884744 | tf_op jit(solution)/shard_map/ppermute | solution.py:544
  80.9 1.4 %copy-start.8 = (s16[1040,256]{1,0:T(8,128)(2,1)}, s16[1040,256]{1,0:T(8,128)(2,1)S(1)}, u32[]{:S(2)}) copy-start(s16[1040,256]{1,0:T(8,128)(2,1)S(1)} %collective-permute-done.4.rest_0_) | copy-start | bytes 1597444
  80.9 18.0 %collective-permute-start.15 = (bf16[4,144,256]{2,1,0:T(8,128)(2,1)}, bf16[4,144,256]{2,1,0:T(8,128)(2,1)S(1)}, u32[]{:S(2)}, u32[]{:S(2)}) collective-permute-start(bf16[4,144,256]{2,1,0:T(8,128)(2,1)} %get-tuple-element.117), channel_id=1, source_target_pairs={{0,12},{2,14},{4,8},{6,10},{8,4},{10,6},{12,0},{14,2},{16,28},{18,... | collective-permute-start | bytes 884744 | tf_op jit(solution)/shard_map/ppermute | solution.py:544
  82.3 0.8 copy-start.10
  83.2 0.8 copy-start.11
  95.3 8.7 %collective-permute-start.7 = (bf16[4,144,256]{2,1,0:T(8,128)(2,1)}, bf16[4,144,256]{2,1,0:T(8,128)(2,1)S(1)}, u32[]{:S(2)}, u32[]{:S(2)}) collective-permute-start(bf16[4,144,256]{2,1,0:T(8,128)(2,1)} %get-tuple-element.103), channel_id=1, source_target_pairs={{0,4},{2,6},{4,0},{6,2},{8,12},{10,14},{12,8},{14,10},{16,20},{18,... | collective-permute-start | bytes 884744 | tf_op jit(solution)/shard_map/ppermute | solution.py:544
  96.0 11.7 %collective-permute-start.8 = (bf16[4,144,256]{2,1,0:T(8,128)(2,1)}, bf16[4,144,256]{2,1,0:T(8,128)(2,1)S(1)}, u32[]{:S(2)}, u32[]{:S(2)}) collective-permute-start(bf16[4,144,256]{2,1,0:T(8,128)(2,1)} %get-tuple-element.104), channel_id=1, source_target_pairs={{0,8},{2,10},{4,12},{6,14},{8,0},{10,2},{12,4},{14,6},{16,24},{18,... | collective-permute-start | bytes 884744 | tf_op jit(solution)/shard_map/ppermute | solution.py:544
  97.5 17.1 %collective-permute-start.9 = (bf16[4,144,256]{2,1,0:T(8,128)(2,1)}, bf16[4,144,256]{2,1,0:T(8,128)(2,1)S(1)}, u32[]{:S(2)}, u32[]{:S(2)}) collective-permute-start(bf16[4,144,256]{2,1,0:T(8,128)(2,1)} %get-tuple-element.105), channel_id=1, source_target_pairs={{0,12},{2,14},{4,8},{6,10},{8,4},{10,6},{12,0},{14,2},{16,28},{18,... | collective-permute-start | bytes 884744 | tf_op jit(solution)/shard_map/ppermute | solution.py:544
  99.2 17.9 %collective-permute-start.16 = (bf16[144,256]{1,0:T(8,128)(2,1)S(1)}, bf16[144,256]{1,0:T(8,128)(2,1)S(1)}, u32[]{:S(2)}, u32[]{:S(2)}) collective-permute-start(bf16[144,256]{1,0:T(8,128)(2,1)S(1)} %get-tuple-element.120), channel_id=1, source_target_pairs={{0,2},{2,0},{4,6},{6,4},{8,10},{10,8},{12,14},{14,12},{16,18},{18,... | collective-permute-start | bytes 221192 | tf_op jit(solution)/shard_map/ppermute | solution.py:549
  99.3 20.5 %collective-permute-start.17 = (bf16[144,256]{1,0:T(8,128)(2,1)S(1)}, bf16[144,256]{1,0:T(8,128)(2,1)S(1)}, u32[]{:S(2)}, u32[]{:S(2)}) collective-permute-start(bf16[144,256]{1,0:T(8,128)(2,1)S(1)} %get-tuple-element.121), channel_id=1, source_target_pairs={{0,16},{2,18},{4,20},{6,22},{8,24},{10,26},{12,28},{14,30},{16,0},... | collective-permute-start | bytes 221192 | tf_op jit(solution)/shard_map/ppermute | solution.py:549
  104.0 15.7 %collective-permute-start.18 = (bf16[144,256]{1,0:T(8,128)(2,1)S(1)}, bf16[144,256]{1,0:T(8,128)(2,1)S(1)}, u32[]{:S(2)}, u32[]{:S(2)}) collective-permute-start(bf16[144,256]{1,0:T(8,128)(2,1)S(1)} %get-tuple-element.122), channel_id=1, source_target_pairs={{0,18},{2,16},{4,22},{6,20},{8,26},{10,24},{12,30},{14,28},{16,2},... | collective-permute-start | bytes 221192 | tf_op jit(solution)/shard_map/ppermute | solution.py:549
  114.6 1.0 copy-start.1
  115.7 0.8 copy-start.3
  116.7 3.9 %collective-permute-start.10 = (bf16[144,256]{1,0:T(8,128)(2,1)S(1)}, bf16[144,256]{1,0:T(8,128)(2,1)S(1)}, u32[]{:S(2)}, u32[]{:S(2)}) collective-permute-start(bf16[144,256]{1,0:T(8,128)(2,1)S(1)} %get-tuple-element.108), channel_id=1, source_target_pairs={{0,2},{2,0},{4,6},{6,4},{8,10},{10,8},{12,14},{14,12},{16,18},{18,... | collective-permute-start | bytes 221192 | tf_op jit(solution)/shard_map/ppermute | solution.py:549
  116.8 8.3 %collective-permute-start.11 = (bf16[144,256]{1,0:T(8,128)(2,1)S(1)}, bf16[144,256]{1,0:T(8,128)(2,1)S(1)}, u32[]{:S(2)}, u32[]{:S(2)}) collective-permute-start(bf16[144,256]{1,0:T(8,128)(2,1)S(1)} %get-tuple-element.109), channel_id=1, source_target_pairs={{0,16},{2,18},{4,20},{6,22},{8,24},{10,26},{12,28},{14,30},{16,0},... | collective-permute-start | bytes 221192 | tf_op jit(solution)/shard_map/ppermute | solution.py:549
  117.2 9.4 %collective-permute-start.12 = (bf16[144,256]{1,0:T(8,128)(2,1)S(1)}, bf16[144,256]{1,0:T(8,128)(2,1)S(1)}, u32[]{:S(2)}, u32[]{:S(2)}) collective-permute-start(bf16[144,256]{1,0:T(8,128)(2,1)S(1)} %get-tuple-element.110), channel_id=1, source_target_pairs={{0,18},{2,16},{4,22},{6,20},{8,26},{10,24},{12,30},{14,28},{16,2},... | collective-permute-start | bytes 221192 | tf_op jit(solution)/shard_map/ppermute | solution.py:549
Sparse Core Ops, SparseCore 0:
  9.6 53.9 all-gather.2
